TPU v7x, 256 devices: a whole 4x4x8 slice. The times are simulated.
256 devices in a mesh: tm: 16 (over z, core), tile: 16 (over y, x).
Axes of the slice: x: 4, y: 4, z: 8, core: 2. Of those that a mesh axis runs over, the one named last changes fastest.
Arguments:
- video: bfloat16 [512, 2, 8, 256, 128], P('tm', None, None, 'tile')
- slot_block: int32 [512], P('tm'), may hold values from -1 to 255, as said below
- clip_frames: int32 [8], replicated, may hold values from 1 to 128, 512 in all
- conv1_weight: bfloat16 [3, 3, 3, 128, 128], replicated, may hold values from -0.109375 to 0.109375
- norm_gain: float32 [128], replicated, may hold values from 0.5 to 1.5
- norm_bias: float32 [128], replicated, may hold values from -3 to 3
- conv2_weight: bfloat16 [3, 3, 3, 128, 128], replicated, may hold values from -0.109375 to 0.109375
- conv2_bias: float32 [128], replicated, may hold values from -3 to 3
Outputs:
- encoded: bfloat16 [512, 8, 256, 128], P('tm', None, 'tile')
Inputs may be any that keep to these rules, and one draw needn't show every extreme that they name: `slot_block`: each of the 256 blocks of the pack sits in exactly one slot and the other slots hold -1; block k belongs to owner k // 16, and the slots of one index of tm hold at most 2 blocks of any one owner. `clip_frames`: the counts sum to 512.
All inputs are finite; a program needn't handle non-finite values.
Results may differ from a plain program's by a relative error of at most 0.002.
Values may be sent and summed in bfloat16 or wider, within the bound.
No kernel may reach another device: no remote copies, remote signals or barrier semaphores. Data moves between devices by JAX's collectives and lax.ppermute only.
A program may use at most 128 MiB of HBM per device.

v0:
```python
import jax
import jax.numpy as jnp
from jax import lax
from jax.sharding import PartitionSpec as P

GROUPS = 32
OWN = 16
CAP = 2


epsilon = 1e-06


def padded_2(cells, sides, width):
    for axis, dim in sides:
        count = lax.axis_size(axis)
        ends = count - 1
        head = lax.slice_in_dim(cells, 0, width, axis=dim)
        tail = lax.slice_in_dim(cells, cells.shape[dim] - width, cells.shape[dim], axis=dim)
        cells = jnp.concatenate(
            [
                lax.ppermute(tail, axis, [(i, (i + 1) % count) for i in range(ends)]),
                cells,
                lax.ppermute(head, axis, [((i + 1) % count, i) for i in range(ends)]),
            ],
            axis=dim,
        )
    return cells


def passed_along(block, axis, distance):
    devices = range(lax.axis_size(axis))
    route = [(i - distance, i) for i in devices if i - distance in devices]
    return lax.ppermute(block, axis, route)


def frame_clips(clip_frames, first_frame, frame_count):
    clip_ends = jnp.cumsum(clip_frames)
    frame_index = first_frame + jnp.arange(frame_count, dtype=jnp.int32)
    clip_ids = jnp.sum((frame_index[:, None] >= clip_ends[None, :]).astype(jnp.int32), axis=1)
    return jnp.where(frame_index < 0, -1, clip_ids)


def causal_conv(padded, clip_ids, weight):
    outputs = padded.shape[0] - 2
    height = padded.shape[1] - 2
    width = padded.shape[2] - 2
    channels = padded.shape[3]
    summed = jnp.zeros((outputs * height * width, weight.shape[4]), jnp.float32)
    for offset in range(3):
        valid_lag = (clip_ids[2 - offset : 2 - offset + outputs] == clip_ids[2:]).astype(
            padded.dtype
        )
        source = padded[2 - offset : 2 - offset + outputs] * valid_lag[:, None, None, None]
        windows = [
            source[:, row_tap : row_tap + height, col_tap : col_tap + width, :]
            for row_tap in range(3)
            for col_tap in range(3)
        ]
        stacked = jnp.concatenate(windows, axis=3).reshape(outputs * height * width, 9 * channels)
        kernel = weight[2 - offset].reshape(9 * channels, weight.shape[4])
        summed = summed + jnp.dot(stacked, kernel, preferred_element_type=jnp.float32)
    return summed.reshape(outputs, height, width, weight.shape[4])


def pad_input(frames):
    widened = padded_2(frames, (("tile", 2),), 1)
    return jnp.pad(widened, ((0, 0), (1, 1), (0, 0), (0, 0)))


def pad_active(active):
    widened = padded_2(active, (("tile", 2),), 1)
    return jnp.pad(widened, ((0, 0), (1, 1), (0, 0), (0, 0)))


def norm_silu(hidden, norm_gain, norm_bias):
    frame_count, height, width, channels = hidden.shape
    grouped = hidden.reshape(frame_count, height, width, GROUPS, channels // GROUPS)
    number = height * width * lax.axis_size("tile") * (channels // GROUPS)
    summed = lax.psum(jnp.sum(grouped, axis=(1, 2, 4), keepdims=True), "tile")
    group_mean = summed / number
    centred = grouped - group_mean
    spread = lax.psum(jnp.sum(centred * centred, axis=(1, 2, 4), keepdims=True), "tile")
    group_var = spread / number
    normed = ((grouped - group_mean) * lax.rsqrt(group_var + epsilon)).reshape(hidden.shape)
    return jax.nn.silu(normed * norm_gain + norm_bias).astype(jnp.bfloat16)


def place_blocks(arrived, arrived_places):
    sources = arrived.shape[0] * arrived.shape[1]
    stacked_in = arrived.reshape((sources,) + arrived.shape[2:])
    slot_places = arrived_places.reshape(sources).astype(jnp.float32)
    wanted = jnp.arange(OWN, dtype=jnp.float32)
    matches = slot_places[None, :] == wanted[:, None]
    chosen = jnp.sum(jnp.where(matches, jnp.arange(sources, dtype=jnp.int32)[None, :], 0), axis=1)
    picked = jnp.take(stacked_in, chosen, axis=0)
    return picked.reshape((OWN * arrived.shape[2],) + arrived.shape[3:])


def shards(
    video, slot_block, clip_frames, conv1_weight, norm_gain, norm_bias, conv2_weight, conv2_bias
):
    owners = lax.axis_size("tm")
    position = lax.axis_index("tm")
    slots, block_frames = (video.shape[0], video.shape[1])
    filled = slot_block >= 0
    owner_of = jnp.where(filled, slot_block // OWN, -1)
    slot_ids = jnp.arange(slots, dtype=jnp.int32)
    precedes = (owner_of[None, :] == owner_of[:, None]) & (slot_ids[None, :] < slot_ids[:, None])
    arrival = jnp.sum(precedes.astype(jnp.int32), axis=1)
    where_to = jnp.where(filled, owner_of * CAP + arrival, -1)
    places = jnp.arange(owners * CAP, dtype=jnp.int32)
    matches = where_to[None, :] == places[:, None]
    present = jnp.any(matches, axis=1)
    chosen = jnp.sum(jnp.where(matches, slot_ids[None, :], 0), axis=1)
    outgoing = jnp.where(
        present[:, None, None, None, None],
        jnp.take(video, chosen, axis=0),
        jnp.zeros((), video.dtype),
    )
    outgoing = outgoing.reshape((owners, CAP) + video.shape[1:])
    placing = (
        jnp.where(present, jnp.take(slot_block, chosen) % OWN, -1)
        .astype(jnp.bfloat16)
        .reshape(owners, CAP)
    )
    length = OWN * block_frames
    lead_frames = 2
    arrived, arrived_places = (
        lax.all_to_all(outgoing, "tm", split_axis=0, concat_axis=0, tiled=True),
        lax.all_to_all(placing, "tm", split_axis=0, concat_axis=0, tiled=True),
    )
    frames = place_blocks(arrived, arrived_places)
    earlier_frames = passed_along(frames[length - lead_frames :], "tm", 1)
    extended = jnp.concatenate([earlier_frames, frames], axis=0)
    clip_ids = frame_clips(clip_frames, position * length - lead_frames, length + lead_frames)
    hidden = causal_conv(pad_input(extended), clip_ids, conv1_weight)
    active = norm_silu(hidden, norm_gain, norm_bias)
    act_prior = passed_along(active[length - 2 :], "tm", 1)
    active = jnp.concatenate([act_prior, active], axis=0)
    branch = causal_conv(pad_active(active), clip_ids, conv2_weight)
    return (frames.astype(jnp.float32) + branch + conv2_bias).astype(jnp.bfloat16)


def solution(mesh):
    placed = (P("tm", None, None, "tile", None), P("tm"), P(), P(), P(), P(), P(), P())
    return jax.shard_map(
        shards, mesh=mesh, in_specs=placed, out_specs=P("tm", None, "tile", None), check_vma=False
    )
```

profile of v0, /device:TPU:96, one launch (start us, length us, event | category | flops | bytes accessed | tf_op | source)
XLA Modules:
  0.0 341.8 jit_solution(6249926938578894697)
XLA Ops:
  0.0 0.8 compare_select_fusion.12
  1.0 0.7 compare_select_fusion.11
  2.2 1.4 gather_fusion
  3.8 0.7 copy.56
  4.5 7.7 %all-to-all-start = ((bf16[16,1,2]{2,1,0:T(2,128)(2,1)}), bf16[16,1,2]{2,1,0:T(2,128)(2,1)S(1)}, u32[]{:S(2)}, u32[]{:S(2)}) async-start(bf16[16,1,2]{2,1,0:T(2,128)(2,1)} %copy.56), calls=%async_computation | async-start | bytes 16384 | tf_op jit(solution)/shard_map/all_to_all | solution.py:131
  12.4 2.1 gather_fusion.1
  14.6 3.4 select_select_fusion
  17.9 7.2 %all-to-all-start.1 = ((bf16[16,2,2,8,16,128]{5,4,3,2,1,0:T(8,128)(2,1)}), bf16[16,2,2,8,16,128]{5,4,3,2,1,0:T(8,128)(2,1)S(1)}, u32[]{:S(2)}, u32[]{:S(2)}) async-start(bf16[16,2,2,8,16,128]{5,4,3,2,1,0:T(8,128)(2,1)} %select_select_fusion), calls=%async_computation.1 | async-start | bytes 4194304 | tf_op jit(solution)/shard_map/all_to_all | solution.py:130
  25.4 0.9 fusion.24
  26.6 0.7 slice.337
  27.5 46.4 %all-to-all-done.1 = bf16[16,2,2,8,16,128]{5,4,3,2,1,0:T(8,128)(2,1)S(1)} async-done(((bf16[16,2,2,8,16,128]{5,4,3,2,1,0:T(8,128)(2,1)}), bf16[16,2,2,8,16,128]{5,4,3,2,1,0:T(8,128)(2,1)S(1)}, u32[]{:S(2)}, u32[]{:S(2)}) %all-to-all-start.1) | async-done | bytes 2097184 | tf_op jit(solution)/shard_map/all_to_all | solution.py:130
  73.9 0.7 gather_fusion.2
  74.6 0.7 fusion.15
  75.3 2.0 collective-permute-start
  77.6 3.3 collective-permute-done
  81.1 1.3 collective-permute-start.2
  82.5 4.5 %collective-permute-start.1 = (bf16[34,8,1,128]{3,1,2,0:T(8,128)(2,1)S(1)}, bf16[34,8,1,128]{3,1,2,0:T(8,128)(2,1)S(1)}, u32[]{:S(2)}, u32[]{:S(2)}) collective-permute-start(bf16[34,8,1,128]{3,1,2,0:T(8,128)(2,1)S(1)} %copy.57), channel_id=1, source_target_pairs={{0,1},{1,2},{2,3},{3,4},{4,5},{5,6},{6,7},{7,8},{8,9},{9,10},{10,1... | collective-permute-start | bytes 208904 | tf_op jit(solution)/shard_map/ppermute | solution.py:22
  87.5 1.5 collective-permute-done.1
  89.1 1.4 fusion.8
  90.7 0.7 slice_dynamic-update-slice_fusion.46
  91.4 0.7 slice_dynamic-update-slice_fusion.45
  93.2 0.8 fusion.13
  94.4 0.7 slice_dynamic-update-slice_fusion.43
  95.1 0.7 slice_dynamic-update-slice_fusion.42
  97.0 0.7 slice_dynamic-update-slice_fusion.30
  100.9 0.7 slice_dynamic-update-slice_fusion.40
  101.6 0.7 slice_dynamic-update-slice_fusion.39
  102.7 0.9 slice_dynamic-update-slice_fusion.37
  103.6 0.7 slice_dynamic-update-slice_fusion.36
  104.7 0.7 slice_dynamic-update-slice_fusion.34
  105.4 2.7 fusion.25
  108.1 1.3 slice_dynamic-update-slice_fusion.24
  109.5 2.7 convolution_add_fusion.3
  112.2 2.7 convolution_add_fusion.2
  115.0 1.9 copy.63
  116.9 10.8 %reshape_reshape.6 = f32[32,8,16,32,4]{2,1,0,4,3:T(8,128)} reshape(f32[4096,128]{0,1:T(8,128)} %copy.63) | data formatting | bytes 4194304 | tf_op jit(solution)/shard_map/reshape;reshape | solution.py:78
  127.7 8.5 %reduce_sum.70 = f32[32,32]{0,1:T(8,128)S(1)} reduce(f32[32,8,16,32,4]{2,1,0,4,3:T(8,128)} %reshape_reshape.6, f32[]{:T(128)} %constant.100.clone.1), dimensions={1,2,4}, to_apply=%region_6.7 | reduce | flops 523264 | bytes 2101252 | tf_op jit(solution)/shard_map/reduce_sum | solution.py:80
  136.2 75.8 %psum.14 = f32[32,1,1,32,1]{0,3,4,2,1:T(8,128)S(1)} all-reduce(f32[32,1,1,32,1]{0,3,4,2,1:T(8,128)S(1)} %bitcast.73), channel_id=1, replica_groups=mesh['tm'=16,'tile'=16] {'tile'}, use_global_device_ids=true, to_apply=%region_7.8 | all-reduce | flops 1024 | bytes 8192 | tf_op jit(solution)/shard_map/psum | solution.py:80
  212.0 17.6 %multiply_reduce_fusion = f32[32,32]{0,1:T(8,128)S(1)} fusion(f32[32,8,16,32,4]{2,1,0,4,3:T(8,128)} %reshape_reshape.6, f32[32,32]{0,1:T(8,128)S(1)} %multiply_bitcast_fusion), kind=kLoop, calls=%fused_computation.3 | loop fusion | flops 1571840 | bytes 2105344 | tf_op jit(solution)/shard_map/reduce_sum | solution.py:83
  229.6 69.5 %psum.15 = f32[32,1,1,32,1]{0,3,4,2,1:T(8,128)S(1)} all-reduce(f32[32,1,1,32,1]{0,3,4,2,1:T(8,128)S(1)} %bitcast.74), channel_id=1, replica_groups=mesh['tm'=16,'tile'=16] {'tile'}, use_global_device_ids=true, to_apply=%region_9.10 | all-reduce | flops 1024 | bytes 8192 | tf_op jit(solution)/shard_map/psum | solution.py:83
  299.4 0.7 multiply_convert_fusion
  300.1 1.9 collective-permute-start.3
  302.0 3.7 %collective-permute-done.3 = bf16[2,8,16,128]{3,2,1,0:T(8,128)(2,1)S(1)} collective-permute-done((bf16[2,8,16,128]{3,2,1,0:T(8,128)(2,1)S(1)}, bf16[2,8,16,128]{3,2,1,0:T(8,128)(2,1)S(1)}, u32[]{:S(2)}, u32[]{:S(2)}) %collective-permute-start.3) | collective-permute-done | bytes 65568 | tf_op jit(solution)/shard_map/ppermute | solution.py:34
  305.9 1.3 collective-permute-start.5
  307.2 4.5 %collective-permute-start.4 = (bf16[34,8,1,128]{3,1,2,0:T(8,128)(2,1)S(1)}, bf16[34,8,1,128]{3,1,2,0:T(8,128)(2,1)S(1)}, u32[]{:S(2)}, u32[]{:S(2)}) collective-permute-start(bf16[34,8,1,128]{3,1,2,0:T(8,128)(2,1)S(1)} %copy.66), channel_id=1, source_target_pairs={{0,1},{1,2},{2,3},{3,4},{4,5},{5,6},{6,7},{7,8},{8,9},{9,10},{10,1... | collective-permute-start | bytes 208904 | tf_op jit(solution)/shard_map/ppermute | solution.py:22
  312.2 1.5 collective-permute-done.4
  313.8 1.4 select_maximum_fusion
  315.9 0.7 slice_dynamic-update-slice_fusion.22
  316.5 0.7 slice_dynamic-update-slice_fusion.21
  317.8 0.9 constant_dynamic-update-slice_fusion.1
  318.7 0.8 fusion.11
  320.0 0.7 slice_dynamic-update-slice_fusion.19
  320.6 0.7 slice_dynamic-update-slice_fusion.18
  321.6 0.7 slice_dynamic-update-slice_fusion.16
  322.3 0.7 slice_dynamic-update-slice_fusion.15
  323.4 0.7 slice_dynamic-update-slice_fusion.13
  324.1 0.7 slice_dynamic-update-slice_fusion.12
  325.2 0.7 slice_dynamic-update-slice_fusion.10
  325.9 0.7 slice_dynamic-update-slice_fusion.9
  327.5 0.9 slice_dynamic-update-slice_fusion.6
  331.9 2.7 fusion.26
  334.6 2.7 convolution_add_fusion.1
  337.4 2.7 convolution_add_fusion
  340.1 1.5 add_convert_fusion
  (104 shorter events, 18.4 us)
Async XLA Ops:
  0.0 12.4 %copy-start = (bf16[32,2,8,16,128]{4,3,2,1,0:T(8,128)(2,1)S(1)}, bf16[32,2,8,16,128]{4,3,2,1,0:T(8,128)(2,1)}, u32[]{:S(2)}) copy-start(bf16[32,2,8,16,128]{4,3,2,1,0:T(8,128)(2,1)} %param.8) | copy-start | bytes 6291460
  4.5 13.4 %all-to-all-start = ((bf16[16,1,2]{2,1,0:T(2,128)(2,1)}), bf16[16,1,2]{2,1,0:T(2,128)(2,1)S(1)}, u32[]{:S(2)}, u32[]{:S(2)}) async-start(bf16[16,1,2]{2,1,0:T(2,128)(2,1)} %copy.56), calls=%async_computation | async-start | bytes 16384 | tf_op jit(solution)/shard_map/all_to_all | solution.py:131
  14.5 10.6 %copy-start.11 = (s32[8]{0:T(128)S(1)}, s32[8]{0:T(128)}, u32[]{:S(2)}) copy-start(s32[8]{0:T(128)} %param.10) | copy-start | bytes 100
  14.5 10.9 %copy-start.6 = (bf16[3,3,3,128,128]{4,3,2,1,0:T(8,128)(2,1)S(1)}, bf16[3,3,3,128,128]{4,3,2,1,0:T(8,128)(2,1)}, u32[]{:S(2)}) copy-start(bf16[3,3,3,128,128]{4,3,2,1,0:T(8,128)(2,1)} %param.11) | copy-start | bytes 2654212
  17.9 55.9 %all-to-all-start.1 = ((bf16[16,2,2,8,16,128]{5,4,3,2,1,0:T(8,128)(2,1)}), bf16[16,2,2,8,16,128]{5,4,3,2,1,0:T(8,128)(2,1)S(1)}, u32[]{:S(2)}, u32[]{:S(2)}) async-start(bf16[16,2,2,8,16,128]{5,4,3,2,1,0:T(8,128)(2,1)} %select_select_fusion), calls=%async_computation.1 | async-start | bytes 4194304 | tf_op jit(solution)/shard_map/all_to_all | solution.py:130
  75.3 5.6 %collective-permute-start = (bf16[2,8,16,128]{3,2,1,0:T(8,128)(2,1)S(1)}, bf16[2,8,16,128]{3,2,1,0:T(8,128)(2,1)S(1)}, u32[]{:S(2)}, u32[]{:S(2)}) collective-permute-start(bf16[2,8,16,128]{3,2,1,0:T(8,128)(2,1)S(1)} %fusion.15), channel_id=1, source_target_pairs={{0,16},{16,32},{32,48},{48,64},{64,80},{80,96},{96,112},{112,128},... | collective-permute-start | bytes 196616 | tf_op jit(solution)/shard_map/ppermute | solution.py:34
  81.1 6.2 %collective-permute-start.2 = (bf16[34,8,1,128]{3,1,2,0:T(8,128)(2,1)S(1)}, bf16[34,8,1,128]{3,1,2,0:T(8,128)(2,1)S(1)}, u32[]{:S(2)}, u32[]{:S(2)}) collective-permute-start(bf16[34,8,1,128]{3,1,2,0:T(8,128)(2,1)S(1)} %copy.58), channel_id=1, source_target_pairs={{1,0},{2,1},{3,2},{4,3},{5,4},{6,5},{7,6},{8,7},{9,8},{10,9},{11,1... | collective-permute-start | bytes 208904 | tf_op jit(solution)/shard_map/ppermute | solution.py:24
  82.5 6.5 %collective-permute-start.1 = (bf16[34,8,1,128]{3,1,2,0:T(8,128)(2,1)S(1)}, bf16[34,8,1,128]{3,1,2,0:T(8,128)(2,1)S(1)}, u32[]{:S(2)}, u32[]{:S(2)}) collective-permute-start(bf16[34,8,1,128]{3,1,2,0:T(8,128)(2,1)S(1)} %copy.57), channel_id=1, source_target_pairs={{0,1},{1,2},{2,3},{3,4},{4,5},{5,6},{6,7},{7,8},{8,9},{9,10},{10,1... | collective-permute-start | bytes 208904 | tf_op jit(solution)/shard_map/ppermute | solution.py:22
  108.1 1.3 copy-start.5
  109.5 2.7 copy-start.4
  114.9 184.4 %copy-start.2 = (f32[4096,128]{1,0:T(8,128)}, f32[4096,128]{1,0:T(8,128)S(1)}, u32[]{:S(2)}) copy-start(f32[4096,128]{1,0:T(8,128)S(1)} %convolution_add_fusion.2) | copy-start | bytes 6291460
  212.0 87.3 %copy-start.8 = (f32[128]{0:T(128)S(1)}, f32[128]{0:T(128)}, u32[]{:S(2)}) copy-start(f32[128]{0:T(128)} %param.13) | copy-start | bytes 1540
  212.0 87.4 %copy-start.9 = (f32[128]{0:T(128)S(1)}, f32[128]{0:T(128)}, u32[]{:S(2)}) copy-start(f32[128]{0:T(128)} %param.12) | copy-start | bytes 1540
  299.3 12.5 %copy-start.7 = (bf16[3,3,3,128,128]{4,3,2,1,0:T(8,128)(2,1)S(1)}, bf16[3,3,3,128,128]{4,3,2,1,0:T(8,128)(2,1)}, u32[]{:S(2)}) copy-start(bf16[3,3,3,128,128]{4,3,2,1,0:T(8,128)(2,1)} %param.14) | copy-start | bytes 2654212
  300.1 5.6 %collective-permute-start.3 = (bf16[2,8,16,128]{3,2,1,0:T(8,128)(2,1)S(1)}, bf16[2,8,16,128]{3,2,1,0:T(8,128)(2,1)S(1)}, u32[]{:S(2)}, u32[]{:S(2)}) collective-permute-start(bf16[2,8,16,128]{3,2,1,0:T(8,128)(2,1)S(1)} %slice.365), channel_id=1, source_target_pairs={{0,16},{16,32},{32,48},{48,64},{64,80},{80,96},{96,112},{112,128},... | collective-permute-start | bytes 196616 | tf_op jit(solution)/shard_map/ppermute | solution.py:34
  305.9 6.2 %collective-permute-start.5 = (bf16[34,8,1,128]{3,1,2,0:T(8,128)(2,1)S(1)}, bf16[34,8,1,128]{3,1,2,0:T(8,128)(2,1)S(1)}, u32[]{:S(2)}, u32[]{:S(2)}) collective-permute-start(bf16[34,8,1,128]{3,1,2,0:T(8,128)(2,1)S(1)} %copy.67), channel_id=1, source_target_pairs={{1,0},{2,1},{3,2},{4,3},{5,4},{6,5},{7,6},{8,7},{9,8},{10,9},{11,1... | collective-permute-start | bytes 208904 | tf_op jit(solution)/shard_map/ppermute | solution.py:24
  307.2 6.5 %collective-permute-start.4 = (bf16[34,8,1,128]{3,1,2,0:T(8,128)(2,1)S(1)}, bf16[34,8,1,128]{3,1,2,0:T(8,128)(2,1)S(1)}, u32[]{:S(2)}, u32[]{:S(2)}) collective-permute-start(bf16[34,8,1,128]{3,1,2,0:T(8,128)(2,1)S(1)} %copy.66), channel_id=1, source_target_pairs={{0,1},{1,2},{2,3},{3,4},{4,5},{5,6},{6,7},{7,8},{8,9},{9,10},{10,1... | collective-permute-start | bytes 208904 | tf_op jit(solution)/shard_map/ppermute | solution.py:22
  315.9 2.0 copy-start.3
  337.4 2.7 copy-start.10
  337.4 4.2 %copy-start.1 = (bf16[32,2,8,16,128]{4,3,2,1,0:T(8,128)(2,1)S(1)}, bf16[32,2,8,16,128]{4,3,2,1,0:T(8,128)(2,1)}, u32[]{:S(2)}) copy-start(bf16[32,2,8,16,128]{4,3,2,1,0:T(8,128)(2,1)} %param.8) | copy-start | bytes 6291460
where the time goes:
time: 346 us; the launch traced here: 342 us
  blocking collectives  145 us (42%)
  waiting for transfers between devices  56.8 us (16%)
  local copies, waits for them, and re-layouts  49.2 us (14%)
  other arithmetic  42.6 us (12%)
  starting transfers between devices  30.5 us (9%)
  matrix products  16.3 us (5%)
    psum x1, blocking collectives, norm_silu(): summed = lax.psum(jnp.sum(grouped, axis=(1, 2, 4), keepdims=True), 'tile')  75.8 us
    psum x1, blocking collectives, norm_silu(): lax.psum(jnp.sum(centred * centred, axis=(1, 2, 4), keepdims=True), 'tile')  69.5 us
    all_to_all x1, waiting for transfers between devices, shards(): lax.all_to_all(outgoing, 'tm', split_axis=0, concat_axis=0, tiled=True)  46.4 us
    unnamed x67, local copies, waits for them, and re-layouts  24.3 us
    reduce_sum x1, other arithmetic, norm_silu(): jnp.sum(centred * centred, axis=(1, 2, 4), keepdims=True)  17.6 us
    dot_general x6, matrix products, causal_conv(): jnp.dot(stacked, kernel, preferred_element_type=jnp.float32)  16.3 us
    another operation x1, local copies, waits for them, and re-layouts, norm_silu(): hidden.reshape(frame_count, height, width, GROUPS, channels // GROUPS)  10.8 us
    ppermute x2, starting transfers between devices, padded_2(): lax.ppermute(tail, axis, [(i, (i + 1) % count) for i in range(ends)])  9.1 us
  transfers between devices with their start and end apart: 8, of which 7 were waited for; matrix products, arithmetic and copies ran while one was open for 3% of the time, Pallas kernels for 0%

commit v1 on v0

v1 whole, which is shorter than its diff:
```python
import functools

import jax
import jax.numpy as jnp
from jax import lax
from jax.experimental import pallas as pl
from jax.experimental.pallas import tpu as pltpu
from jax.sharding import PartitionSpec as P

GROUPS = 32
OWN = 16
CAP = 2
C = 128
ROWS = 8
COLS = 16
POS = ROWS * COLS
LEAD = 4
CHUNK = 4
EPSILON = 1e-06
VMEM_BYTES = 48 * 1024 * 1024

f32 = jnp.float32
bf16 = jnp.bfloat16


def vmem():
    return pl.BlockSpec(memory_space=pltpu.VMEM)


def smem():
    return pl.BlockSpec(memory_space=pltpu.SMEM)


def hbm():
    return pl.BlockSpec(memory_space=pl.ANY)


def params():
    return pltpu.CompilerParams(vmem_limit_bytes=VMEM_BYTES)


def send_kernel(slot_ref, video_ref, out_ref, count, sems):
    slots = slot_ref.shape[0]
    for owner in range(count.shape[0]):
        count[owner] = 0

    for slot in range(slots):
        block = slot_ref[slot]

        @pl.when(block >= 0)
        def _():
            owner = block >> 4
            rank = count[owner]
            count[owner] = rank + 1
            pltpu.make_async_copy(
                video_ref.at[slot], out_ref.at[owner * CAP + rank], sems.at[slot]
            ).start()

    for slot in range(slots):

        @pl.when(slot_ref[slot] >= 0)
        def _():
            pltpu.make_async_copy(video_ref.at[slot], out_ref.at[0], sems.at[slot]).wait()


def send_blocks(slot_block, video, owners):
    return pl.pallas_call(
        send_kernel,
        out_shape=jax.ShapeDtypeStruct((owners * CAP,) + video.shape[1:], video.dtype),
        in_specs=[smem(), hbm()],
        out_specs=hbm(),
        scratch_shapes=[
            pltpu.SMEM((owners,), jnp.int32),
            pltpu.SemaphoreType.DMA((video.shape[0],)),
        ],
        compiler_params=params(),
        name="send_blocks",
    )(slot_block, video)


def place_kernel(order_ref, arrived_ref, lead_ref, frames_ref, left_ref, right_ref, wide, sems):
    blocks = order_ref.shape[0]
    length = LEAD + blocks * 2
    copies = [
        pltpu.make_async_copy(
            arrived_ref.at[order_ref[k]],
            frames_ref.at[pl.ds(LEAD + 2 * k, 2)],
            sems.at[k],
        )
        for k in range(blocks)
    ]
    for copy in copies:
        copy.start()
    frames_ref[0:LEAD] = lead_ref[...]

    def edges(start):
        wide[...] = frames_ref[pl.ds(start, 2)].reshape(2 * POS, C).astype(f32)
        left = wide[pl.ds(0, 2 * ROWS, stride=COLS), :].astype(bf16)
        right = wide[pl.ds(COLS - 1, 2 * ROWS, stride=COLS), :].astype(bf16)
        left_ref[pl.ds(start, 2)] = left.reshape(2, ROWS, C)
        right_ref[pl.ds(start, 2)] = right.reshape(2, ROWS, C)

    for start in range(0, LEAD, 2):
        edges(start)
    for k in range(blocks):
        copies[k].wait()
        edges(LEAD + 2 * k)


def place_blocks(order, arrived, lead):
    blocks = order.shape[0]
    length = LEAD + 2 * blocks
    edge = jax.ShapeDtypeStruct((length, ROWS, C), bf16)
    return pl.pallas_call(
        place_kernel,
        out_shape=(jax.ShapeDtypeStruct((length, ROWS, COLS, C), bf16), edge, edge),
        in_specs=[smem(), hbm(), vmem()],
        out_specs=(vmem(), vmem(), vmem()),
        scratch_shapes=[
            pltpu.VMEM((2 * POS, C), f32),
            pltpu.SemaphoreType.DMA((blocks,)),
        ],
        compiler_params=params(),
        name="place_blocks",
    )(order, arrived, lead)


def conv_kernel(valid_ref, frames_ref, weight_ref, out_ref, shifted, taps):
    length = frames_ref.shape[0]
    rows = CHUNK * POS
    column = lax.broadcasted_iota(jnp.int32, (rows, C), 0) % COLS
    first = column == 0
    last = column == COLS - 1
    for j in range(3):
        taps[j, :, 0] = jnp.zeros((CHUNK, COLS, C), bf16)
        taps[j, :, ROWS + 1] = jnp.zeros((CHUNK, COLS, C), bf16)
    shifted[0:8] = jnp.zeros((8, C), f32)
    shifted[rows + 8 :] = jnp.zeros((8, C), f32)
    out_ref[0:2] = jnp.zeros((2, POS, C), f32)

    def step(chunk, carry):
        start = chunk * CHUNK
        here = frames_ref[pl.ds(start, CHUNK)]
        shifted[8 : rows + 8] = here.reshape(rows, C).astype(f32)
        before = jnp.where(first, 0.0, shifted[7 : rows + 7]).astype(bf16)
        after = jnp.where(last, 0.0, shifted[9 : rows + 9]).astype(bf16)
        taps[0, :, 1 : ROWS + 1] = before.reshape(CHUNK, ROWS, COLS, C)
        taps[1, :, 1 : ROWS + 1] = here
        taps[2, :, 1 : ROWS + 1] = after.reshape(CHUNK, ROWS, COLS, C)
        windows = jnp.concatenate(
            [taps[j, :, i : i + ROWS].reshape(rows, C) for j in range(3) for i in range(3)],
            axis=1,
        )
        product = jnp.dot(windows, weight_ref[...], preferred_element_type=f32)
        for q in range(CHUNK):
            frame = start + q
            part = product[q * POS : (q + 1) * POS]
            out_ref[frame] += part[:, 0:C]

            @pl.when(frame + 1 < length)
            def _():
                out_ref[frame + 1] += valid_ref[0, frame + 1] * part[:, C : 2 * C]

            @pl.when(frame + 2 < length)
            def _():
                out_ref[frame + 2] = valid_ref[1, frame + 2] * part[:, 2 * C :]

        return carry

    lax.fori_loop(0, length // CHUNK, step, 0)


def conv(valid, frames, weight):
    length = frames.shape[0]
    return pl.pallas_call(
        conv_kernel,
        out_shape=jax.ShapeDtypeStruct((length, POS, C), f32),
        in_specs=[smem(), vmem(), vmem()],
        out_specs=vmem(),
        scratch_shapes=[
            pltpu.VMEM((CHUNK * POS + 16, C), f32),
            pltpu.VMEM((3, CHUNK, ROWS + 2, COLS, C), bf16),
        ],
        compiler_params=params(),
        cost_estimate=pl.CostEstimate(
            flops=2 * length * POS * 27 * C * C, bytes_accessed=4 << 20, transcendentals=0
        ),
        name="conv",
    )(valid, frames, weight)


def edge_product(edge_ref, weight):
    length = edge_ref.shape[0]
    rows = length * ROWS
    edge = edge_ref[...].astype(f32).reshape(rows, C)
    row = lax.broadcasted_iota(jnp.int32, (rows, C), 0) % ROWS
    above = jnp.where(row == 0, 0.0, pltpu.roll(edge, 1, 0))
    below = jnp.where(row == ROWS - 1, 0.0, pltpu.roll(edge, rows - 1, 0))
    windows = jnp.concatenate([above, edge, below], axis=1).astype(bf16)
    product = jnp.dot(windows, weight, preferred_element_type=f32)
    return product.reshape(length, ROWS, 3 * C)


def edge_sum(valid_ref, product_ref, frame):
    return (
        product_ref[frame, :, 0:C]
        + valid_ref[0, frame] * product_ref[frame - 1, :, C : 2 * C]
        + valid_ref[1, frame] * product_ref[frame - 2, :, 2 * C :]
    )


def group_total(entries):
    lane = lax.broadcasted_iota(jnp.int32, entries.shape, 1)
    for bit in (1, 2):
        up = pltpu.roll(entries, C - bit, 1)
        down = pltpu.roll(entries, bit, 1)
        entries = entries + jnp.where((lane & bit) == 0, up, down)
    return entries


HALF = 24


def precise_dot(a, b):
    return jnp.dot(a, b, precision=lax.Precision.HIGHEST, preferred_element_type=f32)


def stats_kernel(
    valid_ref, partial_ref, left_ref, right_ref, wl_ref, wr_ref, out_ref, stats_ref,
    product_l, product_r, means, spreads,
):
    length = partial_ref.shape[0]
    product_l[...] = edge_product(left_ref, wl_ref[...])
    product_r[...] = edge_product(right_ref, wr_ref[...])
    out_ref[0:2] = jnp.zeros((2, POS, C), f32)
    means[...] = jnp.zeros_like(means)
    spreads[...] = jnp.zeros_like(spreads)

    def step(pair, carry):
        for q in range(2):
            frame = 2 + pair * 2 + q
            out_ref[frame] = partial_ref[frame]
            at_left = pl.ds(0, ROWS, stride=COLS)
            at_right = pl.ds(COLS - 1, ROWS, stride=COLS)
            out_ref[frame, at_left, :] += edge_sum(valid_ref, product_l, frame)
            out_ref[frame, at_right, :] += edge_sum(valid_ref, product_r, frame)
            hidden = out_ref[frame]
            mean = jnp.sum(hidden, axis=0, keepdims=True) / POS
            centred = hidden - mean
            means[pl.ds(frame, 1), :] = mean
            spreads[pl.ds(frame, 1), :] = jnp.sum(centred * centred, axis=0, keepdims=True)
        return carry

    lax.fori_loop(0, (length - 2) // 2, step, 0)
    mean = group_total(means[...]) / 4
    off = means[...] - mean
    spread = group_total(spreads[...] + POS * off * off)
    channel = lax.broadcasted_iota(jnp.int32, (C, C), 0)
    lane = lax.broadcasted_iota(jnp.int32, (C, C), 1)
    packed = jnp.zeros((HALF, C), f32)
    for q, part in enumerate((mean[:HALF], spread[:HALF], mean[HALF:], spread[HALF:])):
        picks = (channel == 4 * (lane - GROUPS * q)) & (lane // GROUPS == q)
        packed = packed + precise_dot(part, picks.astype(f32))
    for peer in range(stats_ref.shape[0]):
        stats_ref[peer] = packed


def finish_hidden(valid, partial, left, right, wl, wr, tiles):
    length = partial.shape[0]
    return pl.pallas_call(
        stats_kernel,
        out_shape=(
            jax.ShapeDtypeStruct(partial.shape, f32),
            jax.ShapeDtypeStruct((tiles, HALF, C), f32),
        ),
        in_specs=[smem()] + [vmem()] * 5,
        out_specs=(vmem(), vmem()),
        scratch_shapes=[
            pltpu.VMEM((length, ROWS, 3 * C), f32),
            pltpu.VMEM((length, ROWS, 3 * C), f32),
            pltpu.VMEM((2 * HALF, C), f32),
            pltpu.VMEM((2 * HALF, C), f32),
        ],
        compiler_params=params(),
        name="finish_hidden",
    )(valid, partial, left, right, wl, wr)


def norm_kernel(
    hidden_ref, stats_ref, gain_ref, bias_ref, active_ref, left_ref, right_ref,
    means, scales, wide,
):
    length = hidden_ref.shape[0]
    tiles = stats_ref.shape[0]
    here = POS * (C // GROUPS)
    lane = lax.broadcasted_iota(jnp.int32, (HALF, C), 1)
    is_mean = (lane // GROUPS) % 2 == 0
    total = stats_ref[0]
    for peer in range(1, tiles):
        total = total + stats_ref[peer]
    mean = total / tiles
    apart = jnp.zeros((HALF, C), f32)
    for peer in range(tiles):
        off = stats_ref[peer] - mean
        apart = apart + off * off
    apart = jnp.where(is_mean, apart, 0.0)
    variance = (total + here * pltpu.roll(apart, GROUPS, 1)) / (here * tiles)
    packed = jnp.where(is_mean, mean, lax.rsqrt(jnp.where(is_mean, 1.0, variance) + EPSILON))
    channel = lax.broadcasted_iota(jnp.int32, (C, C), 1)
    source = lax.broadcasted_iota(jnp.int32, (C, C), 0)
    spread_out = []
    for q in range(4):
        picks = (source == channel // (C // GROUPS) + GROUPS * q).astype(f32)
        spread_out.append(precise_dot(packed, picks))
    means[0:HALF] = spread_out[0]
    means[HALF:] = spread_out[2]
    scales[0:HALF] = spread_out[1]
    scales[HALF:] = spread_out[3]
    scales[...] = scales[...] * gain_ref[...]
    active_ref[0:2] = jnp.zeros((2, ROWS, COLS, C), bf16)
    left_ref[0:2] = jnp.zeros((2, ROWS, C), bf16)
    right_ref[0:2] = jnp.zeros((2, ROWS, C), bf16)

    def step(pair, carry):
        for q in range(2):
            frame = 2 + pair * 2 + q
            centred = hidden_ref[frame] - means[pl.ds(frame, 1), :]
            normed = centred * scales[pl.ds(frame, 1), :] + bias_ref[...]
            active = normed * (1.0 / (1.0 + jnp.exp(-normed)))
            wide[q] = active
            active_ref[frame] = active.astype(bf16).reshape(ROWS, COLS, C)
            left_ref[frame] = wide[q, pl.ds(0, ROWS, stride=COLS), :].astype(bf16)
            right_ref[frame] = wide[q, pl.ds(COLS - 1, ROWS, stride=COLS), :].astype(bf16)
        return carry

    lax.fori_loop(0, (length - 2) // 2, step, 0)


def norm_silu(hidden, stats, gain, bias):
    length = hidden.shape[0]
    edge = jax.ShapeDtypeStruct((length, ROWS, C), bf16)
    return pl.pallas_call(
        norm_kernel,
        out_shape=(jax.ShapeDtypeStruct((length, ROWS, COLS, C), bf16), edge, edge),
        in_specs=[vmem()] * 4,
        out_specs=(vmem(),) * 3,
        scratch_shapes=[
            pltpu.VMEM((2 * HALF, C), f32),
            pltpu.VMEM((2 * HALF, C), f32),
            pltpu.VMEM((2, POS, C), f32),
        ],
        compiler_params=params(),
        name="norm_silu",
    )(hidden, stats, gain, bias)


def output_kernel(
    valid_ref, partial_ref, left_ref, right_ref, wl_ref, wr_ref, frames_ref, bias_ref, out_ref,
    product_l, product_r, wide,
):
    product_l[...] = edge_product(left_ref, wl_ref[...])
    product_r[...] = edge_product(right_ref, wr_ref[...])

    def step(pair, carry):
        for q in range(2):
            frame = LEAD + pair * 2 + q
            wide[q] = partial_ref[frame] + bias_ref[...]
            at_left = pl.ds(0, ROWS, stride=COLS)
            at_right = pl.ds(COLS - 1, ROWS, stride=COLS)
            wide[q, at_left, :] += edge_sum(valid_ref, product_l, frame)
            wide[q, at_right, :] += edge_sum(valid_ref, product_r, frame)
            total = frames_ref[frame].reshape(POS, C).astype(f32) + wide[q]
            out_ref[frame - LEAD] = total.astype(bf16).reshape(ROWS, COLS, C)
        return carry

    lax.fori_loop(0, out_ref.shape[0] // 2, step, 0)


def finish_output(valid, partial, left, right, wl, wr, frames, bias):
    length = partial.shape[0]
    return pl.pallas_call(
        output_kernel,
        out_shape=jax.ShapeDtypeStruct((length - LEAD, ROWS, COLS, C), bf16),
        in_specs=[smem()] + [vmem()] * 7,
        out_specs=vmem(),
        scratch_shapes=[
            pltpu.VMEM((length, ROWS, 3 * C), f32),
            pltpu.VMEM((length, ROWS, 3 * C), f32),
            pltpu.VMEM((2, POS, C), f32),
        ],
        compiler_params=params(),
        name="finish_output",
    )(valid, partial, left, right, wl, wr, frames, bias)


def block_order(all_slots, position):
    owner_of = jnp.where(all_slots >= 0, all_slots >> 4, -1)
    slot_ids = jnp.arange(all_slots.shape[1], dtype=jnp.int32)
    precedes = (owner_of[:, None, :] == owner_of[:, :, None]) & (
        slot_ids[None, None, :] < slot_ids[None, :, None]
    )
    rank = jnp.sum(precedes.astype(jnp.int32), axis=2)
    sources = jnp.arange(all_slots.shape[0], dtype=jnp.int32)
    arrival = sources[:, None] * CAP + rank
    wanted = position * OWN + jnp.arange(OWN, dtype=jnp.int32)
    matches = all_slots[None] == wanted[:, None, None]
    return jnp.sum(jnp.where(matches, arrival[None], 0), axis=(1, 2))


def lag_masks(clip_frames, first_frame, length):
    clip_ends = jnp.cumsum(clip_frames)

    def clip_of(frames):
        ids = jnp.sum((frames[:, None] >= clip_ends[None, :]).astype(jnp.int32), axis=1)
        return jnp.where(frames < 0, -1, ids)

    frames = first_frame + jnp.arange(length, dtype=jnp.int32)
    here = clip_of(frames)
    return jnp.stack([clip_of(frames - lag) == here for lag in (1, 2)]).astype(f32)


def lag_weight(weight):
    lags = weight[::-1].transpose(2, 1, 3, 0, 4)
    return lags.reshape(9 * C, 3 * C)


def swap_edges(left, right):
    count = lax.axis_size("tile")
    from_left = lax.ppermute(right, "tile", [(i, i + 1) for i in range(count - 1)])
    from_right = lax.ppermute(left, "tile", [(i + 1, i) for i in range(count - 1)])
    return from_left, from_right


def shards(
    video, slot_block, clip_frames, conv1_weight, norm_gain, norm_bias, conv2_weight, conv2_bias
):
    owners = lax.axis_size("tm")
    tiles = lax.axis_size("tile")
    position = lax.axis_index("tm")
    length = OWN * video.shape[1]

    all_slots = lax.all_gather(slot_block, "tm")
    outgoing = send_blocks(slot_block, video, owners)
    outgoing = outgoing.reshape((owners, CAP) + video.shape[1:])
    arrived = lax.all_to_all(outgoing, "tm", split_axis=0, concat_axis=0, tiled=True)
    arrived = arrived.reshape((owners * CAP,) + video.shape[1:])

    valid = lag_masks(clip_frames, position * length - LEAD, length + LEAD)
    weight1 = lag_weight(conv1_weight)
    weight2 = lag_weight(conv2_weight)
    order = block_order(all_slots, position)

    tail = jnp.take(arrived, order[OWN - LEAD // 2 :], axis=0).reshape((LEAD,) + video.shape[2:])
    lead = lax.ppermute(tail, "tm", [(i, i + 1) for i in range(owners - 1)])
    frames, left, right = place_blocks(order, arrived, lead)
    from_left, from_right = swap_edges(left, right)
    partial = conv(valid, frames, weight1)
    hidden, stats = finish_hidden(
        valid, partial, from_left, from_right, weight1[: 3 * C], weight1[6 * C :], tiles
    )
    stats = lax.all_to_all(stats, "tile", split_axis=0, concat_axis=0, tiled=True)
    active, left, right = norm_silu(hidden, stats, norm_gain[None], norm_bias[None])
    from_left, from_right = swap_edges(left, right)
    partial = conv(valid, active, weight2)
    return finish_output(
        valid, partial, from_left, from_right, weight2[: 3 * C], weight2[6 * C :], frames,
        conv2_bias[None],
    )


def solution(mesh):
    placed = (P("tm", None, None, "tile", None), P("tm"), P(), P(), P(), P(), P(), P())
    return jax.shard_map(
        shards, mesh=mesh, in_specs=placed, out_specs=P("tm", None, "tile", None), check_vma=False
    )
```

time: 346 us -> 146 us (0.42)
  the two profiles are of different devices: /device:TPU:96 before, /device:TPU:40 now
where the time goes in v1:
time: 146 us; the launch traced here: 145 us
  blocking collectives  54.2 us (37%)
  starting transfers between devices  33.5 us (23%)
  Pallas kernels  29.7 us (20%)
  local copies, waits for them, and re-layouts  18 us (12%)
  waiting for transfers between devices  7.16 us (5%)
  other arithmetic  1.47 us (1%)
    unnamed x1, blocking collectives  54.2 us
    pallas_call x2, Pallas kernels, conv(): pl.pallas_call(conv_kernel, out_shape=jax.ShapeDtypeStruct((length, POS,...  17.6 us
    unnamed x45, local copies, waits for them, and re-layouts  11 us
    all_to_all x1, starting transfers between devices, shards(): lax.all_to_all(outgoing, 'tm', split_axis=0, concat_axis=0, tiled=True)  10.3 us
    ppermute x2, starting transfers between devices, swap_edges(): lax.ppermute(left, 'tile', [(i + 1, i) for i in range(count - 1)])  10.3 us
    all_to_all x1, waiting for transfers between devices, shards(): lax.all_to_all(stats, 'tile', split_axis=0, concat_axis=0, tiled=True)  7.15 us
    ppermute x2, starting transfers between devices, swap_edges(): lax.ppermute(right, 'tile', [(i, i + 1) for i in range(count - 1)])  5.64 us
    all_to_all x1, starting transfers between devices, shards(): lax.all_to_all(stats, 'tile', split_axis=0, concat_axis=0, tiled=True)  5.28 us
  transfers between devices with their start and end apart: 7, of which 1 were waited for; matrix products, arithmetic and copies ran while one was open for 7% of the time, Pallas kernels for 12%

profile of v1, /device:TPU:40, one launch (start us, length us, event | category | flops | bytes accessed | tf_op | source)
XLA Modules:
  0.0 145.2 jit_solution(17580663113835488387)
XLA Ops:
  0.0 1.6 %copy-done.3 = bf16[32,2,8,16,128]{4,3,2,1,0:T(8,128)(2,1)S(1)} copy-done((bf16[32,2,8,16,128]{4,3,2,1,0:T(8,128)(2,1)S(1)}, bf16[32,2,8,16,128]{4,3,2,1,0:T(8,128)(2,1)}, u32[]{:S(2)}) %copy-start.3) | copy-done | bytes 2097176
  1.6 0.7 copy-done.7
  2.2 1.5 %send_blocks.1 = bf16[32,2,8,16,128]{4,3,2,1,0:T(8,128)(2,1)S(1)} custom-call(s32[32]{0:T(128)S(1)} %copy-done.7, bf16[32,2,8,16,128]{4,3,2,1,0:T(8,128)(2,1)S(1)} %copy-done.3), custom_call_target="tpu_custom_call" | custom-call | tf_op jit(solution)/shard_map/send_blocks/pallas_call | solution.py:67
  3.8 1.3 copy-done
  5.1 10.3 %all-to-all-start = ((bf16[16,2,2,8,16,128]{5,4,3,2,1,0:T(8,128)(2,1)}), bf16[16,2,2,8,16,128]{5,4,3,2,1,0:T(8,128)(2,1)S(1)}, u32[]{:S(2)}, u32[]{:S(2)}) async-start(bf16[16,2,2,8,16,128]{5,4,3,2,1,0:T(8,128)(2,1)} %bitcast.52), calls=%async_computation | async-start | bytes 4194304 | tf_op jit(solution)/shard_map/all_to_all | solution.py:445
  15.4 0.0 copy-done.18
  15.4 0.2 reduce-window.8
  15.6 0.0 copy-done.19
  15.6 0.6 dynamic-slice
  16.8 0.0 copy-done.8
  16.8 0.2 dynamic-update-slice
  17.1 54.2 %all-reduce = s32[512]{0:T(512)S(1)} all-reduce(s32[512]{0:T(512)S(1)} %dynamic-update-slice), channel_id=2, replica_groups=mesh['tm'=16,'tile'=16] {'tm'}, use_global_device_ids=true, to_apply=%add | all-reduce | flops 512 | bytes 4096
  71.3 0.1 reshape.168
  71.4 0.5 convert_reduce_fusion
  71.9 0.1 broadcast_add_fusion
  71.9 0.5 select_reduce_fusion.order_ref
  72.4 0.1 compare_and_fusion
  72.5 0.1 broadcast_in_dim.62
  72.5 0.1 broadcast_in_dim.63
  72.6 0.1 reverse_bitcast_fusion.1
  72.7 0.0 copy-start.12
  72.7 0.9 copy-done.12
  73.7 0.3 copy.22
  74.0 0.3 copy.23
  74.3 0.1 convert_reduce_fusion.3
  74.4 1.2 reverse_bitcast_fusion
  75.6 0.9 fusion.2
  76.5 0.2 copy-done.13
  76.7 0.1 copy_bitcast_fusion.4
  76.8 0.0 all-to-all-done
  76.8 0.6 gather_fusion
  77.4 0.0 copy-start.14
  77.4 0.1 bitcast_select_fusion
  77.5 2.1 %collective-permute-start = (bf16[4,8,16,128]{3,2,1,0:T(8,128)(2,1)S(1)}, bf16[4,8,16,128]{3,2,1,0:T(8,128)(2,1)S(1)}, u32[]{:S(2)}, u32[]{:S(2)}) collective-permute-start(bf16[4,8,16,128]{3,2,1,0:T(8,128)(2,1)S(1)} %bitcast_select_fusion), channel_id=1, source_target_pairs={{0,16},{16,32},{32,48},{48,64},{64,80},{80,96},{96,112},{112,128},... | collective-permute-start | bytes 393224 | tf_op jit(solution)/shard_map/ppermute | solution.py:454
  79.6 1.9 %copy.21 = bf16[3,3,128,3,128]{4,3,2,1,0:T(4,128)(2,1)S(1)} copy(bf16[3,3,128,3,128]{4,2,0,1,3:T(8,128)(2,1)} %copy-done.12) | data formatting | bytes 1769472 | tf_op jit(solution)/shard_map/transpose | solution.py:423
  81.5 0.8 copy.24
  82.3 0.1 copy.40
  82.5 1.1 copy.39
  83.5 0.3 copy.25
  83.8 0.3 copy.26
  84.1 0.0 collective-permute-done.lead_ref
  84.1 2.5 %place_blocks.1 = (bf16[36,8,16,128]{3,2,1,0:T(8,128)(2,1)S(1)}, bf16[36,8,128]{2,1,0:T(8,128)(2,1)S(1)}, bf16[36,8,128]{2,1,0:T(8,128)(2,1)S(1)}) custom-call(s32[16]{0:T(128)S(1)} %select_reduce_fusion.order_ref, bf16[32,2,8,16,128]{4,3,2,1,0:T(8,128)(2,1)S(1)} %bitcast.51, bf16[4,8,16,128]{3,2,1,0:T(8,128)(2,1)S(1)} %collective-permute-done.lead_ref), custom_call_target="tpu_custom_call" | custom-call | tf_op jit(solution)/shard_map/place_blocks/pallas_call | solution.py:114
  86.6 3.4 %collective-permute-start.1 = (bf16[36,8,128]{2,1,0:T(8,128)(2,1)S(1)}, bf16[36,8,128]{2,1,0:T(8,128)(2,1)S(1)}, u32[]{:S(2)}, u32[]{:S(2)}) collective-permute-start(bf16[36,8,128]{2,1,0:T(8,128)(2,1)S(1)} %get-tuple-element.14), channel_id=1, source_target_pairs={{0,1},{1,2},{2,3},{3,4},{4,5},{5,6},{6,7},{7,8},{8,9},{9,10},{10,1... | collective-permute-start | bytes 221192 | tf_op jit(solution)/shard_map/ppermute | solution.py:429
  90.0 4.6 %collective-permute-start.2 = (bf16[36,8,128]{2,1,0:T(8,128)(2,1)S(1)}, bf16[36,8,128]{2,1,0:T(8,128)(2,1)S(1)}, u32[]{:S(2)}, u32[]{:S(2)}) collective-permute-start(bf16[36,8,128]{2,1,0:T(8,128)(2,1)S(1)} %get-tuple-element.15), channel_id=1, source_target_pairs={{1,0},{2,1},{3,2},{4,3},{5,4},{6,5},{7,6},{8,7},{9,8},{10,9},{11,1... | collective-permute-start | bytes 221192 | tf_op jit(solution)/shard_map/ppermute | solution.py:430
  94.6 8.8 %conv.2.partial_ref = f32[36,128,128]{2,1,0:T(8,128)S(1)} custom-call(f32[2,36]{1,0:T(2,128)S(1)} %add_convert_fusion.valid_ref, bf16[36,8,16,128]{3,2,1,0:T(8,128)(2,1)S(1)} %get-tuple-element.13.frames_ref, bf16[1152,384]{1,0:T(8,128)(2,1)S(1)} %bitcast.54), custom_call_target="tpu_custom_call" | custom-call | flops 4076863488 | bytes 4194304 | tf_op jit(solution)/shard_map/conv/pallas_call | solution.py:175
  103.4 0.0 collective-permute-done.1.left_ref
  103.4 0.0 collective-permute-done.2.right_ref
  103.4 0.0 copy-start.9
  103.4 0.0 copy-start.10
  103.4 4.0 %finish_hidden.1 = (f32[36,128,128]{2,1,0:T(8,128)S(1)}, f32[16,24,128]{2,1,0:T(8,128)}) custom-call(f32[2,36]{1,0:T(2,128)S(1)} %add_convert_fusion.valid_ref, f32[36,128,128]{2,1,0:T(8,128)S(1)} %conv.2.partial_ref, bf16[36,8,128]{2,1,0:T(8,128)(2,1)S(1)} %collective-permute-done.1.left_ref, bf16[36,8,128]{2,1,0:T(8,128)(2,1)S(1)} %collective-permute-done.2.right_ref, ...), custom_call_target="tpu_custom_call" | custom-call | tf_op jit(solution)/shard_map/finish_hidden/pallas_call | solution.py:270
  107.4 1.4 copy-done.1
  108.9 5.3 %all-to-all-start.1 = ((f32[16,24,128]{2,1,0:T(8,128)}), f32[16,24,128]{2,1,0:T(8,128)S(1)}, u32[]{:S(2)}, u32[]{:S(2)}) async-start(f32[16,24,128]{2,1,0:T(8,128)} %get-tuple-element.17), calls=%async_computation.1 | async-start | bytes 393216 | tf_op jit(solution)/shard_map/all_to_all | solution.py:461
  114.1 0.1 copy_bitcast_fusion.2
  114.2 7.1 %all-to-all-done.1.stats_ref = f32[16,24,128]{2,1,0:T(8,128)S(1)} async-done(((f32[16,24,128]{2,1,0:T(8,128)}), f32[16,24,128]{2,1,0:T(8,128)S(1)}, u32[]{:S(2)}, u32[]{:S(2)}) %all-to-all-start.1) | async-done | bytes 196640 | tf_op jit(solution)/shard_map/all_to_all | solution.py:461
  121.4 1.7 %copy-done.2 = f32[36,128,128]{2,1,0:T(8,128)S(1)} copy-done((f32[36,128,128]{2,1,0:T(8,128)S(1)}, f32[36,128,128]{2,1,0:T(8,128)}, u32[]{:S(2)}) %copy-start.2) | copy-done | bytes 2359320
  123.1 1.5 %norm_silu.1 = (bf16[36,8,16,128]{3,2,1,0:T(8,128)(2,1)S(1)}, bf16[36,8,128]{2,1,0:T(8,128)(2,1)S(1)}, bf16[36,8,128]{2,1,0:T(8,128)(2,1)S(1)}) custom-call(f32[36,128,128]{2,1,0:T(8,128)S(1)} %copy-done.2, f32[16,24,128]{2,1,0:T(8,128)S(1)} %all-to-all-done.1.stats_ref, f32[1,128]{1,0:T(1,128)S(1)} %bitcast.55, f32[1,128]{1,0:T(1,128)S(1)} %bitcast.56), custom_call_target="tpu_custom_call" | custom-call | tf_op jit(solution)/shard_map/norm_silu/pallas_call | solution.py:342
  124.6 2.2 %collective-permute-start.3 = (bf16[36,8,128]{2,1,0:T(8,128)(2,1)S(1)}, bf16[36,8,128]{2,1,0:T(8,128)(2,1)S(1)}, u32[]{:S(2)}, u32[]{:S(2)}) collective-permute-start(bf16[36,8,128]{2,1,0:T(8,128)(2,1)S(1)} %get-tuple-element.19), channel_id=1, source_target_pairs={{0,1},{1,2},{2,3},{3,4},{4,5},{5,6},{6,7},{7,8},{8,9},{9,10},{10,1... | collective-permute-start | bytes 221192 | tf_op jit(solution)/shard_map/ppermute | solution.py:429
  126.8 5.7 %collective-permute-start.4 = (bf16[36,8,128]{2,1,0:T(8,128)(2,1)S(1)}, bf16[36,8,128]{2,1,0:T(8,128)(2,1)S(1)}, u32[]{:S(2)}, u32[]{:S(2)}) collective-permute-start(bf16[36,8,128]{2,1,0:T(8,128)(2,1)S(1)} %get-tuple-element.20), channel_id=1, source_target_pairs={{1,0},{2,1},{3,2},{4,3},{5,4},{6,5},{7,6},{8,7},{9,8},{10,9},{11,1... | collective-permute-start | bytes 221192 | tf_op jit(solution)/shard_map/ppermute | solution.py:430
  132.6 0.0 copy-start.6
  132.6 1.2 copy-done.6
  133.7 8.8 %conv.3.partial_ref = f32[36,128,128]{2,1,0:T(8,128)S(1)} custom-call(f32[2,36]{1,0:T(2,128)S(1)} %add_convert_fusion.valid_ref, bf16[36,8,16,128]{3,2,1,0:T(8,128)(2,1)S(1)} %get-tuple-element.18.frames_ref, bf16[1152,384]{1,0:T(8,128)(2,1)S(1)} %bitcast.53), custom_call_target="tpu_custom_call" | custom-call | flops 4076863488 | bytes 4194304 | tf_op jit(solution)/shard_map/conv/pallas_call | solution.py:175
  142.5 0.0 collective-permute-done.3.left_ref
  142.5 0.0 collective-permute-done.4.right_ref
  142.6 2.6 %finish_output.1 = bf16[32,8,16,128]{3,2,1,0:T(8,128)(2,1)} custom-call(f32[2,36]{1,0:T(2,128)S(1)} %add_convert_fusion.valid_ref, f32[36,128,128]{2,1,0:T(8,128)S(1)} %conv.3.partial_ref, bf16[36,8,128]{2,1,0:T(8,128)(2,1)S(1)} %collective-permute-done.3.left_ref, bf16[36,8,128]{2,1,0:T(8,128)(2,1)S(1)} %collective-permute-done.4.right_ref, ...), custom_call_target="tpu_custom_call" | custom-call | tf_op jit(solution)/shard_map/finish_output/pallas_call | solution.py:381
  (35 shorter events, 0.1 us)
Async XLA Ops:
  0.0 1.6 %copy-start.3 = (bf16[32,2,8,16,128]{4,3,2,1,0:T(8,128)(2,1)S(1)}, bf16[32,2,8,16,128]{4,3,2,1,0:T(8,128)(2,1)}, u32[]{:S(2)}) copy-start(bf16[32,2,8,16,128]{4,3,2,1,0:T(8,128)(2,1)} %video_ref.1) | copy-start | bytes 6291460
  1.6 0.7 copy-start.7
  3.7 1.3 copy-start
  5.1 10.3 %copy-start.18 = (s32[8]{0:T(128)S(1)}, s32[8]{0:T(128)}, u32[]{:S(2)}) copy-start(s32[8]{0:T(128)} %param.10) | copy-start | bytes 100
  5.1 10.5 %copy-start.19 = (u32[256]{0:T(256)S(1)}, u32[256]{0:T(256)}, u32[]{:S(2)}) copy-start(u32[256]{0:T(256)} %constant.46) | copy-start | bytes 3076
  5.1 11.7 %copy-start.8 = (s32[32]{0:T(128)S(1)}, s32[32]{0:T(128)}, u32[]{:S(2)}) copy-start(s32[32]{0:T(128)} %slot_ref.1) | copy-start | bytes 388
  5.1 67.5 %copy-start.17 = (bf16[3,3,3,128,128]{4,3,2,1,0:T(8,128)(2,1)S(1)}, bf16[3,3,3,128,128]{4,3,2,1,0:T(8,128)(2,1)}, u32[]{:S(2)}) copy-start(bf16[3,3,3,128,128]{4,3,2,1,0:T(8,128)(2,1)} %param.11) | copy-start | bytes 2654212
  5.1 71.7 %all-to-all-start = ((bf16[16,2,2,8,16,128]{5,4,3,2,1,0:T(8,128)(2,1)}), bf16[16,2,2,8,16,128]{5,4,3,2,1,0:T(8,128)(2,1)S(1)}, u32[]{:S(2)}, u32[]{:S(2)}) async-start(bf16[16,2,2,8,16,128]{5,4,3,2,1,0:T(8,128)(2,1)} %bitcast.52), calls=%async_computation | async-start | bytes 4194304 | tf_op jit(solution)/shard_map/all_to_all | solution.py:445
  72.7 0.9 copy-start.12
  75.6 1.2 copy-start.13
  77.4 4.1 %copy-start.14 = (bf16[3,3,128,3,128]{4,2,0,1,3:T(8,128)(2,1)S(1)}, bf16[3,3,128,3,128]{4,2,0,1,3:T(8,128)(2,1)}, u32[]{:S(2)}) copy-start(bf16[3,3,128,3,128]{4,2,0,1,3:T(8,128)(2,1)} %copy-done.13) | copy-start | bytes 2654212
  77.5 6.6 %collective-permute-start = (bf16[4,8,16,128]{3,2,1,0:T(8,128)(2,1)S(1)}, bf16[4,8,16,128]{3,2,1,0:T(8,128)(2,1)S(1)}, u32[]{:S(2)}, u32[]{:S(2)}) collective-permute-start(bf16[4,8,16,128]{3,2,1,0:T(8,128)(2,1)S(1)} %bitcast_select_fusion), channel_id=1, source_target_pairs={{0,16},{16,32},{32,48},{48,64},{64,80},{80,96},{96,112},{112,128},... | collective-permute-start | bytes 393224 | tf_op jit(solution)/shard_map/ppermute | solution.py:454
  82.3 1.2 copy-start.16
  82.3 1.5 %copy-start.15 = (bf16[1,3,128,3,128]{4,2,0,1,3:T(8,128)(2,1)S(1)}, bf16[1,3,128,3,128]{4,2,0,1,3:T(8,128)(2,1)}, u32[]{:S(2)}) copy-start(bf16[1,3,128,3,128]{4,2,0,1,3:T(8,128)(2,1)} %get-tuple-element.26) | copy-start | bytes 884740
  86.6 16.8 %copy-start.4 = (bf16[36,8,16,128]{3,2,1,0:T(8,128)(2,1)}, bf16[36,8,16,128]{3,2,1,0:T(8,128)(2,1)S(1)}, u32[]{:S(2)}) copy-start(bf16[36,8,16,128]{3,2,1,0:T(8,128)(2,1)S(1)} %get-tuple-element.13.frames_ref) | copy-start | bytes 3538948
  86.6 16.8 %collective-permute-start.1 = (bf16[36,8,128]{2,1,0:T(8,128)(2,1)S(1)}, bf16[36,8,128]{2,1,0:T(8,128)(2,1)S(1)}, u32[]{:S(2)}, u32[]{:S(2)}) collective-permute-start(bf16[36,8,128]{2,1,0:T(8,128)(2,1)S(1)} %get-tuple-element.14), channel_id=1, source_target_pairs={{0,1},{1,2},{2,3},{3,4},{4,5},{5,6},{6,7},{7,8},{8,9},{9,10},{10,1... | collective-permute-start | bytes 221192 | tf_op jit(solution)/shard_map/ppermute | solution.py:429
  90.0 13.4 %collective-permute-start.2 = (bf16[36,8,128]{2,1,0:T(8,128)(2,1)S(1)}, bf16[36,8,128]{2,1,0:T(8,128)(2,1)S(1)}, u32[]{:S(2)}, u32[]{:S(2)}) collective-permute-start(bf16[36,8,128]{2,1,0:T(8,128)(2,1)S(1)} %get-tuple-element.15), channel_id=1, source_target_pairs={{1,0},{2,1},{3,2},{4,3},{5,4},{6,5},{7,6},{8,7},{9,8},{10,9},{11,1... | collective-permute-start | bytes 221192 | tf_op jit(solution)/shard_map/ppermute | solution.py:430
  103.4 18.0 %copy-start.9 = (f32[128]{0:T(128)S(1)}, f32[128]{0:T(128)}, u32[]{:S(2)}) copy-start(f32[128]{0:T(128)} %param.12) | copy-start | bytes 1540
  103.4 18.0 %copy-start.10 = (f32[128]{0:T(128)S(1)}, f32[128]{0:T(128)}, u32[]{:S(2)}) copy-start(f32[128]{0:T(128)} %param.13) | copy-start | bytes 1540
  107.4 1.4 copy-start.1
  108.9 12.5 %all-to-all-start.1 = ((f32[16,24,128]{2,1,0:T(8,128)}), f32[16,24,128]{2,1,0:T(8,128)S(1)}, u32[]{:S(2)}, u32[]{:S(2)}) async-start(f32[16,24,128]{2,1,0:T(8,128)} %get-tuple-element.17), calls=%async_computation.1 | async-start | bytes 393216 | tf_op jit(solution)/shard_map/all_to_all | solution.py:461
  121.4 1.7 %copy-start.2 = (f32[36,128,128]{2,1,0:T(8,128)S(1)}, f32[36,128,128]{2,1,0:T(8,128)}, u32[]{:S(2)}) copy-start(f32[36,128,128]{2,1,0:T(8,128)} %copy-done.1) | copy-start | bytes 7077892
  124.6 17.9 %collective-permute-start.3 = (bf16[36,8,128]{2,1,0:T(8,128)(2,1)S(1)}, bf16[36,8,128]{2,1,0:T(8,128)(2,1)S(1)}, u32[]{:S(2)}, u32[]{:S(2)}) collective-permute-start(bf16[36,8,128]{2,1,0:T(8,128)(2,1)S(1)} %get-tuple-element.19), channel_id=1, source_target_pairs={{0,1},{1,2},{2,3},{3,4},{4,5},{5,6},{6,7},{7,8},{8,9},{9,10},{10,1... | collective-permute-start | bytes 221192 | tf_op jit(solution)/shard_map/ppermute | solution.py:429
  126.8 15.7 %collective-permute-start.4 = (bf16[36,8,128]{2,1,0:T(8,128)(2,1)S(1)}, bf16[36,8,128]{2,1,0:T(8,128)(2,1)S(1)}, u32[]{:S(2)}, u32[]{:S(2)}) collective-permute-start(bf16[36,8,128]{2,1,0:T(8,128)(2,1)S(1)} %get-tuple-element.20), channel_id=1, source_target_pairs={{1,0},{2,1},{3,2},{4,3},{5,4},{6,5},{7,6},{8,7},{9,8},{10,9},{11,1... | collective-permute-start | bytes 221192 | tf_op jit(solution)/shard_map/ppermute | solution.py:430
  132.6 1.2 copy-start.6
  133.7 8.8 %copy-start.5 = (bf16[36,8,16,128]{3,2,1,0:T(8,128)(2,1)S(1)}, bf16[36,8,16,128]{3,2,1,0:T(8,128)(2,1)}, u32[]{:S(2)}) copy-start(bf16[36,8,16,128]{3,2,1,0:T(8,128)(2,1)} %copy-done.4) | copy-start | bytes 3538948
  133.7 8.8 %copy-start.11 = (f32[128]{0:T(128)S(1)}, f32[128]{0:T(128)}, u32[]{:S(2)}) copy-start(f32[128]{0:T(128)} %param.15) | copy-start | bytes 1540

commit v2 on v0

v2 whole, which is shorter than its diff:
```python
import functools

import jax
import jax.numpy as jnp
from jax import lax
from jax.experimental import pallas as pl
from jax.experimental.pallas import tpu as pltpu
from jax.sharding import PartitionSpec as P

GROUPS = 32
OWN = 16
CAP = 2
C = 128
ROWS = 8
COLS = 16
POS = ROWS * COLS
LEAD = 4
CHUNK = 4
EPSILON = 1e-06
HALF = 24
PITCH = 24
UNROLL = 8
PAIR_ROWS = CAP * 2 * POS
INFO_ROWS = 16
MIB = 1024 * 1024

f32 = jnp.float32
bf16 = jnp.bfloat16


def vmem():
    return pl.BlockSpec(memory_space=pltpu.VMEM)


def smem():
    return pl.BlockSpec(memory_space=pltpu.SMEM)


def hbm():
    return pl.BlockSpec(memory_space=pl.ANY)


def params(mib=16):
    return pltpu.CompilerParams(vmem_limit_bytes=mib * MIB)


def hbm_only():
    return pl.BlockSpec(memory_space=pltpu.HBM)


def send_kernel(slot_ref, video_ref, out_ref, count, info, info_out, sems):
    slots = slot_ref.shape[0]
    owners = count.shape[0]
    for owner in range(owners):
        count[owner] = 0
    info[...] = jnp.zeros_like(info)
    lane = lax.broadcasted_iota(jnp.int32, info.shape[1:], 1)

    def copy(slot, owner, rank):
        block_rows = PAIR_ROWS // CAP
        rows = pl.ds(pl.multiple_of(rank * block_rows, block_rows), block_rows)
        return pltpu.make_async_copy(
            video_ref.at[slot], out_ref.at[owner, rows], sems.at[slot]
        )

    for slot in range(slots):
        block = slot_ref[slot]

        @pl.when(block >= 0)
        def _():
            owner = block >> 4
            rank = count[owner]
            count[owner] = rank + 1
            copy(slot, owner, rank).start()
            mark = jnp.where(lane == (block & (OWN - 1)), (rank + 1).astype(f32), 0.0)
            info[owner] = info[owner] + mark

    for owner in range(owners):
        info_out[owner] = jnp.concatenate([info[owner]] * 2, axis=0).astype(bf16)
    notes = pltpu.make_async_copy(
        info_out, out_ref.at[:, pl.ds(PAIR_ROWS, INFO_ROWS)], sems.at[slots]
    )
    notes.start()
    for slot in range(slots):

        @pl.when(slot_ref[slot] >= 0)
        def _():
            copy(slot, 0, 0).wait()

    notes.wait()


def send_blocks(slot_block, video, owners):
    slots = video.shape[0]
    return pl.pallas_call(
        send_kernel,
        out_shape=jax.ShapeDtypeStruct((owners, PAIR_ROWS + INFO_ROWS, C), video.dtype),
        in_specs=[smem(), hbm_only()],
        out_specs=hbm_only(),
        scratch_shapes=[
            pltpu.SMEM((owners,), jnp.int32),
            pltpu.VMEM((owners, 8, C), f32),
            pltpu.VMEM((owners, INFO_ROWS, C), bf16),
            pltpu.SemaphoreType.DMA((slots + 1,)),
        ],
        compiler_params=params(62),
        name="send_blocks",
    )(slot_block, video.reshape(slots, PAIR_ROWS // CAP, C))


def order_kernel(arrived_ref, order_ref, tail_ref, notes, picks, sems):
    owners = arrived_ref.shape[0]
    note = pltpu.make_async_copy(
        arrived_ref.at[:, pl.ds(PAIR_ROWS, INFO_ROWS)], notes, sems.at[0]
    )
    note.start()
    note.wait()
    total = jnp.zeros((8, C), f32)
    for source in range(owners):
        rank = notes[source].astype(f32)[0:8]
        total = total + jnp.where(rank > 0.0, rank + (CAP * source - 1.0), 0.0)
    picks[...] = total.astype(jnp.int32)
    to_scalars = pltpu.make_async_copy(picks.at[pl.ds(0, 1)], order_ref, sems.at[0])
    to_scalars.start()
    to_scalars.wait()
    copies = []
    for k in range(LEAD // 2):
        copies.append(
            pltpu.make_async_copy(
                block_at(arrived_ref, order_ref[0, OWN - LEAD // 2 + k]),
                tail_ref.at[pl.ds(k * 2 * POS, 2 * POS)],
                sems.at[k],
            )
        )
        copies[-1].start()
    for copy in copies:
        copy.wait()


def block_at(arrived_ref, arrival):
    block_rows = PAIR_ROWS // CAP
    rows = pl.ds(pl.multiple_of((arrival & 1) * block_rows, block_rows), block_rows)
    return arrived_ref.at[arrival >> 1, rows]


def block_order(arrived):
    return pl.pallas_call(
        order_kernel,
        out_shape=(
            jax.ShapeDtypeStruct((1, C), jnp.int32),
            jax.ShapeDtypeStruct((LEAD * POS, C), bf16),
        ),
        in_specs=[hbm_only()],
        out_specs=(smem(), vmem()),
        scratch_shapes=[
            pltpu.VMEM((arrived.shape[0], INFO_ROWS, C), bf16),
            pltpu.VMEM((8, C), jnp.int32),
            pltpu.SemaphoreType.DMA((LEAD // 2,)),
        ],
        compiler_params=params(),
        name="block_order",
    )(arrived)


def edge_rows(wide, column):
    return wide[pl.ds(column, wide.shape[0] // COLS, stride=COLS), :]


EDGE_ROWS = (LEAD + 2 * OWN) * ROWS


def put_edges(wide, start, left_ref, right_ref):
    count = wide.shape[0] // COLS
    for c in range(2):
        at = pl.ds(c * EDGE_ROWS + start, count)
        left_ref[at] = edge_rows(wide, c).astype(bf16)
        right_ref[at] = edge_rows(wide, COLS - 2 + c).astype(bf16)


def place_kernel(order_ref, arrived_ref, frames_ref, left_ref, right_ref, wide, sems):
    copies = [
        pltpu.make_async_copy(
            block_at(arrived_ref, order_ref[0, k]),
            frames_ref.at[pl.ds(k * 2 * POS, 2 * POS)],
            sems.at[k],
        )
        for k in range(OWN)
    ]
    for copy in copies:
        copy.start()
    for k in range(OWN):
        copies[k].wait()
        wide[k % 2] = frames_ref[k * 2 * POS : (k + 1) * 2 * POS].astype(f32)
        put_edges(wide.at[k % 2], (LEAD + 2 * k) * ROWS, left_ref, right_ref)


def edge_shape(dtype):
    return jax.ShapeDtypeStruct((2 * EDGE_ROWS, C), dtype)


def place_blocks(order, arrived):
    edge = edge_shape(bf16)
    return pl.pallas_call(
        place_kernel,
        out_shape=(jax.ShapeDtypeStruct((2 * OWN * POS, C), bf16), edge, edge),
        in_specs=[smem(), hbm_only()],
        out_specs=(vmem(), vmem(), vmem()),
        scratch_shapes=[
            pltpu.VMEM((2, 2 * POS, C), f32),
            pltpu.SemaphoreType.DMA((OWN,)),
        ],
        compiler_params=params(),
        name="place_blocks",
    )(order, arrived)


def lead_kernel(lead_ref, left_in, right_in, left_ref, right_ref, wide):
    wide[...] = lead_ref[...].astype(f32)
    left_ref[...] = left_in[...]
    right_ref[...] = right_in[...]
    put_edges(wide, 0, left_ref, right_ref)


def lead_edges(lead, left, right):
    edge = edge_shape(bf16)
    return pl.pallas_call(
        lead_kernel,
        out_shape=(edge, edge),
        in_specs=[vmem()] * 3,
        out_specs=(vmem(), vmem()),
        scratch_shapes=[pltpu.VMEM((LEAD * POS, C), f32)],
        compiler_params=params(),
        name="lead_edges",
    )(lead, left, right)


def join_weight(weight_ref, joined):
    for j in range(3):
        for i in range(3):
            for lag in range(3):
                at = (3 * j + i) * C
                joined[at : at + C, lag * C : (lag + 1) * C] = weight_ref[2 - lag, i, j]


def conv_chunk(valid_ref, start, count, wide, taps, joined, carry, sides):
    rows = count * ROWS
    for at in range(rows):
        q, r = at // ROWS, at % ROWS + 1
        base = at * PITCH + 8
        for j in range(3):
            taps[j, q, r] = wide[base + j - 1 : base + j - 1 + COLS].astype(bf16)
    pieces = [
        taps[j, 0:count, i : i + ROWS].reshape(count * POS, C) for j in range(3) for i in range(3)
    ]
    if sides:
        row = lax.broadcasted_iota(jnp.int32, (2 * rows, C), 0) % ROWS
        for j in range(3):
            column = jnp.concatenate(
                [wide[pl.ds(at + j, rows, stride=PITCH), :] for at in (6, 7 + COLS)], axis=0
            )
            above = jnp.where(row == 0, 0.0, pltpu.roll(column, 1, 0))
            below = jnp.where(row == ROWS - 1, 0.0, pltpu.roll(column, 2 * rows - 1, 0))
            for i, piece in enumerate((above, column, below)):
                at = 3 * j + i
                pieces[at] = jnp.concatenate([pieces[at], piece.astype(bf16)], axis=0)
    product = jnp.dot(
        jnp.concatenate(pieces, axis=1), joined[...], preferred_element_type=f32
    )

    def part(q, lag):
        lanes = slice(lag * C, (lag + 1) * C)
        own = product[q * POS : (q + 1) * POS, lanes]
        if not sides:
            return own
        left = count * POS + q * ROWS
        right = left + rows
        edges = [product[at : at + ROWS, lanes] for at in (left, right)]
        return jnp.concatenate([own] + edges, axis=0)

    totals = []
    for q in range(count):
        one = part(q - 1, 1) if q >= 1 else carry[0]
        two = part(q - 2, 2) if q >= 2 else carry[1 + q]
        totals.append(
            part(q, 0) + valid_ref[0, start + q] * one + valid_ref[1, start + q] * two
        )
    carry[0] = part(count - 1, 1)
    carry[1] = part(count - 2, 2)
    carry[2] = part(count - 1, 2)
    return totals


def conv_scratch(sides):
    return [
        pltpu.VMEM((UNROLL, CHUNK * ROWS * PITCH + 8, C), f32),
        pltpu.VMEM((UNROLL, 3, CHUNK, ROWS + 2, COLS, C), bf16),
        pltpu.VMEM((9 * C, 3 * C), bf16),
        pltpu.VMEM((3, POS + (2 * ROWS if sides else 0), C), f32),
    ]


def conv_setup(weight_ref, taps, joined, carry):
    join_weight(weight_ref, joined)
    carry[...] = jnp.zeros_like(carry)
    for u in range(UNROLL):
        for j in range(3):
            for edge in (0, ROWS + 1):
                taps[u, j, :, edge] = jnp.zeros((CHUNK, COLS, C), bf16)


def put_column(wide, at, column):
    wide[pl.ds(at, column.shape[0], stride=PITCH), :] = column


def over_chunks(chunk_step):
    def step(trip, done):
        for u in range(UNROLL):
            chunk_step(u, (trip * UNROLL + u) * CHUNK)
        return done

    lax.fori_loop(0, 2 * OWN // CHUNK // UNROLL, step, 0)


def group_total(entries):
    lane = lax.broadcasted_iota(jnp.int32, entries.shape, 1)
    for bit in (1, 2):
        up = pltpu.roll(entries, C - bit, 1)
        down = pltpu.roll(entries, bit, 1)
        entries = entries + jnp.where((lane & bit) == 0, up, down)
    return entries


def precise_dot(a, b):
    return jnp.dot(a, b, precision=lax.Precision.HIGHEST, preferred_element_type=f32)


def hidden_kernel(
    valid_ref, lead_ref, frames_ref, left_ref, right_ref, weight_ref,
    hidden_ref, edge_l_ref, edge_r_ref, stats_ref,
    wide, taps, joined, carry, means, spreads,
):
    conv_setup(weight_ref, taps, joined, carry)
    means[...] = jnp.zeros_like(means)
    spreads[...] = jnp.zeros_like(spreads)

    def chunk_step(u, start, count, source, at):
        for row in range(count * ROWS):
            here = source[pl.ds(pl.multiple_of(at + row * COLS, COLS), COLS)]
            wide[u, row * PITCH + 8 : row * PITCH + 8 + COLS] = here.astype(f32)
        for c in range(2):
            edge_at = pl.multiple_of(c * EDGE_ROWS + start * ROWS, 2 * ROWS)
            edge_at = pl.ds(edge_at, count * ROWS)
            put_column(wide.at[u], 6 + c, left_ref[edge_at].astype(f32))
            put_column(wide.at[u], 8 + COLS + c, right_ref[edge_at].astype(f32))
        totals = conv_chunk(
            valid_ref, start, count, wide.at[u], taps.at[u], joined, carry, True
        )
        for q in range(count):
            frame = start + q
            own = totals[q][:POS]
            hidden_ref[frame] = own
            edge_l_ref[frame] = totals[q][POS : POS + ROWS]
            edge_r_ref[frame] = totals[q][POS + ROWS :]
            mean = jnp.sum(own, axis=0, keepdims=True) / POS
            centred = own - mean
            means[pl.ds(frame, 1), :] = mean
            spreads[pl.ds(frame, 1), :] = jnp.sum(centred * centred, axis=0, keepdims=True)

    for start in range(0, LEAD, CHUNK):
        chunk_step(0, start, min(CHUNK, LEAD), lead_ref, start * POS)
    over_chunks(lambda u, at: chunk_step(u, LEAD + at, CHUNK, frames_ref, at * POS))

    mean = group_total(means[...]) / 4
    off = means[...] - mean
    spread = group_total(spreads[...] + POS * off * off)
    channel = lax.broadcasted_iota(jnp.int32, (C, C), 0)
    lane = lax.broadcasted_iota(jnp.int32, (C, C), 1)
    packed = jnp.zeros((HALF, C), f32)
    for q, part in enumerate((mean[:HALF], spread[:HALF], mean[HALF:], spread[HALF:])):
        picks = (channel == 4 * (lane - GROUPS * q)) & (lane // GROUPS == q)
        packed = packed + precise_dot(part, picks.astype(f32))
    for peer in range(stats_ref.shape[0]):
        stats_ref[peer] = packed


def first_layer(valid, lead, frames, left, right, weight, tiles):
    length = LEAD + 2 * OWN
    edge = jax.ShapeDtypeStruct((length, ROWS, C), f32)
    return pl.pallas_call(
        hidden_kernel,
        out_shape=(
            jax.ShapeDtypeStruct((length, POS, C), f32),
            edge,
            edge,
            jax.ShapeDtypeStruct((tiles, HALF, C), f32),
        ),
        in_specs=[smem()] + [vmem()] * 5,
        out_specs=(vmem(),) * 4,
        scratch_shapes=conv_scratch(True)
        + [pltpu.VMEM((2 * HALF, C), f32), pltpu.VMEM((2 * HALF, C), f32)],
        compiler_params=params(),
        name="first_layer",
    )(valid, lead, frames, left, right, weight)


def combine_stats(stats_ref, gain_ref, means, scales):
    tiles = stats_ref.shape[0]
    here = POS * (C // GROUPS)
    lane = lax.broadcasted_iota(jnp.int32, (HALF, C), 1)
    is_mean = (lane // GROUPS) % 2 == 0
    total = stats_ref[0]
    for peer in range(1, tiles):
        total = total + stats_ref[peer]
    mean = total / tiles
    apart = jnp.zeros((HALF, C), f32)
    for peer in range(tiles):
        off = stats_ref[peer] - mean
        apart = apart + off * off
    apart = jnp.where(is_mean, apart, 0.0)
    variance = (total + here * pltpu.roll(apart, GROUPS, 1)) / (here * tiles)
    packed = jnp.where(is_mean, mean, lax.rsqrt(jnp.where(is_mean, 1.0, variance) + EPSILON))
    channel = lax.broadcasted_iota(jnp.int32, (C, C), 1)
    source = lax.broadcasted_iota(jnp.int32, (C, C), 0)
    for q in range(4):
        picks = (source == channel // (C // GROUPS) + GROUPS * q).astype(f32)
        target = scales if q % 2 else means
        half = pl.ds((q // 2) * HALF, HALF)
        target[half, :] = precise_dot(packed, picks)
    scales[...] = scales[...] * gain_ref[...]


def silu(v):
    return v * (1.0 / (1.0 + jnp.exp(-v)))


def output_kernel(
    valid_ref, hidden_ref, edge_l_ref, edge_r_ref, stats_ref, frames_ref,
    gain_ref, norm_bias_ref, weight_ref, bias_ref, out_ref,
    wide, taps, joined, carry, means, scales, halo,
):
    conv_setup(weight_ref, taps, joined, carry)
    combine_stats(stats_ref, gain_ref, means, scales)
    has_left = valid_ref[2, 0]
    has_right = valid_ref[2, 1]

    def norm(hidden, frame):
        centred = hidden - means[pl.ds(frame, 1), :]
        return silu(centred * scales[pl.ds(frame, 1), :] + norm_bias_ref[...])

    def chunk_step(u, start, count):
        for q in range(count):
            frame = start + q
            active = norm(hidden_ref[frame], frame)
            for r in range(ROWS):
                at = (q * ROWS + r) * PITCH + 8
                wide[u, at : at + COLS] = active[r * COLS : (r + 1) * COLS]
            halo[u, 0, q * ROWS : (q + 1) * ROWS] = norm(edge_l_ref[frame], frame) * has_left
            halo[u, 1, q * ROWS : (q + 1) * ROWS] = norm(edge_r_ref[frame], frame) * has_right
        put_column(wide.at[u], 7, halo[u, 0, 0 : count * ROWS])
        put_column(wide.at[u], 8 + COLS, halo[u, 1, 0 : count * ROWS])
        return conv_chunk(
            valid_ref, start, count, wide.at[u], taps.at[u], joined, carry, False
        )

    def own_chunk(u, start):
        totals = chunk_step(u, LEAD + start, CHUNK)
        for q in range(CHUNK):
            rows = pl.ds(pl.multiple_of((start + q) * POS, POS), POS)
            total = frames_ref[rows].astype(f32) + (totals[q] + bias_ref[...])
            out_ref[rows] = total.astype(bf16)

    chunk_step(0, LEAD - 2, 2)
    over_chunks(own_chunk)


def second_layer(valid, hidden, edge_l, edge_r, stats, frames, gain, norm_bias, weight, bias):
    return pl.pallas_call(
        output_kernel,
        out_shape=jax.ShapeDtypeStruct(frames.shape, bf16),
        in_specs=[smem()] + [vmem()] * 9,
        out_specs=vmem(),
        scratch_shapes=conv_scratch(False)
        + [
            pltpu.VMEM((2 * HALF, C), f32),
            pltpu.VMEM((2 * HALF, C), f32),
            pltpu.VMEM((UNROLL, 2, CHUNK * ROWS, C), f32),
        ],
        compiler_params=params(),
        name="second_layer",
    )(valid, hidden, edge_l, edge_r, stats, frames, gain, norm_bias, weight, bias)


def lag_masks(clip_frames, first_frame, length):
    clip_ends = jnp.cumsum(clip_frames)

    def clip_of(frames):
        ids = jnp.sum((frames[:, None] >= clip_ends[None, :]).astype(jnp.int32), axis=1)
        return jnp.where(frames < 0, -1, ids)

    frames = first_frame + jnp.arange(length, dtype=jnp.int32)
    here = clip_of(frames)
    return jnp.stack([clip_of(frames - lag) == here for lag in (1, 2)])


def swap_edges(left, right):
    count = lax.axis_size("tile")
    from_left = lax.ppermute(right, "tile", [(i, i + 1) for i in range(count - 1)])
    from_right = lax.ppermute(left, "tile", [(i + 1, i) for i in range(count - 1)])
    return from_left, from_right


def shards(
    video, slot_block, clip_frames, conv1_weight, norm_gain, norm_bias, conv2_weight, conv2_bias
):
    owners = lax.axis_size("tm")
    tiles = lax.axis_size("tile")
    position = lax.axis_index("tm")
    tile = lax.axis_index("tile")
    length = 2 * OWN

    outgoing = send_blocks(slot_block, video, owners)
    arrived = lax.all_to_all(outgoing, "tm", split_axis=0, concat_axis=0, tiled=True)

    inside = jnp.stack([tile > 0, tile < tiles - 1] + [tile < 0] * (length + LEAD - 2))
    valid = jnp.concatenate(
        [lag_masks(clip_frames, position * length - LEAD, length + LEAD), inside[None]]
    ).astype(f32)

    order, tail = block_order(arrived)
    lead = lax.ppermute(tail, "tm", [(i, i + 1) for i in range(owners - 1)])
    frames, left, right = place_blocks(order, arrived)
    left, right = lead_edges(lead, left, right)
    from_left, from_right = swap_edges(left, right)
    hidden, edge_l, edge_r, stats = first_layer(
        valid, lead, frames, from_left, from_right, conv1_weight, tiles
    )
    stats = lax.all_to_all(stats, "tile", split_axis=0, concat_axis=0, tiled=True)
    encoded = second_layer(
        valid, hidden, edge_l, edge_r, stats, frames, norm_gain[None], norm_bias[None],
        conv2_weight, conv2_bias[None],
    )
    return encoded.reshape((length,) + video.shape[2:])


def solution(mesh):
    placed = (P("tm", None, None, "tile", None), P("tm"), P(), P(), P(), P(), P(), P())
    return jax.shard_map(
        shards, mesh=mesh, in_specs=placed, out_specs=P("tm", None, "tile", None), check_vma=False
    )
```

time: 346 us -> 173 us (0.50); the launches traced: 342 us -> 173 us
  blocking collectives: 145 us -> 16.7 us
  Pallas kernels: 0 us -> 56.4 us
  local copies, waits for them, and re-layouts: 49.2 us -> 1.33 us
  other arithmetic: 42.6 us -> 0.3 us
  matrix products: 16.3 us -> 0 us
  starting transfers between devices: 30.5 us -> 41.1 us
    psum x2 -> x0, blocking collectives: 145 us -> none  [the longest x1 75.8 us: norm_silu(): summed = lax.psum(jnp.sum(grouped, axis=(1, 2, 4), keepdims=True), 'tile')]
    pallas_call x0 -> x6, Pallas kernels: none -> 56.4 us  [the longest x1 35.8 us: send_blocks(): pl.pallas_call(send_kernel, out_shape=jax.ShapeDtypeStruct((owners, PAIR_...]
    all_to_all x1, starting transfers between devices: 7.23 us -> 34.3 us  [shards(): lax.all_to_all(outgoing, 'tm', split_axis=0, concat_axis=0, tiled=True)]
    reduce_sum x6 -> x1, other arithmetic: 26.7 us -> 0.09 us  [clip_of(): jnp.sum((frames[:, None] >= clip_ends[None, :]).astype(jnp.int32), axis=1)]
    unnamed x67 -> x12, local copies, waits for them, and re-layouts: 24.3 us -> 1.19 us
    all_to_all x0 -> x1, blocking collectives: none -> 16.7 us  [shards(): lax.all_to_all(stats, 'tile', split_axis=0, concat_axis=0, tiled=True)]
    dot_general x6 -> x0, matrix products: 16.3 us -> none  [causal_conv(): jnp.dot(stacked, kernel, preferred_element_type=jnp.float32)]
    another operation x1, local copies, waits for them, and re-layouts: 10.8 us -> 0.14 us  [shards(): jnp.stack([tile > 0, tile < tiles - 1] + [tile < 0] * (length + LEAD - 2))]
  transfers between devices with their start and end apart: 8 -> 4, of which waited for: 7 -> 4; matrix products, arithmetic and copies ran while one was open for 3% -> 0% of each run, Pallas kernels for 0% -> 1%
where the time goes in v2:
time: 173 us
  waiting for transfers between devices  57 us (33%)
  Pallas kernels  56.4 us (33%)
  starting transfers between devices  41.1 us (24%)
  blocking collectives  16.7 us (10%)
    all_to_all x1, waiting for transfers between devices, shards(): lax.all_to_all(outgoing, 'tm', split_axis=0, concat_axis=0, tiled=True)  50.1 us
    pallas_call x1, Pallas kernels, send_blocks(): pl.pallas_call(send_kernel, out_shape=jax.ShapeDtypeStruct((owners, PAIR_...  35.8 us
    all_to_all x1, starting transfers between devices, shards(): lax.all_to_all(outgoing, 'tm', split_axis=0, concat_axis=0, tiled=True)  34.3 us
    all_to_all x1, blocking collectives, shards(): lax.all_to_all(stats, 'tile', split_axis=0, concat_axis=0, tiled=True)  16.7 us
    pallas_call x1, Pallas kernels, first_layer(): pl.pallas_call(hidden_kernel, out_shape=(jax.ShapeDtypeStruct((length, PO...  8.53 us
    pallas_call x1, Pallas kernels, second_layer(): pl.pallas_call(output_kernel, out_shape=jax.ShapeDtypeStruct(frames.shape...  8.06 us
    ppermute x1, waiting for transfers between devices, swap_edges(): lax.ppermute(left, 'tile', [(i + 1, i) for i in range(count - 1)])  4.33 us
  transfers between devices with their start and end apart: 4, of which 4 were waited for; matrix products, arithmetic and copies ran while one was open for 0% of the time, Pallas kernels for 1%

profile of v2, /device:TPU:96, one launch (start us, length us, event | category | flops | bytes accessed | tf_op | source)
XLA Modules:
  0.0 173.0 jit_solution(6926612949393108732)
XLA Ops:
  0.0 35.8 %send_blocks.1 = bf16[16,528,128]{2,1,0:T(8,128)(2,1)} custom-call(s32[32]{0:T(128)} %slot_ref.1, bf16[32,256,128]{2,1,0:T(8,128)(2,1)} %bitcast.24), custom_call_target="tpu_custom_call" | custom-call | tf_op jit(solution)/shard_map/send_blocks/pallas_call | solution.py:95
  35.8 34.3 %all-to-all-start = ((bf16[16,528,128]{2,1,0:T(8,128)(2,1)}), bf16[16,528,128]{2,1,0:T(8,128)(2,1)S(1)}, u32[]{:S(2)}, u32[]{:S(2)}) async-start(bf16[16,528,128]{2,1,0:T(8,128)(2,1)} %send_blocks.1), calls=%async_computation | async-start | bytes 4325376 | tf_op jit(solution)/shard_map/all_to_all | solution.py:522
  70.2 0.0 copy-start.5
  70.2 50.1 %all-to-all-done.arrived_ref = bf16[16,528,128]{2,1,0:T(8,128)(2,1)S(1)} async-done(((bf16[16,528,128]{2,1,0:T(8,128)(2,1)}), bf16[16,528,128]{2,1,0:T(8,128)(2,1)S(1)}, u32[]{:S(2)}, u32[]{:S(2)}) %all-to-all-start) | async-done | bytes 2162720 | tf_op jit(solution)/shard_map/all_to_all | solution.py:522
  120.3 1.4 block_order.1
  121.7 2.0 %collective-permute-start = (bf16[512,128]{1,0:T(8,128)(2,1)S(1)}, bf16[512,128]{1,0:T(8,128)(2,1)S(1)}, u32[]{:S(2)}, u32[]{:S(2)}) collective-permute-start(bf16[512,128]{1,0:T(8,128)(2,1)S(1)} %get-tuple-element.16), channel_id=1, source_target_pairs={{0,16},{16,32},{32,48},{48,64},{64,80},{80,96},{96,112},{112,128},... | collective-permute-start | bytes 393224 | tf_op jit(solution)/shard_map/ppermute | solution.py:530
  123.7 0.0 copy-done.5
  123.7 0.2 reduce-window.8
  123.9 0.1 convert_reduce_fusion.2
  124.0 0.0 copy-start.2
  124.0 0.0 copy-start.3
  124.0 0.0 copy-start.4
  124.0 2.6 %place_blocks.1 = (bf16[4096,128]{1,0:T(8,128)(2,1)S(1)}, bf16[576,128]{1,0:T(8,128)(2,1)S(1)}, bf16[576,128]{1,0:T(8,128)(2,1)S(1)}) custom-call(s32[1,128]{1,0:T(1,128)S(1)} %get-tuple-element.17.order_ref, bf16[16,528,128]{2,1,0:T(8,128)(2,1)S(1)} %all-to-all-done.arrived_ref), custom_call_target="tpu_custom_call" | custom-call | tf_op jit(solution)/shard_map/place_blocks/pallas_call | solution.py:203
  126.6 0.0 copy-start
  126.6 1.4 collective-permute-done.lead_ref
  127.9 0.1 lead_edges.1
  128.0 3.4 %collective-permute-start.1 = (bf16[576,128]{1,0:T(8,128)(2,1)S(1)}, bf16[576,128]{1,0:T(8,128)(2,1)S(1)}, u32[]{:S(2)}, u32[]{:S(2)}) collective-permute-start(bf16[576,128]{1,0:T(8,128)(2,1)S(1)} %get-tuple-element.21), channel_id=1, source_target_pairs={{0,1},{1,2},{2,3},{3,4},{4,5},{5,6},{6,7},{7,8},{8,9},{9,10},{10,1... | collective-permute-start | bytes 442376 | tf_op jit(solution)/shard_map/ppermute | solution.py:507
  131.4 1.3 collective-permute-start.2
  132.7 0.1 stack.11
  132.9 1.2 collective-permute-done.1.left_ref
  134.1 4.3 %collective-permute-done.2.right_ref = bf16[576,128]{1,0:T(8,128)(2,1)S(1)} collective-permute-done((bf16[576,128]{1,0:T(8,128)(2,1)S(1)}, bf16[576,128]{1,0:T(8,128)(2,1)S(1)}, u32[]{:S(2)}, u32[]{:S(2)}) %collective-permute-start.2) | collective-permute-done | bytes 147488 | tf_op jit(solution)/shard_map/ppermute | solution.py:508
  138.5 0.0 copy-start.1
  138.5 1.2 copy-done.1
  139.6 8.5 %first_layer.1 = (f32[36,128,128]{2,1,0:T(8,128)S(1)}, f32[36,8,128]{2,1,0:T(8,128)S(1)}, f32[36,8,128]{2,1,0:T(8,128)S(1)}, f32[16,24,128]{2,1,0:T(8,128)S(1)}) custom-call(f32[3,36]{1,0:T(4,128)S(1)} %add_convert_fusion.valid_ref, bf16[512,128]{1,0:T(8,128)(2,1)S(1)} %collective-permute-done.lead_ref, bf16[4096,128]{1,0:T(8,128)(2,1)S(1)} %get-tuple-element.18.frames_ref, ...), custom_call_target="tpu_custom_call" | custom-call | tf_op jit(solution)/shard_map/first_layer/pallas_call | solution.py:389
  148.2 16.7 %all_to_all.10.stats_ref = f32[16,24,128]{2,1,0:T(8,128)S(1)} all-to-all(f32[16,24,128]{2,1,0:T(8,128)S(1)} %get-tuple-element.26), channel_id=1, replica_groups=mesh['tm'=16,'tile'=16] {'tile'}, dimensions={0} | all-to-all | bytes 393216 | tf_op jit(solution)/shard_map/all_to_all | solution.py:537
  164.9 0.0 copy-done.2
  164.9 0.0 copy-done.3
  164.9 0.0 copy-done.4
  164.9 0.0 copy-done
  164.9 8.1 %second_layer.1 = bf16[4096,128]{1,0:T(8,128)(2,1)} custom-call(f32[3,36]{1,0:T(4,128)S(1)} %add_convert_fusion.valid_ref, f32[36,128,128]{2,1,0:T(8,128)S(1)} %get-tuple-element.23.hidden_ref, f32[36,8,128]{2,1,0:T(8,128)S(1)} %get-tuple-element.24.edge_l_ref, f32[36,8,128]{2,1,0:T(8,128)S(1)} %get-tuple-element.25.edge_r_ref, ...), custom_call_target="tpu_custom_call" | custom-call | tf_op jit(solution)/shard_map/second_layer/pallas_call | solution.py:477
  (4 shorter events, 0.0 us)
Async XLA Ops:
  35.8 84.5 %all-to-all-start = ((bf16[16,528,128]{2,1,0:T(8,128)(2,1)}), bf16[16,528,128]{2,1,0:T(8,128)(2,1)S(1)}, u32[]{:S(2)}, u32[]{:S(2)}) async-start(bf16[16,528,128]{2,1,0:T(8,128)(2,1)} %send_blocks.1), calls=%async_computation | async-start | bytes 4325376 | tf_op jit(solution)/shard_map/all_to_all | solution.py:522
  70.2 53.5 %copy-start.5 = (s32[8]{0:T(128)S(1)}, s32[8]{0:T(128)}, u32[]{:S(2)}) copy-start(s32[8]{0:T(128)} %param.10) | copy-start | bytes 100
  121.7 6.3 %collective-permute-start = (bf16[512,128]{1,0:T(8,128)(2,1)S(1)}, bf16[512,128]{1,0:T(8,128)(2,1)S(1)}, u32[]{:S(2)}, u32[]{:S(2)}) collective-permute-start(bf16[512,128]{1,0:T(8,128)(2,1)S(1)} %get-tuple-element.16), channel_id=1, source_target_pairs={{0,16},{16,32},{32,48},{48,64},{64,80},{80,96},{96,112},{112,128},... | collective-permute-start | bytes 393224 | tf_op jit(solution)/shard_map/ppermute | solution.py:530
  124.0 40.9 %copy-start.2 = (f32[128]{0:T(128)S(1)}, f32[128]{0:T(128)}, u32[]{:S(2)}) copy-start(f32[128]{0:T(128)} %param.12) | copy-start | bytes 1540
  124.0 40.9 %copy-start.3 = (f32[128]{0:T(128)S(1)}, f32[128]{0:T(128)}, u32[]{:S(2)}) copy-start(f32[128]{0:T(128)} %param.13) | copy-start | bytes 1540
  124.0 40.9 %copy-start.4 = (f32[128]{0:T(128)S(1)}, f32[128]{0:T(128)}, u32[]{:S(2)}) copy-start(f32[128]{0:T(128)} %param.15) | copy-start | bytes 1540
  126.6 38.3 %copy-start = (bf16[3,3,3,128,128]{4,3,2,1,0:T(8,128)(2,1)S(1)}, bf16[3,3,3,128,128]{4,3,2,1,0:T(8,128)(2,1)}, u32[]{:S(2)}) copy-start(bf16[3,3,3,128,128]{4,3,2,1,0:T(8,128)(2,1)} %weight_ref.3) | copy-start | bytes 2654212
  128.0 6.1 %collective-permute-start.1 = (bf16[576,128]{1,0:T(8,128)(2,1)S(1)}, bf16[576,128]{1,0:T(8,128)(2,1)S(1)}, u32[]{:S(2)}, u32[]{:S(2)}) collective-permute-start(bf16[576,128]{1,0:T(8,128)(2,1)S(1)} %get-tuple-element.21), channel_id=1, source_target_pairs={{0,1},{1,2},{2,3},{3,4},{4,5},{5,6},{6,7},{7,8},{8,9},{9,10},{10,1... | collective-permute-start | bytes 442376 | tf_op jit(solution)/shard_map/ppermute | solution.py:507
  131.4 7.0 %collective-permute-start.2 = (bf16[576,128]{1,0:T(8,128)(2,1)S(1)}, bf16[576,128]{1,0:T(8,128)(2,1)S(1)}, u32[]{:S(2)}, u32[]{:S(2)}) collective-permute-start(bf16[576,128]{1,0:T(8,128)(2,1)S(1)} %get-tuple-element.22), channel_id=1, source_target_pairs={{1,0},{2,1},{3,2},{4,3},{5,4},{6,5},{7,6},{8,7},{9,8},{10,9},{11,1... | collective-permute-start | bytes 442376 | tf_op jit(solution)/shard_map/ppermute | solution.py:508
  138.5 1.2 copy-start.1

commit v3 on v2

--- a/solution.py
+++ b/solution.py
@@ -48,21 +48,30 @@
     return pl.BlockSpec(memory_space=pltpu.HBM)
 
 
-def send_kernel(slot_ref, video_ref, out_ref, count, info, info_out, sems):
+def send_kernel(slot_ref, video_ref, out_ref, count, held, info, info_out, sems_in, sems_out):
     slots = slot_ref.shape[0]
     owners = count.shape[0]
+    block_rows = PAIR_ROWS // CAP
+
+    def load(slot):
+        return pltpu.make_async_copy(video_ref.at[slot], held.at[slot], sems_in.at[slot])
+
+    def store(slot, owner, rank):
+        rows = pl.ds(pl.multiple_of(rank * block_rows, block_rows), block_rows)
+        return pltpu.make_async_copy(
+            held.at[slot], out_ref.at[owner, rows], sems_out.at[slot]
+        )
+
+    for slot in range(slots):
+
+        @pl.when(slot_ref[slot] >= 0)
+        def _():
+            load(slot).start()
+
     for owner in range(owners):
         count[owner] = 0
     info[...] = jnp.zeros_like(info)
     lane = lax.broadcasted_iota(jnp.int32, info.shape[1:], 1)
-
-    def copy(slot, owner, rank):
-        block_rows = PAIR_ROWS // CAP
-        rows = pl.ds(pl.multiple_of(rank * block_rows, block_rows), block_rows)
-        return pltpu.make_async_copy(
-            video_ref.at[slot], out_ref.at[owner, rows], sems.at[slot]
-        )
-
     for slot in range(slots):
         block = slot_ref[slot]
 
@@ -71,21 +80,22 @@
             owner = block >> 4
             rank = count[owner]
             count[owner] = rank + 1
-            copy(slot, owner, rank).start()
             mark = jnp.where(lane == (block & (OWN - 1)), (rank + 1).astype(f32), 0.0)
             info[owner] = info[owner] + mark
+            load(slot).wait()
+            store(slot, owner, rank).start()
 
     for owner in range(owners):
         info_out[owner] = jnp.concatenate([info[owner]] * 2, axis=0).astype(bf16)
     notes = pltpu.make_async_copy(
-        info_out, out_ref.at[:, pl.ds(PAIR_ROWS, INFO_ROWS)], sems.at[slots]
+        info_out, out_ref.at[:, pl.ds(PAIR_ROWS, INFO_ROWS)], sems_out.at[slots]
     )
     notes.start()
     for slot in range(slots):
 
         @pl.when(slot_ref[slot] >= 0)
         def _():
-            copy(slot, 0, 0).wait()
+            store(slot, 0, 0).wait()
 
     notes.wait()
 
@@ -99,8 +109,10 @@
         out_specs=hbm_only(),
         scratch_shapes=[
             pltpu.SMEM((owners,), jnp.int32),
+            pltpu.VMEM((slots, PAIR_ROWS // CAP, C), bf16),
             pltpu.VMEM((owners, 8, C), f32),
             pltpu.VMEM((owners, INFO_ROWS, C), bf16),
+            pltpu.SemaphoreType.DMA((slots,)),
             pltpu.SemaphoreType.DMA((slots + 1,)),
         ],
         compiler_params=params(62),
@@ -108,7 +120,8 @@
     )(slot_block, video.reshape(slots, PAIR_ROWS // CAP, C))
 
 
-def order_kernel(arrived_ref, order_ref, tail_ref, notes, picks, sems):
+def order_kernel(arrived_ref, *refs):
+    order_ref, tail_ref, notes, picks, sems = refs[-5:]
     owners = arrived_ref.shape[0]
     note = pltpu.make_async_copy(
         arrived_ref.at[:, pl.ds(PAIR_ROWS, INFO_ROWS)], notes, sems.at[0]
@@ -143,14 +156,14 @@
     return arrived_ref.at[arrival >> 1, rows]
 
 
-def block_order(arrived):
+def block_order(arrived, ready):
     return pl.pallas_call(
         order_kernel,
         out_shape=(
             jax.ShapeDtypeStruct((1, C), jnp.int32),
             jax.ShapeDtypeStruct((LEAD * POS, C), bf16),
         ),
-        in_specs=[hbm_only()],
+        in_specs=[hbm_only()] + [hbm()] * len(ready),
         out_specs=(smem(), vmem()),
         scratch_shapes=[
             pltpu.VMEM((arrived.shape[0], INFO_ROWS, C), bf16),
@@ -159,7 +172,7 @@
         ],
         compiler_params=params(),
         name="block_order",
-    )(arrived)
+    )(arrived, *ready)
 
 
 def edge_rows(wide, column):
@@ -234,48 +247,46 @@
     )(lead, left, right)
 
 
-def join_weight(weight_ref, joined):
-    for j in range(3):
-        for i in range(3):
-            for lag in range(3):
-                at = (3 * j + i) * C
-                joined[at : at + C, lag * C : (lag + 1) * C] = weight_ref[2 - lag, i, j]
-
-
-def conv_chunk(valid_ref, start, count, wide, taps, joined, carry, sides):
-    rows = count * ROWS
-    for at in range(rows):
+def join_kernel(first_ref, second_ref, first_out, second_out, token_out):
+    token_out[...] = jnp.zeros_like(token_out)
+    for weight_ref, joined in ((first_ref, first_out), (second_ref, second_out)):
+        for j in range(3):
+            for i in range(3):
+                for lag in range(3):
+                    at = (3 * j + i) * C
+                    joined[at : at + C, lag * C : (lag + 1) * C] = weight_ref[2 - lag, i, j]
+
+
+def join_weights(first, second):
+    joined = jax.ShapeDtypeStruct((9 * C, 3 * C), bf16)
+    return pl.pallas_call(
+        join_kernel,
+        out_shape=(joined, joined, jax.ShapeDtypeStruct((8, C), f32)),
+        in_specs=[vmem()] * 2,
+        out_specs=(vmem(),) * 3,
+        compiler_params=params(),
+        name="join_weights",
+    )(first, second)
+
+
+def conv_chunk(valid_ref, start, count, wide, taps, joined, carry):
+    for at in range(count * ROWS):
         q, r = at // ROWS, at % ROWS + 1
         base = at * PITCH + 8
         for j in range(3):
             taps[j, q, r] = wide[base + j - 1 : base + j - 1 + COLS].astype(bf16)
-    pieces = [
-        taps[j, 0:count, i : i + ROWS].reshape(count * POS, C) for j in range(3) for i in range(3)
-    ]
-    if sides:
-        row = lax.broadcasted_iota(jnp.int32, (2 * rows, C), 0) % ROWS
-        for j in range(3):
-            column = jnp.concatenate(
-                [wide[pl.ds(at + j, rows, stride=PITCH), :] for at in (6, 7 + COLS)], axis=0
-            )
-            above = jnp.where(row == 0, 0.0, pltpu.roll(column, 1, 0))
-            below = jnp.where(row == ROWS - 1, 0.0, pltpu.roll(column, 2 * rows - 1, 0))
-            for i, piece in enumerate((above, column, below)):
-                at = 3 * j + i
-                pieces[at] = jnp.concatenate([pieces[at], piece.astype(bf16)], axis=0)
-    product = jnp.dot(
-        jnp.concatenate(pieces, axis=1), joined[...], preferred_element_type=f32
+    windows = jnp.concatenate(
+        [
+            taps[j, 0:count, i : i + ROWS].reshape(count * POS, C)
+            for j in range(3)
+            for i in range(3)
+        ],
+        axis=1,
     )
+    product = jnp.dot(windows, joined[...], preferred_element_type=f32)
 
     def part(q, lag):
-        lanes = slice(lag * C, (lag + 1) * C)
-        own = product[q * POS : (q + 1) * POS, lanes]
-        if not sides:
-            return own
-        left = count * POS + q * ROWS
-        right = left + rows
-        edges = [product[at : at + ROWS, lanes] for at in (left, right)]
-        return jnp.concatenate([own] + edges, axis=0)
+        return product[q * POS : (q + 1) * POS, lag * C : (lag + 1) * C]
 
     totals = []
     for q in range(count):
@@ -290,17 +301,15 @@
     return totals
 
 
-def conv_scratch(sides):
+def conv_scratch():
     return [
         pltpu.VMEM((UNROLL, CHUNK * ROWS * PITCH + 8, C), f32),
         pltpu.VMEM((UNROLL, 3, CHUNK, ROWS + 2, COLS, C), bf16),
-        pltpu.VMEM((9 * C, 3 * C), bf16),
-        pltpu.VMEM((3, POS + (2 * ROWS if sides else 0), C), f32),
+        pltpu.VMEM((3, POS, C), f32),
     ]
 
 
-def conv_setup(weight_ref, taps, joined, carry):
-    join_weight(weight_ref, joined)
+def conv_setup(taps, carry):
     carry[...] = jnp.zeros_like(carry)
     for u in range(UNROLL):
         for j in range(3):
@@ -334,73 +343,127 @@
     return jnp.dot(a, b, precision=lax.Precision.HIGHEST, preferred_element_type=f32)
 
 
+INNER = ROWS * (COLS - 2)
+
+
 def hidden_kernel(
-    valid_ref, lead_ref, frames_ref, left_ref, right_ref, weight_ref,
-    hidden_ref, edge_l_ref, edge_r_ref, stats_ref,
-    wide, taps, joined, carry, means, spreads,
+    valid_ref, lead_ref, frames_ref, joined, hidden_ref, means_ref, spreads_ref,
+    wide, taps, carry,
 ):
-    conv_setup(weight_ref, taps, joined, carry)
-    means[...] = jnp.zeros_like(means)
-    spreads[...] = jnp.zeros_like(spreads)
+    conv_setup(taps, carry)
+    none = jnp.zeros((CHUNK * ROWS, C), f32)
+    for u in range(UNROLL):
+        put_column(wide.at[u], 7, none)
+        put_column(wide.at[u], 8 + COLS, none)
+    means_ref[...] = jnp.zeros_like(means_ref)
+    spreads_ref[...] = jnp.zeros_like(spreads_ref)
+    column = lax.broadcasted_iota(jnp.int32, (POS, C), 0) % COLS
+    inner = (column > 0) & (column < COLS - 1)
 
     def chunk_step(u, start, count, source, at):
         for row in range(count * ROWS):
             here = source[pl.ds(pl.multiple_of(at + row * COLS, COLS), COLS)]
             wide[u, row * PITCH + 8 : row * PITCH + 8 + COLS] = here.astype(f32)
-        for c in range(2):
-            edge_at = pl.multiple_of(c * EDGE_ROWS + start * ROWS, 2 * ROWS)
-            edge_at = pl.ds(edge_at, count * ROWS)
-            put_column(wide.at[u], 6 + c, left_ref[edge_at].astype(f32))
-            put_column(wide.at[u], 8 + COLS + c, right_ref[edge_at].astype(f32))
-        totals = conv_chunk(
-            valid_ref, start, count, wide.at[u], taps.at[u], joined, carry, True
-        )
+        totals = conv_chunk(valid_ref, start, count, wide.at[u], taps.at[u], joined, carry)
         for q in range(count):
             frame = start + q
-            own = totals[q][:POS]
+            own = totals[q]
             hidden_ref[frame] = own
-            edge_l_ref[frame] = totals[q][POS : POS + ROWS]
-            edge_r_ref[frame] = totals[q][POS + ROWS :]
-            mean = jnp.sum(own, axis=0, keepdims=True) / POS
-            centred = own - mean
-            means[pl.ds(frame, 1), :] = mean
-            spreads[pl.ds(frame, 1), :] = jnp.sum(centred * centred, axis=0, keepdims=True)
-
-    for start in range(0, LEAD, CHUNK):
-        chunk_step(0, start, min(CHUNK, LEAD), lead_ref, start * POS)
+            mean = jnp.sum(jnp.where(inner, own, 0.0), axis=0, keepdims=True) / INNER
+            centred = jnp.where(inner, own - mean, 0.0)
+            means_ref[pl.ds(frame, 1), :] = mean
+            spreads_ref[pl.ds(frame, 1), :] = jnp.sum(centred * centred, axis=0, keepdims=True)
+
+    chunk_step(0, 0, LEAD, lead_ref, 0)
     over_chunks(lambda u, at: chunk_step(u, LEAD + at, CHUNK, frames_ref, at * POS))
 
-    mean = group_total(means[...]) / 4
-    off = means[...] - mean
-    spread = group_total(spreads[...] + POS * off * off)
+
+def first_layer(valid, lead, frames, joined):
+    length = LEAD + 2 * OWN
+    sums = jax.ShapeDtypeStruct((2 * HALF, C), f32)
+    return pl.pallas_call(
+        hidden_kernel,
+        out_shape=(jax.ShapeDtypeStruct((length, POS, C), f32), sums, sums),
+        in_specs=[smem()] + [vmem()] * 3,
+        out_specs=(vmem(),) * 3,
+        scratch_shapes=conv_scratch(),
+        compiler_params=params(),
+        cost_estimate=pl.CostEstimate(
+            flops=2 * length * POS * 27 * C * C, bytes_accessed=4 * MIB, transcendentals=0
+        ),
+        name="first_layer",
+    )(valid, lead, frames, joined)
+
+
+def edge_kernel(
+    valid_ref, own_l, own_r, halo_l, halo_r, joined, means_ref, spreads_ref,
+    edges_ref, stats_ref, means, spreads,
+):
+    row = lax.broadcasted_iota(jnp.int32, (EDGE_ROWS, C), 0) % ROWS
+    length = EDGE_ROWS // ROWS
+
+    def rows_of(ref, c):
+        column = ref[c * EDGE_ROWS : (c + 1) * EDGE_ROWS].astype(f32)
+        above = jnp.where(row == 0, 0.0, pltpu.roll(column, 1, 0))
+        below = jnp.where(row == ROWS - 1, 0.0, pltpu.roll(column, EDGE_ROWS - 1, 0))
+        return [piece.astype(bf16) for piece in (above, column, below)]
+
+    for side, refs in enumerate(((halo_l, own_l), (own_r, halo_r))):
+        columns = [rows_of(ref, c) for ref in refs for c in range(2)]
+        for k in range(2):
+            windows = jnp.concatenate(sum(columns[k : k + 3], []), axis=1)
+            product = jnp.dot(windows, joined[...], preferred_element_type=f32)
+
+            def part(frame, lag):
+                rows = slice(frame * ROWS, (frame + 1) * ROWS)
+                return product[rows, lag * C : (lag + 1) * C]
+
+            at = 2 * side + k
+            edges_ref[at, 0 : 2 * ROWS] = jnp.zeros((2 * ROWS, C), f32)
+            for frame in range(2, length):
+                edges_ref[at, frame * ROWS : (frame + 1) * ROWS] = (
+                    part(frame, 0)
+                    + valid_ref[0, frame] * part(frame - 1, 1)
+                    + valid_ref[1, frame] * part(frame - 2, 2)
+                )
+
+    means[...] = jnp.zeros_like(means)
+    spreads[...] = jnp.zeros_like(spreads)
+    outer = [edges_ref[at].reshape(length, ROWS, C) for at in (1, 2)]
+    mean = jnp.sum(outer[0] + outer[1], axis=1, keepdims=True) / (2 * ROWS)
+    apart = [(entries - mean) * (entries - mean) for entries in outer]
+    means[0:length] = mean.reshape(length, C)
+    spreads[0:length] = jnp.sum(apart[0] + apart[1], axis=1)
+    off = means[...] - means_ref[...]
+    local = means_ref[...] + off * (2 * ROWS / POS)
+    spread = spreads_ref[...] + spreads[...] + off * off * (INNER * 2 * ROWS / POS)
+
+    mean = group_total(local) / 4
+    off = local - mean
+    spread = group_total(spread + POS * off * off)
     channel = lax.broadcasted_iota(jnp.int32, (C, C), 0)
     lane = lax.broadcasted_iota(jnp.int32, (C, C), 1)
     packed = jnp.zeros((HALF, C), f32)
-    for q, part in enumerate((mean[:HALF], spread[:HALF], mean[HALF:], spread[HALF:])):
+    for q, piece in enumerate((mean[:HALF], spread[:HALF], mean[HALF:], spread[HALF:])):
         picks = (channel == 4 * (lane - GROUPS * q)) & (lane // GROUPS == q)
-        packed = packed + precise_dot(part, picks.astype(f32))
+        packed = packed + precise_dot(piece, picks.astype(f32))
     for peer in range(stats_ref.shape[0]):
         stats_ref[peer] = packed
 
 
-def first_layer(valid, lead, frames, left, right, weight, tiles):
-    length = LEAD + 2 * OWN
-    edge = jax.ShapeDtypeStruct((length, ROWS, C), f32)
-    return pl.pallas_call(
-        hidden_kernel,
+def finish_hidden(valid, own_l, own_r, halo_l, halo_r, joined, means, spreads, tiles):
+    return pl.pallas_call(
+        edge_kernel,
         out_shape=(
-            jax.ShapeDtypeStruct((length, POS, C), f32),
-            edge,
-            edge,
+            jax.ShapeDtypeStruct((4, EDGE_ROWS, C), f32),
             jax.ShapeDtypeStruct((tiles, HALF, C), f32),
         ),
-        in_specs=[smem()] + [vmem()] * 5,
-        out_specs=(vmem(),) * 4,
-        scratch_shapes=conv_scratch(True)
-        + [pltpu.VMEM((2 * HALF, C), f32), pltpu.VMEM((2 * HALF, C), f32)],
+        in_specs=[smem()] + [vmem()] * 7,
+        out_specs=(vmem(),) * 2,
+        scratch_shapes=[pltpu.VMEM((2 * HALF, C), f32), pltpu.VMEM((2 * HALF, C), f32)],
         compiler_params=params(),
-        name="first_layer",
-    )(valid, lead, frames, left, right, weight)
+        name="finish_hidden",
+    )(valid, own_l, own_r, halo_l, halo_r, joined, means, spreads)
 
 
 def combine_stats(stats_ref, gain_ref, means, scales):
@@ -434,11 +497,11 @@
 
 
 def output_kernel(
-    valid_ref, hidden_ref, edge_l_ref, edge_r_ref, stats_ref, frames_ref,
-    gain_ref, norm_bias_ref, weight_ref, bias_ref, out_ref,
-    wide, taps, joined, carry, means, scales, halo,
+    valid_ref, hidden_ref, edges_ref, stats_ref, frames_ref,
+    gain_ref, norm_bias_ref, joined, bias_ref, out_ref,
+    wide, taps, carry, means, scales, halo,
 ):
-    conv_setup(weight_ref, taps, joined, carry)
+    conv_setup(taps, carry)
     combine_stats(stats_ref, gain_ref, means, scales)
     has_left = valid_ref[2, 0]
     has_right = valid_ref[2, 1]
@@ -454,13 +517,12 @@
             for r in range(ROWS):
                 at = (q * ROWS + r) * PITCH + 8
                 wide[u, at : at + COLS] = active[r * COLS : (r + 1) * COLS]
-            halo[u, 0, q * ROWS : (q + 1) * ROWS] = norm(edge_l_ref[frame], frame) * has_left
-            halo[u, 1, q * ROWS : (q + 1) * ROWS] = norm(edge_r_ref[frame], frame) * has_right
-        put_column(wide.at[u], 7, halo[u, 0, 0 : count * ROWS])
-        put_column(wide.at[u], 8 + COLS, halo[u, 1, 0 : count * ROWS])
-        return conv_chunk(
-            valid_ref, start, count, wide.at[u], taps.at[u], joined, carry, False
-        )
+            at = pl.ds(pl.multiple_of(frame * ROWS, ROWS), ROWS)
+            for k, inside in enumerate((has_left, 1.0, 1.0, has_right)):
+                halo[u, k, q * ROWS : (q + 1) * ROWS] = norm(edges_ref[k, at], frame) * inside
+        for k, column in enumerate((7, 8, 7 + COLS, 8 + COLS)):
+            put_column(wide.at[u], column, halo[u, k, 0 : count * ROWS])
+        return conv_chunk(valid_ref, start, count, wide.at[u], taps.at[u], joined, carry)
 
     def own_chunk(u, start):
         totals = chunk_step(u, LEAD + start, CHUNK)
@@ -473,21 +535,21 @@
     over_chunks(own_chunk)
 
 
-def second_layer(valid, hidden, edge_l, edge_r, stats, frames, gain, norm_bias, weight, bias):
+def second_layer(valid, hidden, edges, stats, frames, gain, norm_bias, weight, bias):
     return pl.pallas_call(
         output_kernel,
         out_shape=jax.ShapeDtypeStruct(frames.shape, bf16),
-        in_specs=[smem()] + [vmem()] * 9,
+        in_specs=[smem()] + [vmem()] * 8,
         out_specs=vmem(),
-        scratch_shapes=conv_scratch(False)
+        scratch_shapes=conv_scratch()
         + [
             pltpu.VMEM((2 * HALF, C), f32),
             pltpu.VMEM((2 * HALF, C), f32),
-            pltpu.VMEM((UNROLL, 2, CHUNK * ROWS, C), f32),
+            pltpu.VMEM((UNROLL, 4, CHUNK * ROWS, C), f32),
         ],
         compiler_params=params(),
         name="second_layer",
-    )(valid, hidden, edge_l, edge_r, stats, frames, gain, norm_bias, weight, bias)
+    )(valid, hidden, edges, stats, frames, gain, norm_bias, weight, bias)
 
 
 def lag_masks(clip_frames, first_frame, length):
@@ -526,18 +588,20 @@
         [lag_masks(clip_frames, position * length - LEAD, length + LEAD), inside[None]]
     ).astype(f32)
 
-    order, tail = block_order(arrived)
+    weight1, weight2, token = join_weights(conv1_weight, conv2_weight)
+    order, tail = block_order(arrived, (valid, token))
     lead = lax.ppermute(tail, "tm", [(i, i + 1) for i in range(owners - 1)])
     frames, left, right = place_blocks(order, arrived)
     left, right = lead_edges(lead, left, right)
     from_left, from_right = swap_edges(left, right)
-    hidden, edge_l, edge_r, stats = first_layer(
-        valid, lead, frames, from_left, from_right, conv1_weight, tiles
+    hidden, means, spreads = first_layer(valid, lead, frames, weight1)
+    edges, stats = finish_hidden(
+        valid, left, right, from_left, from_right, weight1, means, spreads, tiles
     )
     stats = lax.all_to_all(stats, "tile", split_axis=0, concat_axis=0, tiled=True)
     encoded = second_layer(
-        valid, hidden, edge_l, edge_r, stats, frames, norm_gain[None], norm_bias[None],
-        conv2_weight, conv2_bias[None],
+        valid, hidden, edges, stats, frames, norm_gain[None], norm_bias[None],
+        weight2, conv2_bias[None],
     )
     return encoded.reshape((length,) + video.shape[2:])
 

time: 173 us -> 110 us (0.64)
  Pallas kernels: 56.4 us -> 25.8 us
  starting transfers between devices: 41.1 us -> 15.7 us
  waiting for transfers between devices: 57 us -> 48 us
  local copies, waits for them, and re-layouts: 1.33 us -> 3.18 us
    pallas_call x1, Pallas kernels: 35.8 us -> 3.43 us  [send_blocks(): pl.pallas_call(send_kernel, out_shape=jax.ShapeDtypeStruct((owners, PAIR_...]
    all_to_all x1, starting transfers between devices: 34.3 us -> 7.82 us  [shards(): lax.all_to_all(outgoing, 'tm', split_axis=0, concat_axis=0, tiled=True)]
    ppermute x1, waiting for transfers between devices: 4.33 us -> 0.01 us  [swap_edges(): lax.ppermute(left, 'tile', [(i + 1, i) for i in range(count - 1)])]
    all_to_all x1, waiting for transfers between devices: 50.1 us -> 46.3 us  [shards(): lax.all_to_all(outgoing, 'tm', split_axis=0, concat_axis=0, tiled=True)]
    pallas_call x0 -> x2, Pallas kernels: none -> 3.21 us  [the longest x1 2.9 us: finish_hidden(): pl.pallas_call(edge_kernel, out_shape=(jax.ShapeDtypeStruct((4, EDGE_ROWS...]
    unnamed x12 -> x20, local copies, waits for them, and re-layouts: 1.19 us -> 3.04 us
  transfers between devices with their start and end apart: 4 -> 4, of which waited for: 4 -> 2; matrix products, arithmetic and copies ran while one was open for 0% -> 0% of each run, Pallas kernels for 1% -> 9%
where the time goes in v3:
time: 110 us
  waiting for transfers between devices  48 us (44%)
  Pallas kernels  25.8 us (23%)
  blocking collectives  17 us (15%)
  starting transfers between devices  15.7 us (14%)
  local copies, waits for them, and re-layouts  3.18 us (3%)
    all_to_all x1, waiting for transfers between devices, shards(): lax.all_to_all(outgoing, 'tm', split_axis=0, concat_axis=0, tiled=True)  46.3 us
    all_to_all x1, blocking collectives, shards(): lax.all_to_all(stats, 'tile', split_axis=0, concat_axis=0, tiled=True)  17 us
    pallas_call x1, Pallas kernels, second_layer(): pl.pallas_call(output_kernel, out_shape=jax.ShapeDtypeStruct(frames.shape...  8.17 us
    all_to_all x1, starting transfers between devices, shards(): lax.all_to_all(outgoing, 'tm', split_axis=0, concat_axis=0, tiled=True)  7.82 us
    pallas_call x1, Pallas kernels, first_layer(): pl.pallas_call(hidden_kernel, out_shape=(jax.ShapeDtypeStruct((length, PO...  7.06 us
    ppermute x1, starting transfers between devices, swap_edges(): lax.ppermute(right, 'tile', [(i, i + 1) for i in range(count - 1)])  4.55 us
    pallas_call x1, Pallas kernels, send_blocks(): pl.pallas_call(send_kernel, out_shape=jax.ShapeDtypeStruct((owners, PAIR_...  3.43 us
    unnamed x20, local copies, waits for them, and re-layouts  3.04 us
  transfers between devices with their start and end apart: 4, of which 2 were waited for; matrix products, arithmetic and copies ran while one was open for 0% of the time, Pallas kernels for 9%

profile of v3, /device:TPU:96, one launch (start us, length us, event | category | flops | bytes accessed | tf_op | source)
XLA Modules:
  0.0 110.2 jit_solution(12883378486489797006)
XLA Ops:
  0.0 3.4 %send_blocks.1 = bf16[16,528,128]{2,1,0:T(8,128)(2,1)} custom-call(s32[32]{0:T(128)} %slot_ref.1, bf16[32,256,128]{2,1,0:T(8,128)(2,1)} %bitcast.24), custom_call_target="tpu_custom_call" | custom-call | tf_op jit(solution)/shard_map/send_blocks/pallas_call | solution.py:105
  3.4 0.0 copy-start.9
  3.4 0.0 copy-start
  3.5 7.8 %all-to-all-start = ((bf16[16,528,128]{2,1,0:T(8,128)(2,1)}), bf16[16,528,128]{2,1,0:T(8,128)(2,1)S(1)}, u32[]{:S(2)}, u32[]{:S(2)}) async-start(bf16[16,528,128]{2,1,0:T(8,128)(2,1)} %send_blocks.1), calls=%async_computation | async-start | bytes 4325376 | tf_op jit(solution)/shard_map/all_to_all | solution.py:584
  11.3 0.0 copy-done.9
  11.3 0.2 reduce-window.8
  11.5 0.0 copy-done
  11.5 0.0 copy-start.1
  11.5 1.2 %copy-done.1 = bf16[3,3,3,128,128]{4,3,2,1,0:T(8,128)(2,1)S(1)} copy-done((bf16[3,3,3,128,128]{4,3,2,1,0:T(8,128)(2,1)S(1)}, bf16[3,3,3,128,128]{4,3,2,1,0:T(8,128)(2,1)}, u32[]{:S(2)}) %copy-start.1) | copy-done | bytes 884760
  12.6 0.3 join_weights.1
  13.0 0.0 copy-start.2
  13.0 0.9 copy-done.2
  13.9 0.0 copy-start.4
  13.9 0.9 copy-done.4
  14.8 0.1 stack.11
  14.9 0.1 convert_reduce_fusion.2
  15.1 46.3 %all-to-all-done.arrived_ref = bf16[16,528,128]{2,1,0:T(8,128)(2,1)S(1)} async-done(((bf16[16,528,128]{2,1,0:T(8,128)(2,1)}), bf16[16,528,128]{2,1,0:T(8,128)(2,1)S(1)}, u32[]{:S(2)}, u32[]{:S(2)}) %all-to-all-start) | async-done | bytes 2162720 | tf_op jit(solution)/shard_map/all_to_all | solution.py:584
  61.4 0.0 copy-start.5
  61.4 1.4 %block_order.1 = (s32[1,128]{1,0:T(1,128)S(1)}, bf16[512,128]{1,0:T(8,128)(2,1)S(1)}) custom-call(bf16[16,528,128]{2,1,0:T(8,128)(2,1)S(1)} %all-to-all-done.arrived_ref, f32[3,36]{1,0:T(4,128)S(1)} %add_convert_fusion.refs_0_.valid_ref, f32[8,128]{1,0:T(8,128)S(1)} %get-tuple-element.20.refs_1_), custom_call_target="tpu_custom_call" | custom-call | tf_op jit(solution)/shard_map/block_order/pallas_call | solution.py:160
  62.8 2.0 %collective-permute-start = (bf16[512,128]{1,0:T(8,128)(2,1)S(1)}, bf16[512,128]{1,0:T(8,128)(2,1)S(1)}, u32[]{:S(2)}, u32[]{:S(2)}) collective-permute-start(bf16[512,128]{1,0:T(8,128)(2,1)S(1)} %get-tuple-element.21), channel_id=1, source_target_pairs={{0,16},{16,32},{32,48},{48,64},{64,80},{80,96},{96,112},{112,128},... | collective-permute-start | bytes 393224 | tf_op jit(solution)/shard_map/ppermute | solution.py:593
  64.8 2.6 %place_blocks.1 = (bf16[4096,128]{1,0:T(8,128)(2,1)S(1)}, bf16[576,128]{1,0:T(8,128)(2,1)S(1)}, bf16[576,128]{1,0:T(8,128)(2,1)S(1)}) custom-call(s32[1,128]{1,0:T(1,128)S(1)} %get-tuple-element.22.order_ref, bf16[16,528,128]{2,1,0:T(8,128)(2,1)S(1)} %all-to-all-done.arrived_ref), custom_call_target="tpu_custom_call" | custom-call | tf_op jit(solution)/shard_map/place_blocks/pallas_call | solution.py:216
  67.4 1.7 %collective-permute-done.lead_ref = bf16[512,128]{1,0:T(8,128)(2,1)S(1)} collective-permute-done((bf16[512,128]{1,0:T(8,128)(2,1)S(1)}, bf16[512,128]{1,0:T(8,128)(2,1)S(1)}, u32[]{:S(2)}, u32[]{:S(2)}) %collective-permute-start) | collective-permute-done | bytes 131104 | tf_op jit(solution)/shard_map/ppermute | solution.py:593
  69.1 0.1 lead_edges.1
  69.1 1.3 %collective-permute-start.2 = (bf16[576,128]{1,0:T(8,128)(2,1)S(1)}, bf16[576,128]{1,0:T(8,128)(2,1)S(1)}, u32[]{:S(2)}, u32[]{:S(2)}) collective-permute-start(bf16[576,128]{1,0:T(8,128)(2,1)S(1)} %get-tuple-element.28.own_l), channel_id=1, source_target_pairs={{1,0},{2,1},{3,2},{4,3},{5,4},{6,5},{7,6},{8,7},{9,8},{10,9},{11,1... | collective-permute-start | bytes 442376 | tf_op jit(solution)/shard_map/ppermute | solution.py:570
  70.4 4.6 %collective-permute-start.1 = (bf16[576,128]{1,0:T(8,128)(2,1)S(1)}, bf16[576,128]{1,0:T(8,128)(2,1)S(1)}, u32[]{:S(2)}, u32[]{:S(2)}) collective-permute-start(bf16[576,128]{1,0:T(8,128)(2,1)S(1)} %get-tuple-element.29.own_r), channel_id=1, source_target_pairs={{0,1},{1,2},{2,3},{3,4},{4,5},{5,6},{6,7},{7,8},{8,9},{9,10},{10,1... | collective-permute-start | bytes 442376 | tf_op jit(solution)/shard_map/ppermute | solution.py:569
  75.0 0.0 copy-done.5
  75.0 0.0 copy-start.6
  75.0 0.0 copy-start.7
  75.0 0.0 copy-start.8
  75.0 7.1 %first_layer.1 = (f32[36,128,128]{2,1,0:T(8,128)S(1)}, f32[48,128]{1,0:T(8,128)S(1)}, f32[48,128]{1,0:T(8,128)S(1)}) custom-call(f32[3,36]{1,0:T(4,128)S(1)} %add_convert_fusion.refs_0_.valid_ref, bf16[512,128]{1,0:T(8,128)(2,1)S(1)} %collective-permute-done.lead_ref, bf16[4096,128]{1,0:T(8,128)(2,1)S(1)} %get-tuple-element.23.frames_ref, ...), custom_call_target="tpu_custom_call" | custom-call | flops 4076863488 | bytes 4194304 | tf_op jit(solution)/shard_map/first_layer/pallas_call | solution.py:384
  82.1 0.0 copy-start.3
  82.1 0.0 collective-permute-done.2.halo_r
  82.1 0.0 collective-permute-done.1.halo_l
  82.1 2.9 %finish_hidden.1 = (f32[4,288,128]{2,1,0:T(8,128)S(1)}, f32[16,24,128]{2,1,0:T(8,128)S(1)}) custom-call(f32[3,36]{1,0:T(4,128)S(1)} %add_convert_fusion.refs_0_.valid_ref, bf16[576,128]{1,0:T(8,128)(2,1)S(1)} %get-tuple-element.28.own_l, bf16[576,128]{1,0:T(8,128)(2,1)S(1)} %get-tuple-element.29.own_r, bf16[576,128]{1,0:T(8,128)(2,1)S(1)} %collective-permute-done.1.halo_l, ...), custom_call_target="tpu_custom_call" | custom-call | tf_op jit(solution)/shard_map/finish_hidden/pallas_call | solution.py:455
  85.0 17.0 %all_to_all.10.stats_ref = f32[16,24,128]{2,1,0:T(8,128)S(1)} all-to-all(f32[16,24,128]{2,1,0:T(8,128)S(1)} %get-tuple-element.33), channel_id=1, replica_groups=mesh['tm'=16,'tile'=16] {'tile'}, dimensions={0} | all-to-all | bytes 393216 | tf_op jit(solution)/shard_map/all_to_all | solution.py:601
  102.0 0.0 copy-done.6
  102.0 0.0 copy-done.7
  102.0 0.0 copy-done.8
  102.1 0.0 copy-done.3
  102.1 8.2 %second_layer.1 = bf16[4096,128]{1,0:T(8,128)(2,1)} custom-call(f32[3,36]{1,0:T(4,128)S(1)} %add_convert_fusion.refs_0_.valid_ref, f32[36,128,128]{2,1,0:T(8,128)S(1)} %get-tuple-element.25.hidden_ref, f32[4,288,128]{2,1,0:T(8,128)S(1)} %get-tuple-element.32.edges_ref, f32[16,24,128]{2,1,0:T(8,128)S(1)} %all_to_all.10.stats_ref, ...), custom_call_target="tpu_custom_call" | custom-call | tf_op jit(solution)/shard_map/second_layer/pallas_call | solution.py:539
  (4 shorter events, 0.0 us)
Async XLA Ops:
  3.4 7.9 %copy-start.9 = (s32[8]{0:T(128)S(1)}, s32[8]{0:T(128)}, u32[]{:S(2)}) copy-start(s32[8]{0:T(128)} %param.10) | copy-start | bytes 100
  3.4 8.0 %copy-start = (bf16[3,3,3,128,128]{4,3,2,1,0:T(8,128)(2,1)S(1)}, bf16[3,3,3,128,128]{4,3,2,1,0:T(8,128)(2,1)}, u32[]{:S(2)}) copy-start(bf16[3,3,3,128,128]{4,3,2,1,0:T(8,128)(2,1)} %first_ref.1) | copy-start | bytes 2654212
  3.5 57.9 %all-to-all-start = ((bf16[16,528,128]{2,1,0:T(8,128)(2,1)}), bf16[16,528,128]{2,1,0:T(8,128)(2,1)S(1)}, u32[]{:S(2)}, u32[]{:S(2)}) async-start(bf16[16,528,128]{2,1,0:T(8,128)(2,1)} %send_blocks.1), calls=%async_computation | async-start | bytes 4325376 | tf_op jit(solution)/shard_map/all_to_all | solution.py:584
  11.5 1.2 %copy-start.1 = (bf16[3,3,3,128,128]{4,3,2,1,0:T(8,128)(2,1)S(1)}, bf16[3,3,3,128,128]{4,3,2,1,0:T(8,128)(2,1)}, u32[]{:S(2)}) copy-start(bf16[3,3,3,128,128]{4,3,2,1,0:T(8,128)(2,1)} %second_ref.1) | copy-start | bytes 2654212
  13.0 0.9 copy-start.2
  13.9 0.9 copy-start.4
  61.4 13.6 %copy-start.5 = (bf16[1152,384]{1,0:T(8,128)(2,1)S(1)}, bf16[1152,384]{1,0:T(8,128)(2,1)}, u32[]{:S(2)}) copy-start(bf16[1152,384]{1,0:T(8,128)(2,1)} %copy-done.4) | copy-start | bytes 2654212
  62.8 6.3 %collective-permute-start = (bf16[512,128]{1,0:T(8,128)(2,1)S(1)}, bf16[512,128]{1,0:T(8,128)(2,1)S(1)}, u32[]{:S(2)}, u32[]{:S(2)}) collective-permute-start(bf16[512,128]{1,0:T(8,128)(2,1)S(1)} %get-tuple-element.21), channel_id=1, source_target_pairs={{0,16},{16,32},{32,48},{48,64},{64,80},{80,96},{96,112},{112,128},... | collective-permute-start | bytes 393224 | tf_op jit(solution)/shard_map/ppermute | solution.py:593
  69.1 13.0 %collective-permute-start.2 = (bf16[576,128]{1,0:T(8,128)(2,1)S(1)}, bf16[576,128]{1,0:T(8,128)(2,1)S(1)}, u32[]{:S(2)}, u32[]{:S(2)}) collective-permute-start(bf16[576,128]{1,0:T(8,128)(2,1)S(1)} %get-tuple-element.28.own_l), channel_id=1, source_target_pairs={{1,0},{2,1},{3,2},{4,3},{5,4},{6,5},{7,6},{8,7},{9,8},{10,9},{11,1... | collective-permute-start | bytes 442376 | tf_op jit(solution)/shard_map/ppermute | solution.py:570
  70.4 11.7 %collective-permute-start.1 = (bf16[576,128]{1,0:T(8,128)(2,1)S(1)}, bf16[576,128]{1,0:T(8,128)(2,1)S(1)}, u32[]{:S(2)}, u32[]{:S(2)}) collective-permute-start(bf16[576,128]{1,0:T(8,128)(2,1)S(1)} %get-tuple-element.29.own_r), channel_id=1, source_target_pairs={{0,1},{1,2},{2,3},{3,4},{4,5},{5,6},{6,7},{7,8},{8,9},{9,10},{10,1... | collective-permute-start | bytes 442376 | tf_op jit(solution)/shard_map/ppermute | solution.py:569
  75.0 27.1 %copy-start.6 = (f32[128]{0:T(128)S(1)}, f32[128]{0:T(128)}, u32[]{:S(2)}) copy-start(f32[128]{0:T(128)} %param.12) | copy-start | bytes 1540
  75.0 27.0 %copy-start.7 = (f32[128]{0:T(128)S(1)}, f32[128]{0:T(128)}, u32[]{:S(2)}) copy-start(f32[128]{0:T(128)} %param.13) | copy-start | bytes 1540
  75.0 27.0 %copy-start.8 = (f32[128]{0:T(128)S(1)}, f32[128]{0:T(128)}, u32[]{:S(2)}) copy-start(f32[128]{0:T(128)} %param.15) | copy-start | bytes 1540
  82.1 20.0 %copy-start.3 = (bf16[1152,384]{1,0:T(8,128)(2,1)S(1)}, bf16[1152,384]{1,0:T(8,128)(2,1)}, u32[]{:S(2)}) copy-start(bf16[1152,384]{1,0:T(8,128)(2,1)} %copy-done.2) | copy-start | bytes 2654212

commit v4 on v3

--- a/solution.py
+++ b/solution.py
@@ -15,11 +15,11 @@
 COLS = 16
 POS = ROWS * COLS
 LEAD = 4
-CHUNK = 4
+CHUNK = 8
 EPSILON = 1e-06
 HALF = 24
 PITCH = 24
-UNROLL = 8
+UNROLL = 4
 PAIR_ROWS = CAP * 2 * POS
 INFO_ROWS = 16
 MIB = 1024 * 1024
@@ -48,13 +48,19 @@
     return pl.BlockSpec(memory_space=pltpu.HBM)
 
 
-def send_kernel(slot_ref, video_ref, out_ref, count, held, info, info_out, sems_in, sems_out):
+LOADS = 4
+
+
+def send_kernel(
+    slot_hbm, video_ref, out_ref, slot_ref, count, target, held, info, info_out, sems_in, sems_out
+):
     slots = slot_ref.shape[0]
-    owners = count.shape[0]
+    owners = out_ref.shape[0]
     block_rows = PAIR_ROWS // CAP
 
-    def load(slot):
-        return pltpu.make_async_copy(video_ref.at[slot], held.at[slot], sems_in.at[slot])
+    def load(part):
+        at = pl.ds(part * (slots // LOADS), slots // LOADS)
+        return pltpu.make_async_copy(video_ref.at[at], held.at[at], sems_in.at[part])
 
     def store(slot, owner, rank):
         rows = pl.ds(pl.multiple_of(rank * block_rows, block_rows), block_rows)
@@ -62,29 +68,23 @@
             held.at[slot], out_ref.at[owner, rows], sems_out.at[slot]
         )
 
-    for slot in range(slots):
-
-        @pl.when(slot_ref[slot] >= 0)
-        def _():
-            load(slot).start()
-
-    for owner in range(owners):
+    to_scalars = pltpu.make_async_copy(slot_hbm, slot_ref, sems_in.at[LOADS])
+    to_scalars.start()
+    for part in range(LOADS):
+        load(part).start()
+    for owner in range(owners + 1):
         count[owner] = 0
     info[...] = jnp.zeros_like(info)
     lane = lax.broadcasted_iota(jnp.int32, info.shape[1:], 1)
+    to_scalars.wait()
     for slot in range(slots):
         block = slot_ref[slot]
-
-        @pl.when(block >= 0)
-        def _():
-            owner = block >> 4
-            rank = count[owner]
-            count[owner] = rank + 1
-            mark = jnp.where(lane == (block & (OWN - 1)), (rank + 1).astype(f32), 0.0)
-            info[owner] = info[owner] + mark
-            load(slot).wait()
-            store(slot, owner, rank).start()
-
+        owner = jnp.where(block >= 0, block >> 4, owners)
+        rank = count[owner]
+        count[owner] = rank + 1
+        target[slot] = rank
+        mark = jnp.where(lane == (block & (OWN - 1)), (rank + 1).astype(f32), 0.0)
+        info[owner] = info[owner] + mark
     for owner in range(owners):
         info_out[owner] = jnp.concatenate([info[owner]] * 2, axis=0).astype(bf16)
     notes = pltpu.make_async_copy(
@@ -92,6 +92,14 @@
     )
     notes.start()
     for slot in range(slots):
+        if slot % (slots // LOADS) == 0:
+            load(slot // (slots // LOADS)).wait()
+
+        @pl.when(slot_ref[slot] >= 0)
+        def _():
+            store(slot, slot_ref[slot] >> 4, target[slot]).start()
+
+    for slot in range(slots):
 
         @pl.when(slot_ref[slot] >= 0)
         def _():
@@ -105,14 +113,16 @@
     return pl.pallas_call(
         send_kernel,
         out_shape=jax.ShapeDtypeStruct((owners, PAIR_ROWS + INFO_ROWS, C), video.dtype),
-        in_specs=[smem(), hbm_only()],
+        in_specs=[hbm_only(), hbm_only()],
         out_specs=hbm_only(),
         scratch_shapes=[
-            pltpu.SMEM((owners,), jnp.int32),
+            pltpu.SMEM((slots,), jnp.int32),
+            pltpu.SMEM((owners + 1,), jnp.int32),
+            pltpu.SMEM((slots,), jnp.int32),
             pltpu.VMEM((slots, PAIR_ROWS // CAP, C), bf16),
-            pltpu.VMEM((owners, 8, C), f32),
+            pltpu.VMEM((owners + 1, 8, C), f32),
             pltpu.VMEM((owners, INFO_ROWS, C), bf16),
-            pltpu.SemaphoreType.DMA((slots,)),
+            pltpu.SemaphoreType.DMA((LOADS + 1,)),
             pltpu.SemaphoreType.DMA((slots + 1,)),
         ],
         compiler_params=params(62),
@@ -121,39 +131,24 @@
 
 
 def order_kernel(arrived_ref, *refs):
-    order_ref, tail_ref, notes, picks, sems = refs[-5:]
-    owners = arrived_ref.shape[0]
-    note = pltpu.make_async_copy(
-        arrived_ref.at[:, pl.ds(PAIR_ROWS, INFO_ROWS)], notes, sems.at[0]
-    )
-    note.start()
-    note.wait()
-    total = jnp.zeros((8, C), f32)
-    for source in range(owners):
-        rank = notes[source].astype(f32)[0:8]
+    order_ref, tail_ref, picks, sem = refs[-4:]
+    total = jnp.zeros((INFO_ROWS, C), f32)
+    for source in range(arrived_ref.shape[0]):
+        rank = arrived_ref[source, PAIR_ROWS:].astype(f32)
         total = total + jnp.where(rank > 0.0, rank + (CAP * source - 1.0), 0.0)
-    picks[...] = total.astype(jnp.int32)
-    to_scalars = pltpu.make_async_copy(picks.at[pl.ds(0, 1)], order_ref, sems.at[0])
+    picks[...] = total[0:8].astype(jnp.int32)
+    to_scalars = pltpu.make_async_copy(picks.at[pl.ds(0, 1)], order_ref, sem)
     to_scalars.start()
     to_scalars.wait()
-    copies = []
     for k in range(LEAD // 2):
-        copies.append(
-            pltpu.make_async_copy(
-                block_at(arrived_ref, order_ref[0, OWN - LEAD // 2 + k]),
-                tail_ref.at[pl.ds(k * 2 * POS, 2 * POS)],
-                sems.at[k],
-            )
-        )
-        copies[-1].start()
-    for copy in copies:
-        copy.wait()
+        block = block_at(arrived_ref, order_ref[0, OWN - LEAD // 2 + k])
+        tail_ref[k * 2 * POS : (k + 1) * 2 * POS] = block
 
 
 def block_at(arrived_ref, arrival):
     block_rows = PAIR_ROWS // CAP
     rows = pl.ds(pl.multiple_of((arrival & 1) * block_rows, block_rows), block_rows)
-    return arrived_ref.at[arrival >> 1, rows]
+    return arrived_ref[arrival >> 1, rows]
 
 
 def block_order(arrived, ready):
@@ -163,13 +158,9 @@
             jax.ShapeDtypeStruct((1, C), jnp.int32),
             jax.ShapeDtypeStruct((LEAD * POS, C), bf16),
         ),
-        in_specs=[hbm_only()] + [hbm()] * len(ready),
+        in_specs=[vmem()] + [hbm()] * len(ready),
         out_specs=(smem(), vmem()),
-        scratch_shapes=[
-            pltpu.VMEM((arrived.shape[0], INFO_ROWS, C), bf16),
-            pltpu.VMEM((8, C), jnp.int32),
-            pltpu.SemaphoreType.DMA((LEAD // 2,)),
-        ],
+        scratch_shapes=[pltpu.VMEM((8, C), jnp.int32), pltpu.SemaphoreType.DMA],
         compiler_params=params(),
         name="block_order",
     )(arrived, *ready)
@@ -190,20 +181,11 @@
         right_ref[at] = edge_rows(wide, COLS - 2 + c).astype(bf16)
 
 
-def place_kernel(order_ref, arrived_ref, frames_ref, left_ref, right_ref, wide, sems):
-    copies = [
-        pltpu.make_async_copy(
-            block_at(arrived_ref, order_ref[0, k]),
-            frames_ref.at[pl.ds(k * 2 * POS, 2 * POS)],
-            sems.at[k],
-        )
-        for k in range(OWN)
-    ]
-    for copy in copies:
-        copy.start()
+def place_kernel(order_ref, arrived_ref, frames_ref, left_ref, right_ref, wide):
     for k in range(OWN):
-        copies[k].wait()
-        wide[k % 2] = frames_ref[k * 2 * POS : (k + 1) * 2 * POS].astype(f32)
+        block = block_at(arrived_ref, order_ref[0, k])
+        frames_ref[k * 2 * POS : (k + 1) * 2 * POS] = block
+        wide[k % 2] = block.astype(f32)
         put_edges(wide.at[k % 2], (LEAD + 2 * k) * ROWS, left_ref, right_ref)
 
 
@@ -216,12 +198,9 @@
     return pl.pallas_call(
         place_kernel,
         out_shape=(jax.ShapeDtypeStruct((2 * OWN * POS, C), bf16), edge, edge),
-        in_specs=[smem(), hbm_only()],
+        in_specs=[smem(), vmem()],
         out_specs=(vmem(), vmem(), vmem()),
-        scratch_shapes=[
-            pltpu.VMEM((2, 2 * POS, C), f32),
-            pltpu.SemaphoreType.DMA((OWN,)),
-        ],
+        scratch_shapes=[pltpu.VMEM((2, 2 * POS, C), f32)],
         compiler_params=params(),
         name="place_blocks",
     )(order, arrived)
@@ -247,23 +226,32 @@
     )(lead, left, right)
 
 
-def join_kernel(first_ref, second_ref, first_out, second_out, token_out):
+def join_kernel(first_ref, second_ref, edge_out, first_out, second_out, token_out):
     token_out[...] = jnp.zeros_like(token_out)
-    for weight_ref, joined in ((first_ref, first_out), (second_ref, second_out)):
-        for j in range(3):
+    for j in range(3):
+        for lag in range(3):
             for i in range(3):
-                for lag in range(3):
-                    at = (3 * j + i) * C
-                    joined[at : at + C, lag * C : (lag + 1) * C] = weight_ref[2 - lag, i, j]
+                at = (3 * j + i) * C
+                edge_out[at : at + C, lag * C : (lag + 1) * C] = first_ref[2 - lag, i, j]
+            for weight_ref, joined in ((first_ref, first_out), (second_ref, second_out)):
+                for i in range(4):
+                    for parity in range(2):
+                        at = (4 * j + i) * C
+                        lane = (3 * parity + lag) * C
+                        inside = 0 <= i - parity <= 2
+                        joined[at : at + C, lane : lane + C] = (
+                            weight_ref[2 - lag, i - parity, j] if inside else jnp.zeros((C, C), bf16)
+                        )
 
 
 def join_weights(first, second):
-    joined = jax.ShapeDtypeStruct((9 * C, 3 * C), bf16)
+    edge = jax.ShapeDtypeStruct((9 * C, 3 * C), bf16)
+    joined = jax.ShapeDtypeStruct((12 * C, 6 * C), bf16)
     return pl.pallas_call(
         join_kernel,
-        out_shape=(joined, joined, jax.ShapeDtypeStruct((8, C), f32)),
+        out_shape=(edge, joined, joined, jax.ShapeDtypeStruct((8, C), f32)),
         in_specs=[vmem()] * 2,
-        out_specs=(vmem(),) * 3,
+        out_specs=(vmem(),) * 4,
         compiler_params=params(),
         name="join_weights",
     )(first, second)
@@ -277,16 +265,23 @@
             taps[j, q, r] = wide[base + j - 1 : base + j - 1 + COLS].astype(bf16)
     windows = jnp.concatenate(
         [
-            taps[j, 0:count, i : i + ROWS].reshape(count * POS, C)
+            jnp.concatenate(
+                [taps[j, q, i + 2 * p] for q in range(count) for p in range(ROWS // 2)], axis=0
+            )
             for j in range(3)
-            for i in range(3)
+            for i in range(4)
         ],
         axis=1,
     )
     product = jnp.dot(windows, joined[...], preferred_element_type=f32)
 
     def part(q, lag):
-        return product[q * POS : (q + 1) * POS, lag * C : (lag + 1) * C]
+        rows = []
+        for r in range(ROWS):
+            at = (q * (ROWS // 2) + r // 2) * COLS
+            lane = (3 * (r % 2) + lag) * C
+            rows.append(product[at : at + COLS, lane : lane + C])
+        return jnp.concatenate(rows, axis=0)
 
     totals = []
     for q in range(count):
@@ -339,8 +334,16 @@
     return entries
 
 
-def precise_dot(a, b):
-    return jnp.dot(a, b, precision=lax.Precision.HIGHEST, preferred_element_type=f32)
+def pick_columns(entries, picks):
+    count = entries.shape[0]
+    parts = []
+    for _ in range(3):
+        parts.append(entries.astype(bf16))
+        entries = entries - parts[-1].astype(f32)
+    picked = jnp.dot(
+        jnp.concatenate(parts, axis=0), picks.astype(bf16), preferred_element_type=f32
+    )
+    return picked[0:count] + picked[count : 2 * count] + picked[2 * count :]
 
 
 INNER = ROWS * (COLS - 2)
@@ -441,12 +444,11 @@
     mean = group_total(local) / 4
     off = local - mean
     spread = group_total(spread + POS * off * off)
-    channel = lax.broadcasted_iota(jnp.int32, (C, C), 0)
-    lane = lax.broadcasted_iota(jnp.int32, (C, C), 1)
-    packed = jnp.zeros((HALF, C), f32)
-    for q, piece in enumerate((mean[:HALF], spread[:HALF], mean[HALF:], spread[HALF:])):
-        picks = (channel == 4 * (lane - GROUPS * q)) & (lane // GROUPS == q)
-        packed = packed + precise_dot(piece, picks.astype(f32))
+    pieces = (mean[:HALF], spread[:HALF], mean[HALF:], spread[HALF:])
+    channel = lax.broadcasted_iota(jnp.int32, (4 * C, C), 0)
+    lane = lax.broadcasted_iota(jnp.int32, (4 * C, C), 1)
+    picks = channel == C * (lane // GROUPS) + (C // GROUPS) * (lane % GROUPS)
+    packed = pick_columns(jnp.concatenate(pieces, axis=1), picks.astype(f32))
     for peer in range(stats_ref.shape[0]):
         stats_ref[peer] = packed
 
@@ -482,13 +484,14 @@
     apart = jnp.where(is_mean, apart, 0.0)
     variance = (total + here * pltpu.roll(apart, GROUPS, 1)) / (here * tiles)
     packed = jnp.where(is_mean, mean, lax.rsqrt(jnp.where(is_mean, 1.0, variance) + EPSILON))
-    channel = lax.broadcasted_iota(jnp.int32, (C, C), 1)
-    source = lax.broadcasted_iota(jnp.int32, (C, C), 0)
-    for q in range(4):
-        picks = (source == channel // (C // GROUPS) + GROUPS * q).astype(f32)
-        target = scales if q % 2 else means
-        half = pl.ds((q // 2) * HALF, HALF)
-        target[half, :] = precise_dot(packed, picks)
+    source = lax.broadcasted_iota(jnp.int32, (C, 4 * C), 0)
+    column = lax.broadcasted_iota(jnp.int32, (C, 4 * C), 1)
+    picks = source == GROUPS * (column // C) + (column % C) // (C // GROUPS)
+    spread_out = pick_columns(packed, picks.astype(f32))
+    means[0:HALF] = spread_out[:, 0:C]
+    scales[0:HALF] = spread_out[:, C : 2 * C]
+    means[HALF:] = spread_out[:, 2 * C : 3 * C]
+    scales[HALF:] = spread_out[:, 3 * C :]
     scales[...] = scales[...] * gain_ref[...]
 
 
@@ -499,7 +502,7 @@
 def output_kernel(
     valid_ref, hidden_ref, edges_ref, stats_ref, frames_ref,
     gain_ref, norm_bias_ref, joined, bias_ref, out_ref,
-    wide, taps, carry, means, scales, halo,
+    wide, taps, carry, means, scales, halo, staged, sems,
 ):
     conv_setup(taps, carry)
     combine_stats(stats_ref, gain_ref, means, scales)
@@ -529,10 +532,18 @@
         for q in range(CHUNK):
             rows = pl.ds(pl.multiple_of((start + q) * POS, POS), POS)
             total = frames_ref[rows].astype(f32) + (totals[q] + bias_ref[...])
-            out_ref[rows] = total.astype(bf16)
+            staged[rows] = total.astype(bf16)
+        copy_out(start).start()
+
+    def copy_out(start):
+        rows = pl.ds(pl.multiple_of(start * POS, CHUNK * POS), CHUNK * POS)
+        sem = sems.at[lax.div(jnp.int32(start), jnp.int32(CHUNK))]
+        return pltpu.make_async_copy(staged.at[rows], out_ref.at[rows], sem)
 
     chunk_step(0, LEAD - 2, 2)
     over_chunks(own_chunk)
+    for start in range(0, 2 * OWN, CHUNK):
+        copy_out(start).wait()
 
 
 def second_layer(valid, hidden, edges, stats, frames, gain, norm_bias, weight, bias):
@@ -540,12 +551,14 @@
         output_kernel,
         out_shape=jax.ShapeDtypeStruct(frames.shape, bf16),
         in_specs=[smem()] + [vmem()] * 8,
-        out_specs=vmem(),
+        out_specs=hbm_only(),
         scratch_shapes=conv_scratch()
         + [
             pltpu.VMEM((2 * HALF, C), f32),
             pltpu.VMEM((2 * HALF, C), f32),
             pltpu.VMEM((UNROLL, 4, CHUNK * ROWS, C), f32),
+            pltpu.VMEM(frames.shape, bf16),
+            pltpu.SemaphoreType.DMA((2 * OWN // CHUNK,)),
         ],
         compiler_params=params(),
         name="second_layer",
@@ -588,7 +601,7 @@
         [lag_masks(clip_frames, position * length - LEAD, length + LEAD), inside[None]]
     ).astype(f32)
 
-    weight1, weight2, token = join_weights(conv1_weight, conv2_weight)
+    weight_edge, weight1, weight2, token = join_weights(conv1_weight, conv2_weight)
     order, tail = block_order(arrived, (valid, token))
     lead = lax.ppermute(tail, "tm", [(i, i + 1) for i in range(owners - 1)])
     frames, left, right = place_blocks(order, arrived)
@@ -596,7 +609,7 @@
     from_left, from_right = swap_edges(left, right)
     hidden, means, spreads = first_layer(valid, lead, frames, weight1)
     edges, stats = finish_hidden(
-        valid, left, right, from_left, from_right, weight1, means, spreads, tiles
+        valid, left, right, from_left, from_right, weight_edge, means, spreads, tiles
     )
     stats = lax.all_to_all(stats, "tile", split_axis=0, concat_axis=0, tiled=True)
     encoded = second_layer(

time: 110 us -> 108 us (0.982)
  Pallas kernels: 25.8 us -> 21.4 us
  local copies, waits for them, and re-layouts: 3.18 us -> 5.09 us
    all_to_all x1, waiting for transfers between devices: 46.3 us -> 44 us  [shards(): lax.all_to_all(outgoing, 'tm', split_axis=0, concat_axis=0, tiled=True)]
    unnamed x20 -> x24, local copies, waits for them, and re-layouts: 3.04 us -> 4.95 us
    ppermute x1, waiting for transfers between devices: 1.68 us -> 3.27 us  [shards(): lead = lax.ppermute(tail, 'tm', [(i, i + 1) for i in range(owners - 1)])]
    pallas_call x1, Pallas kernels: 2.57 us -> 0.98 us  [place_blocks(): pl.pallas_call(place_kernel, out_shape=(jax.ShapeDtypeStruct((2 * OWN * P...]
    pallas_call x1, Pallas kernels: 3.43 us -> 1.87 us  [send_blocks(): pl.pallas_call(send_kernel, out_shape=jax.ShapeDtypeStruct((owners, PAIR_...]
  transfers between devices with their start and end apart: 4 -> 4, of which waited for: 2 -> 2; matrix products, arithmetic and copies ran while one was open for 0% -> 0% of each run, Pallas kernels for 9% -> 8%
where the time goes in v4:
time: 108 us
  waiting for transfers between devices  47.3 us (44%)
  Pallas kernels  21.4 us (20%)
  blocking collectives  17 us (16%)
  starting transfers between devices  16.6 us (15%)
  local copies, waits for them, and re-layouts  5.09 us (5%)
    all_to_all x1, waiting for transfers between devices, shards(): lax.all_to_all(outgoing, 'tm', split_axis=0, concat_axis=0, tiled=True)  44 us
    all_to_all x1, blocking collectives, shards(): lax.all_to_all(stats, 'tile', split_axis=0, concat_axis=0, tiled=True)  17 us
    all_to_all x1, starting transfers between devices, shards(): lax.all_to_all(outgoing, 'tm', split_axis=0, concat_axis=0, tiled=True)  8.71 us
    pallas_call x1, Pallas kernels, second_layer(): pl.pallas_call(output_kernel, out_shape=jax.ShapeDtypeStruct(frames.shape...  7.4 us
    pallas_call x1, Pallas kernels, first_layer(): pl.pallas_call(hidden_kernel, out_shape=(jax.ShapeDtypeStruct((length, PO...  6.81 us
    unnamed x24, local copies, waits for them, and re-layouts  4.95 us
    ppermute x1, starting transfers between devices, swap_edges(): lax.ppermute(right, 'tile', [(i, i + 1) for i in range(count - 1)])  4.55 us
    ppermute x1, waiting for transfers between devices, shards(): lead = lax.ppermute(tail, 'tm', [(i, i + 1) for i in range(owners - 1)])  3.27 us
  transfers between devices with their start and end apart: 4, of which 2 were waited for; matrix products, arithmetic and copies ran while one was open for 0% of the time, Pallas kernels for 8%

profile of v4, /device:TPU:96, one launch (start us, length us, event | category | flops | bytes accessed | tf_op | source)
XLA Modules:
  0.0 108.0 jit_solution(1146587726806383441)
XLA Ops:
  0.0 1.9 %send_blocks.1 = bf16[16,528,128]{2,1,0:T(8,128)(2,1)} custom-call(s32[32]{0:T(128)} %slot_hbm.1, bf16[32,256,128]{2,1,0:T(8,128)(2,1)} %bitcast.24), custom_call_target="tpu_custom_call" | custom-call | tf_op jit(solution)/shard_map/send_blocks/pallas_call | solution.py:113
  1.9 0.0 copy-start.11
  1.9 0.0 copy-start.2
  1.9 8.7 %all-to-all-start = ((bf16[16,528,128]{2,1,0:T(8,128)(2,1)}), bf16[16,528,128]{2,1,0:T(8,128)(2,1)S(1)}, u32[]{:S(2)}, u32[]{:S(2)}) async-start(bf16[16,528,128]{2,1,0:T(8,128)(2,1)} %send_blocks.1), calls=%async_computation | async-start | bytes 4325376 | tf_op jit(solution)/shard_map/all_to_all | solution.py:597
  10.6 0.0 copy-done.11
  10.6 0.2 reduce-window.8
  10.8 0.0 copy-done.2
  10.8 0.0 copy-start.3
  10.8 1.2 %copy-done.3 = bf16[3,3,3,128,128]{4,3,2,1,0:T(8,128)(2,1)S(1)} copy-done((bf16[3,3,3,128,128]{4,3,2,1,0:T(8,128)(2,1)S(1)}, bf16[3,3,3,128,128]{4,3,2,1,0:T(8,128)(2,1)}, u32[]{:S(2)}) %copy-start.3) | copy-done | bytes 884760
  12.0 0.7 join_weights.1
  12.7 0.0 copy-start
  12.7 1.4 %copy-done = bf16[1536,768]{1,0:T(8,128)(2,1)} copy-done((bf16[1536,768]{1,0:T(8,128)(2,1)}, bf16[1536,768]{1,0:T(8,128)(2,1)S(1)}, u32[]{:S(2)}) %copy-start) | copy-done | bytes 2359320
  14.1 0.0 copy-start.4
  14.1 0.9 copy-done.4
  15.0 0.0 copy-start.9
  15.0 1.4 %copy-done.9 = bf16[1536,768]{1,0:T(8,128)(2,1)} copy-done((bf16[1536,768]{1,0:T(8,128)(2,1)}, bf16[1536,768]{1,0:T(8,128)(2,1)S(1)}, u32[]{:S(2)}) %copy-start.9) | copy-done | bytes 2359320
  16.4 0.1 stack.11
  16.6 0.1 convert_reduce_fusion.2
  16.7 44.0 %all-to-all-done.arrived_ref = bf16[16,528,128]{2,1,0:T(8,128)(2,1)S(1)} async-done(((bf16[16,528,128]{2,1,0:T(8,128)(2,1)}), bf16[16,528,128]{2,1,0:T(8,128)(2,1)S(1)}, u32[]{:S(2)}, u32[]{:S(2)}) %all-to-all-start) | async-done | bytes 2162720 | tf_op jit(solution)/shard_map/all_to_all | solution.py:597
  60.7 0.0 copy-start.10
  60.7 1.2 %block_order.1 = (s32[1,128]{1,0:T(1,128)S(1)}, bf16[512,128]{1,0:T(8,128)(2,1)S(1)}) custom-call(bf16[16,528,128]{2,1,0:T(8,128)(2,1)S(1)} %all-to-all-done.arrived_ref, f32[3,36]{1,0:T(4,128)S(1)} %add_convert_fusion.refs_0_.valid_ref, f32[8,128]{1,0:T(8,128)S(1)} %get-tuple-element.21.refs_1_), custom_call_target="tpu_custom_call" | custom-call | tf_op jit(solution)/shard_map/block_order/pallas_call | solution.py:155
  61.9 2.0 %collective-permute-start = (bf16[512,128]{1,0:T(8,128)(2,1)S(1)}, bf16[512,128]{1,0:T(8,128)(2,1)S(1)}, u32[]{:S(2)}, u32[]{:S(2)}) collective-permute-start(bf16[512,128]{1,0:T(8,128)(2,1)S(1)} %get-tuple-element.22), channel_id=1, source_target_pairs={{0,16},{16,32},{32,48},{48,64},{64,80},{80,96},{96,112},{112,128},... | collective-permute-start | bytes 393224 | tf_op jit(solution)/shard_map/ppermute | solution.py:606
  63.9 1.0 place_blocks.1
  64.9 3.3 %collective-permute-done.lead_ref = bf16[512,128]{1,0:T(8,128)(2,1)S(1)} collective-permute-done((bf16[512,128]{1,0:T(8,128)(2,1)S(1)}, bf16[512,128]{1,0:T(8,128)(2,1)S(1)}, u32[]{:S(2)}, u32[]{:S(2)}) %collective-permute-start) | collective-permute-done | bytes 131104 | tf_op jit(solution)/shard_map/ppermute | solution.py:606
  68.2 0.1 lead_edges.1
  68.2 1.3 %collective-permute-start.2 = (bf16[576,128]{1,0:T(8,128)(2,1)S(1)}, bf16[576,128]{1,0:T(8,128)(2,1)S(1)}, u32[]{:S(2)}, u32[]{:S(2)}) collective-permute-start(bf16[576,128]{1,0:T(8,128)(2,1)S(1)} %get-tuple-element.29.own_l), channel_id=1, source_target_pairs={{1,0},{2,1},{3,2},{4,3},{5,4},{6,5},{7,6},{8,7},{9,8},{10,9},{11,1... | collective-permute-start | bytes 442376 | tf_op jit(solution)/shard_map/ppermute | solution.py:583
  69.5 4.6 %collective-permute-start.1 = (bf16[576,128]{1,0:T(8,128)(2,1)S(1)}, bf16[576,128]{1,0:T(8,128)(2,1)S(1)}, u32[]{:S(2)}, u32[]{:S(2)}) collective-permute-start(bf16[576,128]{1,0:T(8,128)(2,1)S(1)} %get-tuple-element.30.own_r), channel_id=1, source_target_pairs={{0,1},{1,2},{2,3},{3,4},{4,5},{5,6},{6,7},{7,8},{8,9},{9,10},{10,1... | collective-permute-start | bytes 442376 | tf_op jit(solution)/shard_map/ppermute | solution.py:582
  74.1 0.0 copy-done.10
  74.1 0.0 copy-start.5
  74.1 0.0 copy-start.1
  74.1 0.0 copy-start.6
  74.2 0.0 copy-start.7
  74.2 0.0 copy-start.8
  74.2 6.8 %first_layer.1 = (f32[36,128,128]{2,1,0:T(8,128)S(1)}, f32[48,128]{1,0:T(8,128)S(1)}, f32[48,128]{1,0:T(8,128)S(1)}) custom-call(f32[3,36]{1,0:T(4,128)S(1)} %add_convert_fusion.refs_0_.valid_ref, bf16[512,128]{1,0:T(8,128)(2,1)S(1)} %collective-permute-done.lead_ref, bf16[4096,128]{1,0:T(8,128)(2,1)S(1)} %get-tuple-element.24.frames_ref, ...), custom_call_target="tpu_custom_call" | custom-call | flops 4076863488 | bytes 4194304 | tf_op jit(solution)/shard_map/first_layer/pallas_call | solution.py:387
  81.0 0.0 collective-permute-done.2.halo_r
  81.0 0.0 collective-permute-done.1.halo_l
  81.0 0.0 copy-done.5
  81.0 2.4 %finish_hidden.1 = (f32[4,288,128]{2,1,0:T(8,128)S(1)}, f32[16,24,128]{2,1,0:T(8,128)S(1)}) custom-call(f32[3,36]{1,0:T(4,128)S(1)} %add_convert_fusion.refs_0_.valid_ref, bf16[576,128]{1,0:T(8,128)(2,1)S(1)} %get-tuple-element.29.own_l, bf16[576,128]{1,0:T(8,128)(2,1)S(1)} %get-tuple-element.30.own_r, bf16[576,128]{1,0:T(8,128)(2,1)S(1)} %collective-permute-done.1.halo_l, ...), custom_call_target="tpu_custom_call" | custom-call | tf_op jit(solution)/shard_map/finish_hidden/pallas_call | solution.py:457
  83.4 17.0 %all_to_all.10.stats_ref = f32[16,24,128]{2,1,0:T(8,128)S(1)} all-to-all(f32[16,24,128]{2,1,0:T(8,128)S(1)} %get-tuple-element.35), channel_id=1, replica_groups=mesh['tm'=16,'tile'=16] {'tile'}, dimensions={0} | all-to-all | bytes 393216 | tf_op jit(solution)/shard_map/all_to_all | solution.py:614
  100.4 0.0 copy-done.1
  100.5 0.0 copy-done.6
  100.5 0.0 copy-done.7
  100.5 0.0 copy-done.8
  100.5 7.4 %second_layer.1 = bf16[4096,128]{1,0:T(8,128)(2,1)} custom-call(f32[3,36]{1,0:T(4,128)S(1)} %add_convert_fusion.refs_0_.valid_ref, f32[36,128,128]{2,1,0:T(8,128)S(1)} %get-tuple-element.26.hidden_ref, f32[4,288,128]{2,1,0:T(8,128)S(1)} %get-tuple-element.34.edges_ref, f32[16,24,128]{2,1,0:T(8,128)S(1)} %all_to_all.10.stats_ref, ...), custom_call_target="tpu_custom_call" | custom-call | tf_op jit(solution)/shard_map/second_layer/pallas_call | solution.py:550
  (4 shorter events, 0.0 us)
Async XLA Ops:
  1.9 8.7 %copy-start.11 = (s32[8]{0:T(128)S(1)}, s32[8]{0:T(128)}, u32[]{:S(2)}) copy-start(s32[8]{0:T(128)} %param.10) | copy-start | bytes 100
  1.9 8.9 %copy-start.2 = (bf16[3,3,3,128,128]{4,3,2,1,0:T(8,128)(2,1)S(1)}, bf16[3,3,3,128,128]{4,3,2,1,0:T(8,128)(2,1)}, u32[]{:S(2)}) copy-start(bf16[3,3,3,128,128]{4,3,2,1,0:T(8,128)(2,1)} %first_ref.1) | copy-start | bytes 2654212
  1.9 58.8 %all-to-all-start = ((bf16[16,528,128]{2,1,0:T(8,128)(2,1)}), bf16[16,528,128]{2,1,0:T(8,128)(2,1)S(1)}, u32[]{:S(2)}, u32[]{:S(2)}) async-start(bf16[16,528,128]{2,1,0:T(8,128)(2,1)} %send_blocks.1), calls=%async_computation | async-start | bytes 4325376 | tf_op jit(solution)/shard_map/all_to_all | solution.py:597
  10.8 1.2 %copy-start.3 = (bf16[3,3,3,128,128]{4,3,2,1,0:T(8,128)(2,1)S(1)}, bf16[3,3,3,128,128]{4,3,2,1,0:T(8,128)(2,1)}, u32[]{:S(2)}) copy-start(bf16[3,3,3,128,128]{4,3,2,1,0:T(8,128)(2,1)} %second_ref.1) | copy-start | bytes 2654212
  12.7 1.4 %copy-start = (bf16[1536,768]{1,0:T(8,128)(2,1)}, bf16[1536,768]{1,0:T(8,128)(2,1)S(1)}, u32[]{:S(2)}) copy-start(bf16[1536,768]{1,0:T(8,128)(2,1)S(1)} %get-tuple-element.36.joined) | copy-start | bytes 7077892
  14.1 0.9 copy-start.4
  15.0 1.4 %copy-start.9 = (bf16[1536,768]{1,0:T(8,128)(2,1)}, bf16[1536,768]{1,0:T(8,128)(2,1)S(1)}, u32[]{:S(2)}) copy-start(bf16[1536,768]{1,0:T(8,128)(2,1)S(1)} %get-tuple-element.25.joined) | copy-start | bytes 7077892
  60.7 13.4 %copy-start.10 = (bf16[1536,768]{1,0:T(8,128)(2,1)S(1)}, bf16[1536,768]{1,0:T(8,128)(2,1)}, u32[]{:S(2)}) copy-start(bf16[1536,768]{1,0:T(8,128)(2,1)} %copy-done.9) | copy-start | bytes 7077892
  61.9 6.3 %collective-permute-start = (bf16[512,128]{1,0:T(8,128)(2,1)S(1)}, bf16[512,128]{1,0:T(8,128)(2,1)S(1)}, u32[]{:S(2)}, u32[]{:S(2)}) collective-permute-start(bf16[512,128]{1,0:T(8,128)(2,1)S(1)} %get-tuple-element.22), channel_id=1, source_target_pairs={{0,16},{16,32},{32,48},{48,64},{64,80},{80,96},{96,112},{112,128},... | collective-permute-start | bytes 393224 | tf_op jit(solution)/shard_map/ppermute | solution.py:606
  68.2 12.7 %collective-permute-start.2 = (bf16[576,128]{1,0:T(8,128)(2,1)S(1)}, bf16[576,128]{1,0:T(8,128)(2,1)S(1)}, u32[]{:S(2)}, u32[]{:S(2)}) collective-permute-start(bf16[576,128]{1,0:T(8,128)(2,1)S(1)} %get-tuple-element.29.own_l), channel_id=1, source_target_pairs={{1,0},{2,1},{3,2},{4,3},{5,4},{6,5},{7,6},{8,7},{9,8},{10,9},{11,1... | collective-permute-start | bytes 442376 | tf_op jit(solution)/shard_map/ppermute | solution.py:583
  69.5 11.5 %collective-permute-start.1 = (bf16[576,128]{1,0:T(8,128)(2,1)S(1)}, bf16[576,128]{1,0:T(8,128)(2,1)S(1)}, u32[]{:S(2)}, u32[]{:S(2)}) collective-permute-start(bf16[576,128]{1,0:T(8,128)(2,1)S(1)} %get-tuple-element.30.own_r), channel_id=1, source_target_pairs={{0,1},{1,2},{2,3},{3,4},{4,5},{5,6},{6,7},{7,8},{8,9},{9,10},{10,1... | collective-permute-start | bytes 442376 | tf_op jit(solution)/shard_map/ppermute | solution.py:582
  74.1 6.9 %copy-start.5 = (bf16[1152,384]{1,0:T(8,128)(2,1)S(1)}, bf16[1152,384]{1,0:T(8,128)(2,1)}, u32[]{:S(2)}) copy-start(bf16[1152,384]{1,0:T(8,128)(2,1)} %copy-done.4) | copy-start | bytes 2654212
  74.1 26.3 %copy-start.1 = (bf16[1536,768]{1,0:T(8,128)(2,1)S(1)}, bf16[1536,768]{1,0:T(8,128)(2,1)}, u32[]{:S(2)}) copy-start(bf16[1536,768]{1,0:T(8,128)(2,1)} %copy-done) | copy-start | bytes 7077892
  74.1 26.3 %copy-start.6 = (f32[128]{0:T(128)S(1)}, f32[128]{0:T(128)}, u32[]{:S(2)}) copy-start(f32[128]{0:T(128)} %param.12) | copy-start | bytes 1540
  74.2 26.3 %copy-start.7 = (f32[128]{0:T(128)S(1)}, f32[128]{0:T(128)}, u32[]{:S(2)}) copy-start(f32[128]{0:T(128)} %param.13) | copy-start | bytes 1540
  74.2 26.3 %copy-start.8 = (f32[128]{0:T(128)S(1)}, f32[128]{0:T(128)}, u32[]{:S(2)}) copy-start(f32[128]{0:T(128)} %param.15) | copy-start | bytes 1540

commit v5 on v4

--- a/solution.py
+++ b/solution.py
@@ -226,44 +226,55 @@
     )(lead, left, right)
 
 
-def join_kernel(first_ref, second_ref, edge_out, first_out, second_out, token_out):
+def join_kernel(first_ref, second_ref, edge_out, near1, far1, near2, far2, token_out):
     token_out[...] = jnp.zeros_like(token_out)
     for j in range(3):
-        for lag in range(3):
-            for i in range(3):
-                at = (3 * j + i) * C
-                edge_out[at : at + C, lag * C : (lag + 1) * C] = first_ref[2 - lag, i, j]
-            for weight_ref, joined in ((first_ref, first_out), (second_ref, second_out)):
-                for i in range(4):
-                    for parity in range(2):
-                        at = (4 * j + i) * C
-                        lane = (3 * parity + lag) * C
-                        inside = 0 <= i - parity <= 2
-                        joined[at : at + C, lane : lane + C] = (
-                            weight_ref[2 - lag, i - parity, j] if inside else jnp.zeros((C, C), bf16)
-                        )
+        for i in range(3):
+            at = (3 * j + i) * C
+            for lag in range(3):
+                lane = slice(lag * C, (lag + 1) * C)
+                edge_out[at : at + C, lane] = first_ref[2 - lag, i, j]
+                if lag < 2:
+                    near1[at : at + C, lane] = first_ref[2 - lag, i, j]
+                    near2[at : at + C, lane] = second_ref[2 - lag, i, j]
+        for weight_ref, far in ((first_ref, far1), (second_ref, far2)):
+            for i in range(4):
+                for parity in range(2):
+                    at = (4 * j + i) * C
+                    inside = 0 <= i - parity <= 2
+                    far[at : at + C, parity * C : (parity + 1) * C] = (
+                        weight_ref[0, i - parity, j] if inside else jnp.zeros((C, C), bf16)
+                    )
 
 
 def join_weights(first, second):
-    edge = jax.ShapeDtypeStruct((9 * C, 3 * C), bf16)
-    joined = jax.ShapeDtypeStruct((12 * C, 6 * C), bf16)
+    shapes = ((9 * C, 3 * C),) + ((9 * C, 2 * C), (12 * C, 2 * C)) * 2
     return pl.pallas_call(
         join_kernel,
-        out_shape=(edge, joined, joined, jax.ShapeDtypeStruct((8, C), f32)),
+        out_shape=tuple(jax.ShapeDtypeStruct(shape, bf16) for shape in shapes)
+        + (jax.ShapeDtypeStruct((8, C), f32),),
         in_specs=[vmem()] * 2,
-        out_specs=(vmem(),) * 4,
+        out_specs=(vmem(),) * 6,
         compiler_params=params(),
         name="join_weights",
     )(first, second)
 
 
-def conv_chunk(valid_ref, start, count, wide, taps, joined, carry):
+def conv_chunk(valid_ref, start, count, wide, taps, near, far, carry):
     for at in range(count * ROWS):
         q, r = at // ROWS, at % ROWS + 1
         base = at * PITCH + 8
         for j in range(3):
             taps[j, q, r] = wide[base + j - 1 : base + j - 1 + COLS].astype(bf16)
     windows = jnp.concatenate(
+        [
+            taps[j, 0:count, i : i + ROWS].reshape(count * POS, C)
+            for j in range(3)
+            for i in range(3)
+        ],
+        axis=1,
+    )
+    pairs = jnp.concatenate(
         [
             jnp.concatenate(
                 [taps[j, q, i + 2 * p] for q in range(count) for p in range(ROWS // 2)], axis=0
@@ -273,14 +284,16 @@
         ],
         axis=1,
     )
-    product = jnp.dot(windows, joined[...], preferred_element_type=f32)
+    product = jnp.dot(windows, near[...], preferred_element_type=f32)
+    far_product = jnp.dot(pairs, far[...], preferred_element_type=f32)
 
     def part(q, lag):
+        if lag < 2:
+            return product[q * POS : (q + 1) * POS, lag * C : (lag + 1) * C]
         rows = []
         for r in range(ROWS):
             at = (q * (ROWS // 2) + r // 2) * COLS
-            lane = (3 * (r % 2) + lag) * C
-            rows.append(product[at : at + COLS, lane : lane + C])
+            rows.append(far_product[at : at + COLS, (r % 2) * C : (r % 2 + 1) * C])
         return jnp.concatenate(rows, axis=0)
 
     totals = []
@@ -350,7 +363,7 @@
 
 
 def hidden_kernel(
-    valid_ref, lead_ref, frames_ref, joined, hidden_ref, means_ref, spreads_ref,
+    valid_ref, lead_ref, frames_ref, near, far, hidden_ref, means_ref, spreads_ref,
     wide, taps, carry,
 ):
     conv_setup(taps, carry)
@@ -367,7 +380,7 @@
         for row in range(count * ROWS):
             here = source[pl.ds(pl.multiple_of(at + row * COLS, COLS), COLS)]
             wide[u, row * PITCH + 8 : row * PITCH + 8 + COLS] = here.astype(f32)
-        totals = conv_chunk(valid_ref, start, count, wide.at[u], taps.at[u], joined, carry)
+        totals = conv_chunk(valid_ref, start, count, wide.at[u], taps.at[u], near, far, carry)
         for q in range(count):
             frame = start + q
             own = totals[q]
@@ -381,13 +394,13 @@
     over_chunks(lambda u, at: chunk_step(u, LEAD + at, CHUNK, frames_ref, at * POS))
 
 
-def first_layer(valid, lead, frames, joined):
+def first_layer(valid, lead, frames, near, far):
     length = LEAD + 2 * OWN
     sums = jax.ShapeDtypeStruct((2 * HALF, C), f32)
     return pl.pallas_call(
         hidden_kernel,
         out_shape=(jax.ShapeDtypeStruct((length, POS, C), f32), sums, sums),
-        in_specs=[smem()] + [vmem()] * 3,
+        in_specs=[smem()] + [vmem()] * 4,
         out_specs=(vmem(),) * 3,
         scratch_shapes=conv_scratch(),
         compiler_params=params(),
@@ -395,7 +408,7 @@
             flops=2 * length * POS * 27 * C * C, bytes_accessed=4 * MIB, transcendentals=0
         ),
         name="first_layer",
-    )(valid, lead, frames, joined)
+    )(valid, lead, frames, near, far)
 
 
 def edge_kernel(
@@ -501,7 +514,7 @@
 
 def output_kernel(
     valid_ref, hidden_ref, edges_ref, stats_ref, frames_ref,
-    gain_ref, norm_bias_ref, joined, bias_ref, out_ref,
+    gain_ref, norm_bias_ref, near, far, bias_ref, out_ref,
     wide, taps, carry, means, scales, halo, staged, sems,
 ):
     conv_setup(taps, carry)
@@ -525,7 +538,7 @@
                 halo[u, k, q * ROWS : (q + 1) * ROWS] = norm(edges_ref[k, at], frame) * inside
         for k, column in enumerate((7, 8, 7 + COLS, 8 + COLS)):
             put_column(wide.at[u], column, halo[u, k, 0 : count * ROWS])
-        return conv_chunk(valid_ref, start, count, wide.at[u], taps.at[u], joined, carry)
+        return conv_chunk(valid_ref, start, count, wide.at[u], taps.at[u], near, far, carry)
 
     def own_chunk(u, start):
         totals = chunk_step(u, LEAD + start, CHUNK)
@@ -546,11 +559,11 @@
         copy_out(start).wait()
 
 
-def second_layer(valid, hidden, edges, stats, frames, gain, norm_bias, weight, bias):
+def second_layer(valid, hidden, edges, stats, frames, gain, norm_bias, near, far, bias):
     return pl.pallas_call(
         output_kernel,
         out_shape=jax.ShapeDtypeStruct(frames.shape, bf16),
-        in_specs=[smem()] + [vmem()] * 8,
+        in_specs=[smem()] + [vmem()] * 9,
         out_specs=hbm_only(),
         scratch_shapes=conv_scratch()
         + [
@@ -562,7 +575,7 @@
         ],
         compiler_params=params(),
         name="second_layer",
-    )(valid, hidden, edges, stats, frames, gain, norm_bias, weight, bias)
+    )(valid, hidden, edges, stats, frames, gain, norm_bias, near, far, bias)
 
 
 def lag_masks(clip_frames, first_frame, length):
@@ -601,20 +614,20 @@
         [lag_masks(clip_frames, position * length - LEAD, length + LEAD), inside[None]]
     ).astype(f32)
 
-    weight_edge, weight1, weight2, token = join_weights(conv1_weight, conv2_weight)
+    weight_edge, near1, far1, near2, far2, token = join_weights(conv1_weight, conv2_weight)
     order, tail = block_order(arrived, (valid, token))
     lead = lax.ppermute(tail, "tm", [(i, i + 1) for i in range(owners - 1)])
     frames, left, right = place_blocks(order, arrived)
     left, right = lead_edges(lead, left, right)
     from_left, from_right = swap_edges(left, right)
-    hidden, means, spreads = first_layer(valid, lead, frames, weight1)
+    hidden, means, spreads = first_layer(valid, lead, frames, near1, far1)
     edges, stats = finish_hidden(
         valid, left, right, from_left, from_right, weight_edge, means, spreads, tiles
     )
     stats = lax.all_to_all(stats, "tile", split_axis=0, concat_axis=0, tiled=True)
     encoded = second_layer(
         valid, hidden, edges, stats, frames, norm_gain[None], norm_bias[None],
-        weight2, conv2_bias[None],
+        near2, far2, conv2_bias[None],
     )
     return encoded.reshape((length,) + video.shape[2:])
 

time: 108 us -> 105 us (0.972)
  starting transfers between devices: 16.6 us -> 14.5 us
    ppermute x1, starting transfers between devices: 4.55 us -> 3.4 us  [swap_edges(): lax.ppermute(right, 'tile', [(i, i + 1) for i in range(count - 1)])]
    unnamed x24 -> x32, local copies, waits for them, and re-layouts: 4.95 us -> 5.54 us
  transfers between devices with their start and end apart: 4 -> 4, of which waited for: 2 -> 2; matrix products, arithmetic and copies ran while one was open for 0% -> 0% of each run, Pallas kernels for 8% -> 7%
where the time goes in v5:
time: 105 us
  waiting for transfers between devices  47 us (45%)
  Pallas kernels  20.6 us (20%)
  blocking collectives  16.3 us (16%)
  starting transfers between devices  14.5 us (14%)
  local copies, waits for them, and re-layouts  5.67 us (5%)
    all_to_all x1, waiting for transfers between devices, shards(): lax.all_to_all(outgoing, 'tm', split_axis=0, concat_axis=0, tiled=True)  43.7 us
    all_to_all x1, blocking collectives, shards(): lax.all_to_all(stats, 'tile', split_axis=0, concat_axis=0, tiled=True)  16.3 us
    all_to_all x1, starting transfers between devices, shards(): lax.all_to_all(outgoing, 'tm', split_axis=0, concat_axis=0, tiled=True)  7.83 us
    pallas_call x1, Pallas kernels, second_layer(): pl.pallas_call(output_kernel, out_shape=jax.ShapeDtypeStruct(frames.shape...  6.78 us
    pallas_call x1, Pallas kernels, first_layer(): pl.pallas_call(hidden_kernel, out_shape=(jax.ShapeDtypeStruct((length, PO...  6.1 us
    unnamed x32, local copies, waits for them, and re-layouts  5.54 us
    ppermute x1, starting transfers between devices, swap_edges(): lax.ppermute(right, 'tile', [(i, i + 1) for i in range(count - 1)])  3.4 us
    ppermute x1, waiting for transfers between devices, shards(): lead = lax.ppermute(tail, 'tm', [(i, i + 1) for i in range(owners - 1)])  3.27 us
  transfers between devices with their start and end apart: 4, of which 2 were waited for; matrix products, arithmetic and copies ran while one was open for 0% of the time, Pallas kernels for 7%

profile of v5, /device:TPU:96, one launch (start us, length us, event | category | flops | bytes accessed | tf_op | source)
XLA Modules:
  0.0 104.8 jit_solution(16294666541072321929)
XLA Ops:
  0.0 2.6 %send_blocks.1 = bf16[16,528,128]{2,1,0:T(8,128)(2,1)} custom-call(s32[32]{0:T(128)} %slot_hbm.1, bf16[32,256,128]{2,1,0:T(8,128)(2,1)} %bitcast.24), custom_call_target="tpu_custom_call" | custom-call | tf_op jit(solution)/shard_map/send_blocks/pallas_call | solution.py:113
  2.6 0.0 copy-start.15
  2.6 0.0 copy-start
  2.6 7.8 %all-to-all-start = ((bf16[16,528,128]{2,1,0:T(8,128)(2,1)}), bf16[16,528,128]{2,1,0:T(8,128)(2,1)S(1)}, u32[]{:S(2)}, u32[]{:S(2)}) async-start(bf16[16,528,128]{2,1,0:T(8,128)(2,1)} %send_blocks.1), calls=%async_computation | async-start | bytes 4325376 | tf_op jit(solution)/shard_map/all_to_all | solution.py:610
  10.5 0.0 copy-done.15
  10.5 0.2 reduce-window.8
  10.7 0.0 copy-done
  10.7 0.0 copy-start.1
  10.7 1.2 %copy-done.1 = bf16[3,3,3,128,128]{4,3,2,1,0:T(8,128)(2,1)S(1)} copy-done((bf16[3,3,3,128,128]{4,3,2,1,0:T(8,128)(2,1)S(1)}, bf16[3,3,3,128,128]{4,3,2,1,0:T(8,128)(2,1)}, u32[]{:S(2)}) %copy-start.1) | copy-done | bytes 884760
  11.8 0.5 join_weights.1
  12.3 0.0 copy-start.2
  12.3 0.9 copy-done.2
  13.2 0.0 copy-start.4
  13.2 0.9 copy-done.4
  14.1 0.0 copy-start.6
  14.1 0.8 copy-done.6
  14.9 0.0 copy-start.11
  14.9 0.9 copy-done.11
  15.8 0.0 copy-start.13
  15.8 0.8 copy-done.13
  16.6 0.1 stack.11
  16.8 0.1 convert_reduce_fusion.2
  16.9 43.7 %all-to-all-done.arrived_ref = bf16[16,528,128]{2,1,0:T(8,128)(2,1)S(1)} async-done(((bf16[16,528,128]{2,1,0:T(8,128)(2,1)}), bf16[16,528,128]{2,1,0:T(8,128)(2,1)S(1)}, u32[]{:S(2)}, u32[]{:S(2)}) %all-to-all-start) | async-done | bytes 2162720 | tf_op jit(solution)/shard_map/all_to_all | solution.py:610
  60.6 0.0 copy-start.12
  60.6 0.0 copy-start.14
  60.6 1.2 %block_order.1 = (s32[1,128]{1,0:T(1,128)S(1)}, bf16[512,128]{1,0:T(8,128)(2,1)S(1)}) custom-call(bf16[16,528,128]{2,1,0:T(8,128)(2,1)S(1)} %all-to-all-done.arrived_ref, f32[3,36]{1,0:T(4,128)S(1)} %add_convert_fusion.refs_0_.valid_ref, f32[8,128]{1,0:T(8,128)S(1)} %get-tuple-element.23.refs_1_), custom_call_target="tpu_custom_call" | custom-call | tf_op jit(solution)/shard_map/block_order/pallas_call | solution.py:155
  61.8 2.0 %collective-permute-start = (bf16[512,128]{1,0:T(8,128)(2,1)S(1)}, bf16[512,128]{1,0:T(8,128)(2,1)S(1)}, u32[]{:S(2)}, u32[]{:S(2)}) collective-permute-start(bf16[512,128]{1,0:T(8,128)(2,1)S(1)} %get-tuple-element.24), channel_id=1, source_target_pairs={{0,16},{16,32},{32,48},{48,64},{64,80},{80,96},{96,112},{112,128},... | collective-permute-start | bytes 393224 | tf_op jit(solution)/shard_map/ppermute | solution.py:619
  63.8 1.0 place_blocks.1
  64.8 3.3 %collective-permute-done.lead_ref = bf16[512,128]{1,0:T(8,128)(2,1)S(1)} collective-permute-done((bf16[512,128]{1,0:T(8,128)(2,1)S(1)}, bf16[512,128]{1,0:T(8,128)(2,1)S(1)}, u32[]{:S(2)}, u32[]{:S(2)}) %collective-permute-start) | collective-permute-done | bytes 131104 | tf_op jit(solution)/shard_map/ppermute | solution.py:619
  68.1 0.1 lead_edges.1
  68.1 3.4 %collective-permute-start.1 = (bf16[576,128]{1,0:T(8,128)(2,1)S(1)}, bf16[576,128]{1,0:T(8,128)(2,1)S(1)}, u32[]{:S(2)}, u32[]{:S(2)}) collective-permute-start(bf16[576,128]{1,0:T(8,128)(2,1)S(1)} %get-tuple-element.33.own_r), channel_id=1, source_target_pairs={{0,1},{1,2},{2,3},{3,4},{4,5},{5,6},{6,7},{7,8},{8,9},{9,10},{10,1... | collective-permute-start | bytes 442376 | tf_op jit(solution)/shard_map/ppermute | solution.py:595
  71.5 1.3 %collective-permute-start.2 = (bf16[576,128]{1,0:T(8,128)(2,1)S(1)}, bf16[576,128]{1,0:T(8,128)(2,1)S(1)}, u32[]{:S(2)}, u32[]{:S(2)}) collective-permute-start(bf16[576,128]{1,0:T(8,128)(2,1)S(1)} %get-tuple-element.32.own_l), channel_id=1, source_target_pairs={{1,0},{2,1},{3,2},{4,3},{5,4},{6,5},{7,6},{8,7},{9,8},{10,9},{11,1... | collective-permute-start | bytes 442376 | tf_op jit(solution)/shard_map/ppermute | solution.py:596
  72.8 0.0 copy-done.12
  72.8 0.0 copy-done.14
  72.8 0.0 copy-start.3
  72.9 0.0 copy-start.8
  72.9 0.0 copy-start.9
  72.9 0.0 copy-start.10
  72.9 6.1 %first_layer.1 = (f32[36,128,128]{2,1,0:T(8,128)S(1)}, f32[48,128]{1,0:T(8,128)S(1)}, f32[48,128]{1,0:T(8,128)S(1)}) custom-call(f32[3,36]{1,0:T(4,128)S(1)} %add_convert_fusion.refs_0_.valid_ref, bf16[512,128]{1,0:T(8,128)(2,1)S(1)} %collective-permute-done.lead_ref, bf16[4096,128]{1,0:T(8,128)(2,1)S(1)} %get-tuple-element.26.frames_ref, ...), custom_call_target="tpu_custom_call" | custom-call | flops 4076863488 | bytes 4194304 | tf_op jit(solution)/shard_map/first_layer/pallas_call | solution.py:400
  79.0 0.0 copy-start.5
  79.0 0.0 copy-start.7
  79.0 0.0 collective-permute-done.1.halo_l
  79.0 0.0 collective-permute-done.2.halo_r
  79.0 0.0 copy-done.3
  79.0 2.4 %finish_hidden.1 = (f32[4,288,128]{2,1,0:T(8,128)S(1)}, f32[16,24,128]{2,1,0:T(8,128)S(1)}) custom-call(f32[3,36]{1,0:T(4,128)S(1)} %add_convert_fusion.refs_0_.valid_ref, bf16[576,128]{1,0:T(8,128)(2,1)S(1)} %get-tuple-element.32.own_l, bf16[576,128]{1,0:T(8,128)(2,1)S(1)} %get-tuple-element.33.own_r, bf16[576,128]{1,0:T(8,128)(2,1)S(1)} %collective-permute-done.1.halo_l, ...), custom_call_target="tpu_custom_call" | custom-call | tf_op jit(solution)/shard_map/finish_hidden/pallas_call | solution.py:470
  81.5 16.3 %all_to_all.10.stats_ref = f32[16,24,128]{2,1,0:T(8,128)S(1)} all-to-all(f32[16,24,128]{2,1,0:T(8,128)S(1)} %get-tuple-element.38), channel_id=1, replica_groups=mesh['tm'=16,'tile'=16] {'tile'}, dimensions={0} | all-to-all | bytes 393216 | tf_op jit(solution)/shard_map/all_to_all | solution.py:627
  97.8 0.0 copy-done.8
  97.8 0.0 copy-done.9
  97.8 0.0 copy-done.10
  97.8 0.0 copy-done.5
  97.8 0.0 copy-done.7
  97.8 6.8 %second_layer.1 = bf16[4096,128]{1,0:T(8,128)(2,1)} custom-call(f32[3,36]{1,0:T(4,128)S(1)} %add_convert_fusion.refs_0_.valid_ref, f32[36,128,128]{2,1,0:T(8,128)S(1)} %get-tuple-element.29.hidden_ref, f32[4,288,128]{2,1,0:T(8,128)S(1)} %get-tuple-element.37.edges_ref, f32[16,24,128]{2,1,0:T(8,128)S(1)} %all_to_all.10.stats_ref, ...), custom_call_target="tpu_custom_call" | custom-call | tf_op jit(solution)/shard_map/second_layer/pallas_call | solution.py:563
  (4 shorter events, 0.0 us)
Async XLA Ops:
  2.6 7.9 %copy-start.15 = (s32[8]{0:T(128)S(1)}, s32[8]{0:T(128)}, u32[]{:S(2)}) copy-start(s32[8]{0:T(128)} %param.10) | copy-start | bytes 100
  2.6 8.0 %copy-start = (bf16[3,3,3,128,128]{4,3,2,1,0:T(8,128)(2,1)S(1)}, bf16[3,3,3,128,128]{4,3,2,1,0:T(8,128)(2,1)}, u32[]{:S(2)}) copy-start(bf16[3,3,3,128,128]{4,3,2,1,0:T(8,128)(2,1)} %first_ref.1) | copy-start | bytes 2654212
  2.6 57.9 %all-to-all-start = ((bf16[16,528,128]{2,1,0:T(8,128)(2,1)}), bf16[16,528,128]{2,1,0:T(8,128)(2,1)S(1)}, u32[]{:S(2)}, u32[]{:S(2)}) async-start(bf16[16,528,128]{2,1,0:T(8,128)(2,1)} %send_blocks.1), calls=%async_computation | async-start | bytes 4325376 | tf_op jit(solution)/shard_map/all_to_all | solution.py:610
  10.7 1.2 %copy-start.1 = (bf16[3,3,3,128,128]{4,3,2,1,0:T(8,128)(2,1)S(1)}, bf16[3,3,3,128,128]{4,3,2,1,0:T(8,128)(2,1)}, u32[]{:S(2)}) copy-start(bf16[3,3,3,128,128]{4,3,2,1,0:T(8,128)(2,1)} %second_ref.1) | copy-start | bytes 2654212
  12.3 0.9 copy-start.2
  13.2 0.9 copy-start.4
  14.1 0.8 copy-start.6
  14.9 0.9 copy-start.11
  15.8 0.8 copy-start.13
  60.6 12.2 %copy-start.12 = (bf16[1536,256]{1,0:T(8,128)(2,1)S(1)}, bf16[1536,256]{1,0:T(8,128)(2,1)}, u32[]{:S(2)}) copy-start(bf16[1536,256]{1,0:T(8,128)(2,1)} %copy-done.11) | copy-start | bytes 2359300
  60.6 12.2 %copy-start.14 = (bf16[1152,256]{1,0:T(8,128)(2,1)S(1)}, bf16[1152,256]{1,0:T(8,128)(2,1)}, u32[]{:S(2)}) copy-start(bf16[1152,256]{1,0:T(8,128)(2,1)} %copy-done.13) | copy-start | bytes 1769476
  61.8 6.3 %collective-permute-start = (bf16[512,128]{1,0:T(8,128)(2,1)S(1)}, bf16[512,128]{1,0:T(8,128)(2,1)S(1)}, u32[]{:S(2)}, u32[]{:S(2)}) collective-permute-start(bf16[512,128]{1,0:T(8,128)(2,1)S(1)} %get-tuple-element.24), channel_id=1, source_target_pairs={{0,16},{16,32},{32,48},{48,64},{64,80},{80,96},{96,112},{112,128},... | collective-permute-start | bytes 393224 | tf_op jit(solution)/shard_map/ppermute | solution.py:619
  68.1 10.9 %collective-permute-start.1 = (bf16[576,128]{1,0:T(8,128)(2,1)S(1)}, bf16[576,128]{1,0:T(8,128)(2,1)S(1)}, u32[]{:S(2)}, u32[]{:S(2)}) collective-permute-start(bf16[576,128]{1,0:T(8,128)(2,1)S(1)} %get-tuple-element.33.own_r), channel_id=1, source_target_pairs={{0,1},{1,2},{2,3},{3,4},{4,5},{5,6},{6,7},{7,8},{8,9},{9,10},{10,1... | collective-permute-start | bytes 442376 | tf_op jit(solution)/shard_map/ppermute | solution.py:595
  71.5 7.5 %collective-permute-start.2 = (bf16[576,128]{1,0:T(8,128)(2,1)S(1)}, bf16[576,128]{1,0:T(8,128)(2,1)S(1)}, u32[]{:S(2)}, u32[]{:S(2)}) collective-permute-start(bf16[576,128]{1,0:T(8,128)(2,1)S(1)} %get-tuple-element.32.own_l), channel_id=1, source_target_pairs={{1,0},{2,1},{3,2},{4,3},{5,4},{6,5},{7,6},{8,7},{9,8},{10,9},{11,1... | collective-permute-start | bytes 442376 | tf_op jit(solution)/shard_map/ppermute | solution.py:596
  72.8 6.2 %copy-start.3 = (bf16[1152,384]{1,0:T(8,128)(2,1)S(1)}, bf16[1152,384]{1,0:T(8,128)(2,1)}, u32[]{:S(2)}) copy-start(bf16[1152,384]{1,0:T(8,128)(2,1)} %copy-done.2) | copy-start | bytes 2654212
  72.9 24.9 %copy-start.8 = (f32[128]{0:T(128)S(1)}, f32[128]{0:T(128)}, u32[]{:S(2)}) copy-start(f32[128]{0:T(128)} %param.12) | copy-start | bytes 1540
  72.9 24.9 %copy-start.9 = (f32[128]{0:T(128)S(1)}, f32[128]{0:T(128)}, u32[]{:S(2)}) copy-start(f32[128]{0:T(128)} %param.13) | copy-start | bytes 1540
  72.9 24.9 %copy-start.10 = (f32[128]{0:T(128)S(1)}, f32[128]{0:T(128)}, u32[]{:S(2)}) copy-start(f32[128]{0:T(128)} %param.15) | copy-start | bytes 1540
  79.0 18.8 %copy-start.5 = (bf16[1536,256]{1,0:T(8,128)(2,1)S(1)}, bf16[1536,256]{1,0:T(8,128)(2,1)}, u32[]{:S(2)}) copy-start(bf16[1536,256]{1,0:T(8,128)(2,1)} %copy-done.4) | copy-start | bytes 2359300
  79.0 18.8 %copy-start.7 = (bf16[1152,256]{1,0:T(8,128)(2,1)S(1)}, bf16[1152,256]{1,0:T(8,128)(2,1)}, u32[]{:S(2)}) copy-start(bf16[1152,256]{1,0:T(8,128)(2,1)} %copy-done.6) | copy-start | bytes 1769476

commit v6 on v5

--- a/solution.py
+++ b/solution.py
@@ -139,10 +139,12 @@
     picks[...] = total[0:8].astype(jnp.int32)
     to_scalars = pltpu.make_async_copy(picks.at[pl.ds(0, 1)], order_ref, sem)
     to_scalars.start()
+    lane = lax.broadcasted_iota(jnp.int32, (8, C), 1)
+    for k in range(LEAD // 2):
+        arrival = jnp.max(jnp.where(lane == OWN - LEAD // 2 + k, total[0:8], 0.0))
+        block = block_at(arrived_ref, arrival.astype(jnp.int32))
+        tail_ref[k * 2 * POS : (k + 1) * 2 * POS] = block
     to_scalars.wait()
-    for k in range(LEAD // 2):
-        block = block_at(arrived_ref, order_ref[0, OWN - LEAD // 2 + k])
-        tail_ref[k * 2 * POS : (k + 1) * 2 * POS] = block
 
 
 def block_at(arrived_ref, arrival):
@@ -181,11 +183,9 @@
         right_ref[at] = edge_rows(wide, COLS - 2 + c).astype(bf16)
 
 
-def place_kernel(order_ref, arrived_ref, frames_ref, left_ref, right_ref, wide):
+def own_kernel(order_ref, arrived_ref, left_ref, right_ref, wide):
     for k in range(OWN):
-        block = block_at(arrived_ref, order_ref[0, k])
-        frames_ref[k * 2 * POS : (k + 1) * 2 * POS] = block
-        wide[k % 2] = block.astype(f32)
+        wide[k % 2] = block_at(arrived_ref, order_ref[0, k]).astype(f32)
         put_edges(wide.at[k % 2], (LEAD + 2 * k) * ROWS, left_ref, right_ref)
 
 
@@ -193,16 +193,16 @@
     return jax.ShapeDtypeStruct((2 * EDGE_ROWS, C), dtype)
 
 
-def place_blocks(order, arrived):
+def own_edges(order, arrived):
     edge = edge_shape(bf16)
     return pl.pallas_call(
-        place_kernel,
-        out_shape=(jax.ShapeDtypeStruct((2 * OWN * POS, C), bf16), edge, edge),
+        own_kernel,
+        out_shape=(edge, edge),
         in_specs=[smem(), vmem()],
-        out_specs=(vmem(), vmem(), vmem()),
+        out_specs=(vmem(), vmem()),
         scratch_shapes=[pltpu.VMEM((2, 2 * POS, C), f32)],
         compiler_params=params(),
-        name="place_blocks",
+        name="own_edges",
     )(order, arrived)
 
 
@@ -363,7 +363,7 @@
 
 
 def hidden_kernel(
-    valid_ref, lead_ref, frames_ref, near, far, hidden_ref, means_ref, spreads_ref,
+    valid_ref, order_ref, lead_ref, arrived_ref, near, far, hidden_ref, means_ref, spreads_ref,
     wide, taps, carry,
 ):
     conv_setup(taps, carry)
@@ -376,10 +376,12 @@
     column = lax.broadcasted_iota(jnp.int32, (POS, C), 0) % COLS
     inner = (column > 0) & (column < COLS - 1)
 
-    def chunk_step(u, start, count, source, at):
-        for row in range(count * ROWS):
-            here = source[pl.ds(pl.multiple_of(at + row * COLS, COLS), COLS)]
-            wide[u, row * PITCH + 8 : row * PITCH + 8 + COLS] = here.astype(f32)
+    def chunk_step(u, start, count, block_of):
+        for k in range(count // 2):
+            block = block_of(k).astype(f32)
+            for row in range(2 * ROWS):
+                at = (k * 2 * ROWS + row) * PITCH + 8
+                wide[u, at : at + COLS] = block[row * COLS : (row + 1) * COLS]
         totals = conv_chunk(valid_ref, start, count, wide.at[u], taps.at[u], near, far, carry)
         for q in range(count):
             frame = start + q
@@ -390,25 +392,28 @@
             means_ref[pl.ds(frame, 1), :] = mean
             spreads_ref[pl.ds(frame, 1), :] = jnp.sum(centred * centred, axis=0, keepdims=True)
 
-    chunk_step(0, 0, LEAD, lead_ref, 0)
-    over_chunks(lambda u, at: chunk_step(u, LEAD + at, CHUNK, frames_ref, at * POS))
-
-
-def first_layer(valid, lead, frames, near, far):
+    def own_block(at):
+        return lambda k: block_at(arrived_ref, order_ref[0, at // 2 + k])
+
+    chunk_step(0, 0, LEAD, lambda k: lead_ref[k * 2 * POS : (k + 1) * 2 * POS])
+    over_chunks(lambda u, at: chunk_step(u, LEAD + at, CHUNK, own_block(at)))
+
+
+def first_layer(valid, order, lead, arrived, near, far):
     length = LEAD + 2 * OWN
     sums = jax.ShapeDtypeStruct((2 * HALF, C), f32)
     return pl.pallas_call(
         hidden_kernel,
         out_shape=(jax.ShapeDtypeStruct((length, POS, C), f32), sums, sums),
-        in_specs=[smem()] + [vmem()] * 4,
+        in_specs=[smem()] * 2 + [vmem()] * 4,
         out_specs=(vmem(),) * 3,
         scratch_shapes=conv_scratch(),
-        compiler_params=params(),
+        compiler_params=params(24),
         cost_estimate=pl.CostEstimate(
             flops=2 * length * POS * 27 * C * C, bytes_accessed=4 * MIB, transcendentals=0
         ),
         name="first_layer",
-    )(valid, lead, frames, near, far)
+    )(valid, order, lead, arrived, near, far)
 
 
 def edge_kernel(
@@ -513,7 +518,7 @@
 
 
 def output_kernel(
-    valid_ref, hidden_ref, edges_ref, stats_ref, frames_ref,
+    valid_ref, order_ref, hidden_ref, edges_ref, stats_ref, arrived_ref,
     gain_ref, norm_bias_ref, near, far, bias_ref, out_ref,
     wide, taps, carry, means, scales, halo, staged, sems,
 ):
@@ -542,9 +547,10 @@
 
     def own_chunk(u, start):
         totals = chunk_step(u, LEAD + start, CHUNK)
-        for q in range(CHUNK):
-            rows = pl.ds(pl.multiple_of((start + q) * POS, POS), POS)
-            total = frames_ref[rows].astype(f32) + (totals[q] + bias_ref[...])
+        for k in range(CHUNK // 2):
+            block = block_at(arrived_ref, order_ref[0, start // 2 + k]).astype(f32)
+            total = block + (jnp.concatenate(totals[2 * k : 2 * k + 2], axis=0) + bias_ref[...])
+            rows = pl.ds(pl.multiple_of((start + 2 * k) * POS, 2 * POS), 2 * POS)
             staged[rows] = total.astype(bf16)
         copy_out(start).start()
 
@@ -559,23 +565,23 @@
         copy_out(start).wait()
 
 
-def second_layer(valid, hidden, edges, stats, frames, gain, norm_bias, near, far, bias):
+def second_layer(valid, order, hidden, edges, stats, arrived, gain, norm_bias, near, far, bias):
     return pl.pallas_call(
         output_kernel,
-        out_shape=jax.ShapeDtypeStruct(frames.shape, bf16),
-        in_specs=[smem()] + [vmem()] * 9,
+        out_shape=jax.ShapeDtypeStruct((2 * OWN * POS, C), bf16),
+        in_specs=[smem()] * 2 + [vmem()] * 9,
         out_specs=hbm_only(),
         scratch_shapes=conv_scratch()
         + [
             pltpu.VMEM((2 * HALF, C), f32),
             pltpu.VMEM((2 * HALF, C), f32),
             pltpu.VMEM((UNROLL, 4, CHUNK * ROWS, C), f32),
-            pltpu.VMEM(frames.shape, bf16),
+            pltpu.VMEM((2 * OWN * POS, C), bf16),
             pltpu.SemaphoreType.DMA((2 * OWN // CHUNK,)),
         ],
-        compiler_params=params(),
+        compiler_params=params(24),
         name="second_layer",
-    )(valid, hidden, edges, stats, frames, gain, norm_bias, near, far, bias)
+    )(valid, order, hidden, edges, stats, arrived, gain, norm_bias, near, far, bias)
 
 
 def lag_masks(clip_frames, first_frame, length):
@@ -617,16 +623,16 @@
     weight_edge, near1, far1, near2, far2, token = join_weights(conv1_weight, conv2_weight)
     order, tail = block_order(arrived, (valid, token))
     lead = lax.ppermute(tail, "tm", [(i, i + 1) for i in range(owners - 1)])
-    frames, left, right = place_blocks(order, arrived)
+    left, right = own_edges(order, arrived)
     left, right = lead_edges(lead, left, right)
     from_left, from_right = swap_edges(left, right)
-    hidden, means, spreads = first_layer(valid, lead, frames, near1, far1)
+    hidden, means, spreads = first_layer(valid, order, lead, arrived, near1, far1)
     edges, stats = finish_hidden(
         valid, left, right, from_left, from_right, weight_edge, means, spreads, tiles
     )
     stats = lax.all_to_all(stats, "tile", split_axis=0, concat_axis=0, tiled=True)
     encoded = second_layer(
-        valid, hidden, edges, stats, frames, norm_gain[None], norm_bias[None],
+        valid, order, hidden, edges, stats, arrived, norm_gain[None], norm_bias[None],
         near2, far2, conv2_bias[None],
     )
     return encoded.reshape((length,) + video.shape[2:])

time: 105 us -> 105 us (level)
  no operation moved by 1% of the time
where the time goes in v6:
time: 105 us
  waiting for transfers between devices  47.1 us (45%)
  Pallas kernels  20.4 us (19%)
  blocking collectives  16.3 us (16%)
  starting transfers between devices  14.7 us (14%)
  local copies, waits for them, and re-layouts  5.67 us (5%)
    all_to_all x1, waiting for transfers between devices, shards(): lax.all_to_all(outgoing, 'tm', split_axis=0, concat_axis=0, tiled=True)  43.7 us
    all_to_all x1, blocking collectives, shards(): lax.all_to_all(stats, 'tile', split_axis=0, concat_axis=0, tiled=True)  16.3 us
    all_to_all x1, starting transfers between devices, shards(): lax.all_to_all(outgoing, 'tm', split_axis=0, concat_axis=0, tiled=True)  7.97 us
    pallas_call x1, Pallas kernels, second_layer(): pl.pallas_call(output_kernel, out_shape=jax.ShapeDtypeStruct((2 * OWN * P...  6.84 us
    pallas_call x1, Pallas kernels, first_layer(): pl.pallas_call(hidden_kernel, out_shape=(jax.ShapeDtypeStruct((length, PO...  6.09 us
    unnamed x32, local copies, waits for them, and re-layouts  5.54 us
    ppermute x1, waiting for transfers between devices, shards(): lead = lax.ppermute(tail, 'tm', [(i, i + 1) for i in range(owners - 1)])  3.43 us
    ppermute x1, starting transfers between devices, swap_edges(): lax.ppermute(right, 'tile', [(i, i + 1) for i in range(count - 1)])  3.4 us
  transfers between devices with their start and end apart: 4, of which 2 were waited for; matrix products, arithmetic and copies ran while one was open for 0% of the time, Pallas kernels for 7%

profile of v6, /device:TPU:96, one launch (start us, length us, event | category | flops | bytes accessed | tf_op | source)
XLA Modules:
  0.0 104.9 jit_solution(3884190995124034656)
XLA Ops:
  0.0 2.5 %send_blocks.1 = bf16[16,528,128]{2,1,0:T(8,128)(2,1)} custom-call(s32[32]{0:T(128)} %slot_hbm.1, bf16[32,256,128]{2,1,0:T(8,128)(2,1)} %bitcast.24), custom_call_target="tpu_custom_call" | custom-call | tf_op jit(solution)/shard_map/send_blocks/pallas_call | solution.py:113
  2.6 0.0 copy-start.15
  2.6 0.0 copy-start
  2.6 8.0 %all-to-all-start = ((bf16[16,528,128]{2,1,0:T(8,128)(2,1)}), bf16[16,528,128]{2,1,0:T(8,128)(2,1)S(1)}, u32[]{:S(2)}, u32[]{:S(2)}) async-start(bf16[16,528,128]{2,1,0:T(8,128)(2,1)} %send_blocks.1), calls=%async_computation | async-start | bytes 4325376 | tf_op jit(solution)/shard_map/all_to_all | solution.py:616
  10.6 0.0 copy-done.15
  10.6 0.2 reduce-window.8
  10.7 0.0 copy-done
  10.7 0.0 copy-start.1
  10.7 1.2 %copy-done.1 = bf16[3,3,3,128,128]{4,3,2,1,0:T(8,128)(2,1)S(1)} copy-done((bf16[3,3,3,128,128]{4,3,2,1,0:T(8,128)(2,1)S(1)}, bf16[3,3,3,128,128]{4,3,2,1,0:T(8,128)(2,1)}, u32[]{:S(2)}) %copy-start.1) | copy-done | bytes 884760
  11.9 0.5 join_weights.1
  12.4 0.0 copy-start.2
  12.4 0.9 copy-done.2
  13.3 0.0 copy-start.4
  13.3 0.9 copy-done.4
  14.2 0.0 copy-start.6
  14.2 0.8 copy-done.6
  15.0 0.0 copy-start.11
  15.0 0.9 copy-done.11
  15.9 0.0 copy-start.13
  15.9 0.8 copy-done.13
  16.7 0.1 stack.11
  16.9 0.1 convert_reduce_fusion.2
  17.0 43.7 %all-to-all-done.arrived_ref = bf16[16,528,128]{2,1,0:T(8,128)(2,1)S(1)} async-done(((bf16[16,528,128]{2,1,0:T(8,128)(2,1)}), bf16[16,528,128]{2,1,0:T(8,128)(2,1)S(1)}, u32[]{:S(2)}, u32[]{:S(2)}) %all-to-all-start) | async-done | bytes 2162720 | tf_op jit(solution)/shard_map/all_to_all | solution.py:616
  60.7 0.0 copy-start.12
  60.7 0.0 copy-start.14
  60.7 1.2 %block_order.1 = (s32[1,128]{1,0:T(1,128)S(1)}, bf16[512,128]{1,0:T(8,128)(2,1)S(1)}) custom-call(bf16[16,528,128]{2,1,0:T(8,128)(2,1)S(1)} %all-to-all-done.arrived_ref, f32[3,36]{1,0:T(4,128)S(1)} %add_convert_fusion.refs_0_.valid_ref, f32[8,128]{1,0:T(8,128)S(1)} %get-tuple-element.22.refs_1_), custom_call_target="tpu_custom_call" | custom-call | tf_op jit(solution)/shard_map/block_order/pallas_call | solution.py:157
  61.8 2.0 %collective-permute-start = (bf16[512,128]{1,0:T(8,128)(2,1)S(1)}, bf16[512,128]{1,0:T(8,128)(2,1)S(1)}, u32[]{:S(2)}, u32[]{:S(2)}) collective-permute-start(bf16[512,128]{1,0:T(8,128)(2,1)S(1)} %get-tuple-element.24), channel_id=1, source_target_pairs={{0,16},{16,32},{32,48},{48,64},{64,80},{80,96},{96,112},{112,128},... | collective-permute-start | bytes 393224 | tf_op jit(solution)/shard_map/ppermute | solution.py:625
  63.9 0.8 own_edges.1
  64.7 3.4 %collective-permute-done.lead_ref = bf16[512,128]{1,0:T(8,128)(2,1)S(1)} collective-permute-done((bf16[512,128]{1,0:T(8,128)(2,1)S(1)}, bf16[512,128]{1,0:T(8,128)(2,1)S(1)}, u32[]{:S(2)}, u32[]{:S(2)}) %collective-permute-start) | collective-permute-done | bytes 131104 | tf_op jit(solution)/shard_map/ppermute | solution.py:625
  68.1 0.1 lead_edges.1
  68.2 3.4 %collective-permute-start.1 = (bf16[576,128]{1,0:T(8,128)(2,1)S(1)}, bf16[576,128]{1,0:T(8,128)(2,1)S(1)}, u32[]{:S(2)}, u32[]{:S(2)}) collective-permute-start(bf16[576,128]{1,0:T(8,128)(2,1)S(1)} %get-tuple-element.31.own_r), channel_id=1, source_target_pairs={{0,1},{1,2},{2,3},{3,4},{4,5},{5,6},{6,7},{7,8},{8,9},{9,10},{10,1... | collective-permute-start | bytes 442376 | tf_op jit(solution)/shard_map/ppermute | solution.py:601
  71.6 1.3 %collective-permute-start.2 = (bf16[576,128]{1,0:T(8,128)(2,1)S(1)}, bf16[576,128]{1,0:T(8,128)(2,1)S(1)}, u32[]{:S(2)}, u32[]{:S(2)}) collective-permute-start(bf16[576,128]{1,0:T(8,128)(2,1)S(1)} %get-tuple-element.30.own_l), channel_id=1, source_target_pairs={{1,0},{2,1},{3,2},{4,3},{5,4},{6,5},{7,6},{8,7},{9,8},{10,9},{11,1... | collective-permute-start | bytes 442376 | tf_op jit(solution)/shard_map/ppermute | solution.py:602
  72.9 0.0 copy-done.12
  72.9 0.0 copy-done.14
  72.9 0.0 copy-start.3
  72.9 0.0 copy-start.8
  72.9 0.0 copy-start.9
  73.0 0.0 copy-start.10
  73.0 6.1 %first_layer.1 = (f32[36,128,128]{2,1,0:T(8,128)S(1)}, f32[48,128]{1,0:T(8,128)S(1)}, f32[48,128]{1,0:T(8,128)S(1)}) custom-call(f32[3,36]{1,0:T(4,128)S(1)} %add_convert_fusion.refs_0_.valid_ref, s32[1,128]{1,0:T(1,128)S(1)} %get-tuple-element.23.order_ref, bf16[512,128]{1,0:T(8,128)(2,1)S(1)} %collective-permute-done.lead_ref, ...), custom_call_target="tpu_custom_call" | custom-call | flops 4076863488 | bytes 4194304 | tf_op jit(solution)/shard_map/first_layer/pallas_call | solution.py:405
  79.1 0.0 copy-start.5
  79.1 0.0 copy-start.7
  79.1 0.0 collective-permute-done.1.halo_l
  79.1 0.0 collective-permute-done.2.halo_r
  79.1 0.0 copy-done.3
  79.1 2.4 %finish_hidden.1 = (f32[4,288,128]{2,1,0:T(8,128)S(1)}, f32[16,24,128]{2,1,0:T(8,128)S(1)}) custom-call(f32[3,36]{1,0:T(4,128)S(1)} %add_convert_fusion.refs_0_.valid_ref, bf16[576,128]{1,0:T(8,128)(2,1)S(1)} %get-tuple-element.30.own_l, bf16[576,128]{1,0:T(8,128)(2,1)S(1)} %get-tuple-element.31.own_r, bf16[576,128]{1,0:T(8,128)(2,1)S(1)} %collective-permute-done.1.halo_l, ...), custom_call_target="tpu_custom_call" | custom-call | tf_op jit(solution)/shard_map/finish_hidden/pallas_call | solution.py:475
  81.5 16.3 %all_to_all.10.stats_ref = f32[16,24,128]{2,1,0:T(8,128)S(1)} all-to-all(f32[16,24,128]{2,1,0:T(8,128)S(1)} %get-tuple-element.36), channel_id=1, replica_groups=mesh['tm'=16,'tile'=16] {'tile'}, dimensions={0} | all-to-all | bytes 393216 | tf_op jit(solution)/shard_map/all_to_all | solution.py:633
  97.8 0.0 copy-done.8
  97.8 0.0 copy-done.9
  97.8 0.0 copy-done.10
  97.8 0.0 copy-done.5
  97.8 0.0 copy-done.7
  97.9 6.8 %second_layer.1 = bf16[4096,128]{1,0:T(8,128)(2,1)} custom-call(f32[3,36]{1,0:T(4,128)S(1)} %add_convert_fusion.refs_0_.valid_ref, s32[1,128]{1,0:T(1,128)S(1)} %get-tuple-element.23.order_ref, f32[36,128,128]{2,1,0:T(8,128)S(1)} %get-tuple-element.27.hidden_ref, f32[4,288,128]{2,1,0:T(8,128)S(1)} %get-tuple-element.35.edges_ref, ...), custom_call_target="tpu_custom_call" | custom-call | tf_op jit(solution)/shard_map/second_layer/pallas_call | solution.py:569
  (4 shorter events, 0.0 us)
Async XLA Ops:
  2.6 8.0 %copy-start.15 = (s32[8]{0:T(128)S(1)}, s32[8]{0:T(128)}, u32[]{:S(2)}) copy-start(s32[8]{0:T(128)} %param.10) | copy-start | bytes 100
  2.6 8.2 %copy-start = (bf16[3,3,3,128,128]{4,3,2,1,0:T(8,128)(2,1)S(1)}, bf16[3,3,3,128,128]{4,3,2,1,0:T(8,128)(2,1)}, u32[]{:S(2)}) copy-start(bf16[3,3,3,128,128]{4,3,2,1,0:T(8,128)(2,1)} %first_ref.1) | copy-start | bytes 2654212
  2.6 58.1 %all-to-all-start = ((bf16[16,528,128]{2,1,0:T(8,128)(2,1)}), bf16[16,528,128]{2,1,0:T(8,128)(2,1)S(1)}, u32[]{:S(2)}, u32[]{:S(2)}) async-start(bf16[16,528,128]{2,1,0:T(8,128)(2,1)} %send_blocks.1), calls=%async_computation | async-start | bytes 4325376 | tf_op jit(solution)/shard_map/all_to_all | solution.py:616
  10.7 1.2 %copy-start.1 = (bf16[3,3,3,128,128]{4,3,2,1,0:T(8,128)(2,1)S(1)}, bf16[3,3,3,128,128]{4,3,2,1,0:T(8,128)(2,1)}, u32[]{:S(2)}) copy-start(bf16[3,3,3,128,128]{4,3,2,1,0:T(8,128)(2,1)} %second_ref.1) | copy-start | bytes 2654212
  12.4 0.9 copy-start.2
  13.3 0.9 copy-start.4
  14.2 0.8 copy-start.6
  15.0 0.9 copy-start.11
  15.9 0.8 copy-start.13
  60.7 12.2 %copy-start.12 = (bf16[1536,256]{1,0:T(8,128)(2,1)S(1)}, bf16[1536,256]{1,0:T(8,128)(2,1)}, u32[]{:S(2)}) copy-start(bf16[1536,256]{1,0:T(8,128)(2,1)} %copy-done.11) | copy-start | bytes 2359300
  60.7 12.2 %copy-start.14 = (bf16[1152,256]{1,0:T(8,128)(2,1)S(1)}, bf16[1152,256]{1,0:T(8,128)(2,1)}, u32[]{:S(2)}) copy-start(bf16[1152,256]{1,0:T(8,128)(2,1)} %copy-done.13) | copy-start | bytes 1769476
  61.8 6.3 %collective-permute-start = (bf16[512,128]{1,0:T(8,128)(2,1)S(1)}, bf16[512,128]{1,0:T(8,128)(2,1)S(1)}, u32[]{:S(2)}, u32[]{:S(2)}) collective-permute-start(bf16[512,128]{1,0:T(8,128)(2,1)S(1)} %get-tuple-element.24), channel_id=1, source_target_pairs={{0,16},{16,32},{32,48},{48,64},{64,80},{80,96},{96,112},{112,128},... | collective-permute-start | bytes 393224 | tf_op jit(solution)/shard_map/ppermute | solution.py:625
  68.2 10.9 %collective-permute-start.1 = (bf16[576,128]{1,0:T(8,128)(2,1)S(1)}, bf16[576,128]{1,0:T(8,128)(2,1)S(1)}, u32[]{:S(2)}, u32[]{:S(2)}) collective-permute-start(bf16[576,128]{1,0:T(8,128)(2,1)S(1)} %get-tuple-element.31.own_r), channel_id=1, source_target_pairs={{0,1},{1,2},{2,3},{3,4},{4,5},{5,6},{6,7},{7,8},{8,9},{9,10},{10,1... | collective-permute-start | bytes 442376 | tf_op jit(solution)/shard_map/ppermute | solution.py:601
  71.6 7.5 %collective-permute-start.2 = (bf16[576,128]{1,0:T(8,128)(2,1)S(1)}, bf16[576,128]{1,0:T(8,128)(2,1)S(1)}, u32[]{:S(2)}, u32[]{:S(2)}) collective-permute-start(bf16[576,128]{1,0:T(8,128)(2,1)S(1)} %get-tuple-element.30.own_l), channel_id=1, source_target_pairs={{1,0},{2,1},{3,2},{4,3},{5,4},{6,5},{7,6},{8,7},{9,8},{10,9},{11,1... | collective-permute-start | bytes 442376 | tf_op jit(solution)/shard_map/ppermute | solution.py:602
  72.9 6.2 %copy-start.3 = (bf16[1152,384]{1,0:T(8,128)(2,1)S(1)}, bf16[1152,384]{1,0:T(8,128)(2,1)}, u32[]{:S(2)}) copy-start(bf16[1152,384]{1,0:T(8,128)(2,1)} %copy-done.2) | copy-start | bytes 2654212
  72.9 24.9 %copy-start.8 = (f32[128]{0:T(128)S(1)}, f32[128]{0:T(128)}, u32[]{:S(2)}) copy-start(f32[128]{0:T(128)} %param.12) | copy-start | bytes 1540
  72.9 24.9 %copy-start.9 = (f32[128]{0:T(128)S(1)}, f32[128]{0:T(128)}, u32[]{:S(2)}) copy-start(f32[128]{0:T(128)} %param.13) | copy-start | bytes 1540
  73.0 24.9 %copy-start.10 = (f32[128]{0:T(128)S(1)}, f32[128]{0:T(128)}, u32[]{:S(2)}) copy-start(f32[128]{0:T(128)} %param.15) | copy-start | bytes 1540
  79.1 18.8 %copy-start.5 = (bf16[1536,256]{1,0:T(8,128)(2,1)S(1)}, bf16[1536,256]{1,0:T(8,128)(2,1)}, u32[]{:S(2)}) copy-start(bf16[1536,256]{1,0:T(8,128)(2,1)} %copy-done.4) | copy-start | bytes 2359300
  79.1 18.8 %copy-start.7 = (bf16[1152,256]{1,0:T(8,128)(2,1)S(1)}, bf16[1152,256]{1,0:T(8,128)(2,1)}, u32[]{:S(2)}) copy-start(bf16[1152,256]{1,0:T(8,128)(2,1)} %copy-done.6) | copy-start | bytes 1769476

commit v7 on v6

--- a/solution.py
+++ b/solution.py
@@ -335,7 +335,11 @@
             chunk_step(u, (trip * UNROLL + u) * CHUNK)
         return done
 
-    lax.fori_loop(0, 2 * OWN // CHUNK // UNROLL, step, 0)
+    trips = 2 * OWN // CHUNK // UNROLL
+    if trips == 1:
+        step(0, 0)
+    else:
+        lax.fori_loop(0, trips, step, 0)
 
 
 def group_total(entries):
@@ -395,7 +399,7 @@
     def own_block(at):
         return lambda k: block_at(arrived_ref, order_ref[0, at // 2 + k])
 
-    chunk_step(0, 0, LEAD, lambda k: lead_ref[k * 2 * POS : (k + 1) * 2 * POS])
+    chunk_step(UNROLL - 1, 0, LEAD, lambda k: lead_ref[k * 2 * POS : (k + 1) * 2 * POS])
     over_chunks(lambda u, at: chunk_step(u, LEAD + at, CHUNK, own_block(at)))
 
 
@@ -559,7 +563,7 @@
         sem = sems.at[lax.div(jnp.int32(start), jnp.int32(CHUNK))]
         return pltpu.make_async_copy(staged.at[rows], out_ref.at[rows], sem)
 
-    chunk_step(0, LEAD - 2, 2)
+    chunk_step(UNROLL - 1, LEAD - 2, 2)
     over_chunks(own_chunk)
     for start in range(0, 2 * OWN, CHUNK):
         copy_out(start).wait()

time: 105 us -> 105 us (level)
  no operation moved by 1% of the time
where the time goes in v7:
time: 105 us
  waiting for transfers between devices  47.1 us (45%)
  Pallas kernels  20.5 us (20%)
  blocking collectives  16.3 us (16%)
  starting transfers between devices  14.5 us (14%)
  local copies, waits for them, and re-layouts  5.67 us (5%)
    all_to_all x1, waiting for transfers between devices, shards(): lax.all_to_all(outgoing, 'tm', split_axis=0, concat_axis=0, tiled=True)  43.7 us
    all_to_all x1, blocking collectives, shards(): lax.all_to_all(stats, 'tile', split_axis=0, concat_axis=0, tiled=True)  16.3 us
    all_to_all x1, starting transfers between devices, shards(): lax.all_to_all(outgoing, 'tm', split_axis=0, concat_axis=0, tiled=True)  7.75 us
    pallas_call x1, Pallas kernels, second_layer(): pl.pallas_call(output_kernel, out_shape=jax.ShapeDtypeStruct((2 * OWN * P...  6.85 us
    pallas_call x1, Pallas kernels, first_layer(): pl.pallas_call(hidden_kernel, out_shape=(jax.ShapeDtypeStruct((length, PO...  6.1 us
    unnamed x32, local copies, waits for them, and re-layouts  5.54 us
    ppermute x1, waiting for transfers between devices, shards(): lead = lax.ppermute(tail, 'tm', [(i, i + 1) for i in range(owners - 1)])  3.42 us
    ppermute x1, starting transfers between devices, swap_edges(): lax.ppermute(right, 'tile', [(i, i + 1) for i in range(count - 1)])  3.4 us
  transfers between devices with their start and end apart: 4, of which 2 were waited for; matrix products, arithmetic and copies ran while one was open for 0% of the time, Pallas kernels for 7%

profile of v7, /device:TPU:96, one launch (start us, length us, event | category | flops | bytes accessed | tf_op | source)
XLA Modules:
  0.0 104.7 jit_solution(2874587907508528596)
XLA Ops:
  0.0 2.6 %send_blocks.1 = bf16[16,528,128]{2,1,0:T(8,128)(2,1)} custom-call(s32[32]{0:T(128)} %slot_hbm.1, bf16[32,256,128]{2,1,0:T(8,128)(2,1)} %bitcast.24), custom_call_target="tpu_custom_call" | custom-call | tf_op jit(solution)/shard_map/send_blocks/pallas_call | solution.py:113
  2.6 0.0 copy-start.15
  2.7 0.0 copy-start
  2.7 7.8 %all-to-all-start = ((bf16[16,528,128]{2,1,0:T(8,128)(2,1)}), bf16[16,528,128]{2,1,0:T(8,128)(2,1)S(1)}, u32[]{:S(2)}, u32[]{:S(2)}) async-start(bf16[16,528,128]{2,1,0:T(8,128)(2,1)} %send_blocks.1), calls=%async_computation | async-start | bytes 4325376 | tf_op jit(solution)/shard_map/all_to_all | solution.py:620
  10.4 0.0 copy-done.15
  10.4 0.2 reduce-window.8
  10.6 0.0 copy-done
  10.6 0.0 copy-start.1
  10.6 1.2 %copy-done.1 = bf16[3,3,3,128,128]{4,3,2,1,0:T(8,128)(2,1)S(1)} copy-done((bf16[3,3,3,128,128]{4,3,2,1,0:T(8,128)(2,1)S(1)}, bf16[3,3,3,128,128]{4,3,2,1,0:T(8,128)(2,1)}, u32[]{:S(2)}) %copy-start.1) | copy-done | bytes 884760
  11.8 0.5 join_weights.1
  12.3 0.0 copy-start.2
  12.3 0.9 copy-done.2
  13.2 0.0 copy-start.4
  13.2 0.9 copy-done.4
  14.1 0.0 copy-start.6
  14.1 0.8 copy-done.6
  14.9 0.0 copy-start.11
  14.9 0.9 copy-done.11
  15.7 0.0 copy-start.13
  15.7 0.8 copy-done.13
  16.6 0.1 stack.11
  16.7 0.1 convert_reduce_fusion.2
  16.9 43.7 %all-to-all-done.arrived_ref = bf16[16,528,128]{2,1,0:T(8,128)(2,1)S(1)} async-done(((bf16[16,528,128]{2,1,0:T(8,128)(2,1)}), bf16[16,528,128]{2,1,0:T(8,128)(2,1)S(1)}, u32[]{:S(2)}, u32[]{:S(2)}) %all-to-all-start) | async-done | bytes 2162720 | tf_op jit(solution)/shard_map/all_to_all | solution.py:620
  60.5 0.0 copy-start.12
  60.5 0.0 copy-start.14
  60.5 1.2 %block_order.1 = (s32[1,128]{1,0:T(1,128)S(1)}, bf16[512,128]{1,0:T(8,128)(2,1)S(1)}) custom-call(bf16[16,528,128]{2,1,0:T(8,128)(2,1)S(1)} %all-to-all-done.arrived_ref, f32[3,36]{1,0:T(4,128)S(1)} %add_convert_fusion.refs_0_.valid_ref, f32[8,128]{1,0:T(8,128)S(1)} %get-tuple-element.22.refs_1_), custom_call_target="tpu_custom_call" | custom-call | tf_op jit(solution)/shard_map/block_order/pallas_call | solution.py:157
  61.7 2.0 %collective-permute-start = (bf16[512,128]{1,0:T(8,128)(2,1)S(1)}, bf16[512,128]{1,0:T(8,128)(2,1)S(1)}, u32[]{:S(2)}, u32[]{:S(2)}) collective-permute-start(bf16[512,128]{1,0:T(8,128)(2,1)S(1)} %get-tuple-element.24), channel_id=1, source_target_pairs={{0,16},{16,32},{32,48},{48,64},{64,80},{80,96},{96,112},{112,128},... | collective-permute-start | bytes 393224 | tf_op jit(solution)/shard_map/ppermute | solution.py:629
  63.7 0.8 own_edges.1
  64.6 3.4 %collective-permute-done.lead_ref = bf16[512,128]{1,0:T(8,128)(2,1)S(1)} collective-permute-done((bf16[512,128]{1,0:T(8,128)(2,1)S(1)}, bf16[512,128]{1,0:T(8,128)(2,1)S(1)}, u32[]{:S(2)}, u32[]{:S(2)}) %collective-permute-start) | collective-permute-done | bytes 131104 | tf_op jit(solution)/shard_map/ppermute | solution.py:629
  68.0 0.1 lead_edges.1
  68.1 3.4 %collective-permute-start.1 = (bf16[576,128]{1,0:T(8,128)(2,1)S(1)}, bf16[576,128]{1,0:T(8,128)(2,1)S(1)}, u32[]{:S(2)}, u32[]{:S(2)}) collective-permute-start(bf16[576,128]{1,0:T(8,128)(2,1)S(1)} %get-tuple-element.31.own_r), channel_id=1, source_target_pairs={{0,1},{1,2},{2,3},{3,4},{4,5},{5,6},{6,7},{7,8},{8,9},{9,10},{10,1... | collective-permute-start | bytes 442376 | tf_op jit(solution)/shard_map/ppermute | solution.py:605
  71.5 1.3 %collective-permute-start.2 = (bf16[576,128]{1,0:T(8,128)(2,1)S(1)}, bf16[576,128]{1,0:T(8,128)(2,1)S(1)}, u32[]{:S(2)}, u32[]{:S(2)}) collective-permute-start(bf16[576,128]{1,0:T(8,128)(2,1)S(1)} %get-tuple-element.30.own_l), channel_id=1, source_target_pairs={{1,0},{2,1},{3,2},{4,3},{5,4},{6,5},{7,6},{8,7},{9,8},{10,9},{11,1... | collective-permute-start | bytes 442376 | tf_op jit(solution)/shard_map/ppermute | solution.py:606
  72.8 0.0 copy-done.12
  72.8 0.0 copy-done.14
  72.8 0.0 copy-start.3
  72.8 0.0 copy-start.8
  72.8 0.0 copy-start.9
  72.8 0.0 copy-start.10
  72.8 6.1 %first_layer.1 = (f32[36,128,128]{2,1,0:T(8,128)S(1)}, f32[48,128]{1,0:T(8,128)S(1)}, f32[48,128]{1,0:T(8,128)S(1)}) custom-call(f32[3,36]{1,0:T(4,128)S(1)} %add_convert_fusion.refs_0_.valid_ref, s32[1,128]{1,0:T(1,128)S(1)} %get-tuple-element.23.order_ref, bf16[512,128]{1,0:T(8,128)(2,1)S(1)} %collective-permute-done.lead_ref, ...), custom_call_target="tpu_custom_call" | custom-call | flops 4076863488 | bytes 4194304 | tf_op jit(solution)/shard_map/first_layer/pallas_call | solution.py:409
  78.9 0.0 copy-start.5
  78.9 0.0 copy-start.7
  78.9 0.0 collective-permute-done.1.halo_l
  79.0 0.0 collective-permute-done.2.halo_r
  79.0 0.0 copy-done.3
  79.0 2.4 %finish_hidden.1 = (f32[4,288,128]{2,1,0:T(8,128)S(1)}, f32[16,24,128]{2,1,0:T(8,128)S(1)}) custom-call(f32[3,36]{1,0:T(4,128)S(1)} %add_convert_fusion.refs_0_.valid_ref, bf16[576,128]{1,0:T(8,128)(2,1)S(1)} %get-tuple-element.30.own_l, bf16[576,128]{1,0:T(8,128)(2,1)S(1)} %get-tuple-element.31.own_r, bf16[576,128]{1,0:T(8,128)(2,1)S(1)} %collective-permute-done.1.halo_l, ...), custom_call_target="tpu_custom_call" | custom-call | tf_op jit(solution)/shard_map/finish_hidden/pallas_call | solution.py:479
  81.4 16.3 %all_to_all.10.stats_ref = f32[16,24,128]{2,1,0:T(8,128)S(1)} all-to-all(f32[16,24,128]{2,1,0:T(8,128)S(1)} %get-tuple-element.36), channel_id=1, replica_groups=mesh['tm'=16,'tile'=16] {'tile'}, dimensions={0} | all-to-all | bytes 393216 | tf_op jit(solution)/shard_map/all_to_all | solution.py:637
  97.7 0.0 copy-done.8
  97.7 0.0 copy-done.9
  97.7 0.0 copy-done.10
  97.7 0.0 copy-done.5
  97.7 0.0 copy-done.7
  97.7 6.8 %second_layer.1 = bf16[4096,128]{1,0:T(8,128)(2,1)} custom-call(f32[3,36]{1,0:T(4,128)S(1)} %add_convert_fusion.refs_0_.valid_ref, s32[1,128]{1,0:T(1,128)S(1)} %get-tuple-element.23.order_ref, f32[36,128,128]{2,1,0:T(8,128)S(1)} %get-tuple-element.27.hidden_ref, f32[4,288,128]{2,1,0:T(8,128)S(1)} %get-tuple-element.35.edges_ref, ...), custom_call_target="tpu_custom_call" | custom-call | tf_op jit(solution)/shard_map/second_layer/pallas_call | solution.py:573
  (4 shorter events, 0.0 us)
Async XLA Ops:
  2.6 7.8 %copy-start.15 = (s32[8]{0:T(128)S(1)}, s32[8]{0:T(128)}, u32[]{:S(2)}) copy-start(s32[8]{0:T(128)} %param.10) | copy-start | bytes 100
  2.7 8.0 %copy-start = (bf16[3,3,3,128,128]{4,3,2,1,0:T(8,128)(2,1)S(1)}, bf16[3,3,3,128,128]{4,3,2,1,0:T(8,128)(2,1)}, u32[]{:S(2)}) copy-start(bf16[3,3,3,128,128]{4,3,2,1,0:T(8,128)(2,1)} %first_ref.1) | copy-start | bytes 2654212
  2.7 57.9 %all-to-all-start = ((bf16[16,528,128]{2,1,0:T(8,128)(2,1)}), bf16[16,528,128]{2,1,0:T(8,128)(2,1)S(1)}, u32[]{:S(2)}, u32[]{:S(2)}) async-start(bf16[16,528,128]{2,1,0:T(8,128)(2,1)} %send_blocks.1), calls=%async_computation | async-start | bytes 4325376 | tf_op jit(solution)/shard_map/all_to_all | solution.py:620
  10.6 1.2 %copy-start.1 = (bf16[3,3,3,128,128]{4,3,2,1,0:T(8,128)(2,1)S(1)}, bf16[3,3,3,128,128]{4,3,2,1,0:T(8,128)(2,1)}, u32[]{:S(2)}) copy-start(bf16[3,3,3,128,128]{4,3,2,1,0:T(8,128)(2,1)} %second_ref.1) | copy-start | bytes 2654212
  12.3 0.9 copy-start.2
  13.2 0.9 copy-start.4
  14.1 0.8 copy-start.6
  14.9 0.9 copy-start.11
  15.7 0.8 copy-start.13
  60.5 12.2 %copy-start.12 = (bf16[1536,256]{1,0:T(8,128)(2,1)S(1)}, bf16[1536,256]{1,0:T(8,128)(2,1)}, u32[]{:S(2)}) copy-start(bf16[1536,256]{1,0:T(8,128)(2,1)} %copy-done.11) | copy-start | bytes 2359300
  60.5 12.2 %copy-start.14 = (bf16[1152,256]{1,0:T(8,128)(2,1)S(1)}, bf16[1152,256]{1,0:T(8,128)(2,1)}, u32[]{:S(2)}) copy-start(bf16[1152,256]{1,0:T(8,128)(2,1)} %copy-done.13) | copy-start | bytes 1769476
  61.7 6.3 %collective-permute-start = (bf16[512,128]{1,0:T(8,128)(2,1)S(1)}, bf16[512,128]{1,0:T(8,128)(2,1)S(1)}, u32[]{:S(2)}, u32[]{:S(2)}) collective-permute-start(bf16[512,128]{1,0:T(8,128)(2,1)S(1)} %get-tuple-element.24), channel_id=1, source_target_pairs={{0,16},{16,32},{32,48},{48,64},{64,80},{80,96},{96,112},{112,128},... | collective-permute-start | bytes 393224 | tf_op jit(solution)/shard_map/ppermute | solution.py:629
  68.1 10.9 %collective-permute-start.1 = (bf16[576,128]{1,0:T(8,128)(2,1)S(1)}, bf16[576,128]{1,0:T(8,128)(2,1)S(1)}, u32[]{:S(2)}, u32[]{:S(2)}) collective-permute-start(bf16[576,128]{1,0:T(8,128)(2,1)S(1)} %get-tuple-element.31.own_r), channel_id=1, source_target_pairs={{0,1},{1,2},{2,3},{3,4},{4,5},{5,6},{6,7},{7,8},{8,9},{9,10},{10,1... | collective-permute-start | bytes 442376 | tf_op jit(solution)/shard_map/ppermute | solution.py:605
  71.5 7.5 %collective-permute-start.2 = (bf16[576,128]{1,0:T(8,128)(2,1)S(1)}, bf16[576,128]{1,0:T(8,128)(2,1)S(1)}, u32[]{:S(2)}, u32[]{:S(2)}) collective-permute-start(bf16[576,128]{1,0:T(8,128)(2,1)S(1)} %get-tuple-element.30.own_l), channel_id=1, source_target_pairs={{1,0},{2,1},{3,2},{4,3},{5,4},{6,5},{7,6},{8,7},{9,8},{10,9},{11,1... | collective-permute-start | bytes 442376 | tf_op jit(solution)/shard_map/ppermute | solution.py:606
  72.8 6.2 %copy-start.3 = (bf16[1152,384]{1,0:T(8,128)(2,1)S(1)}, bf16[1152,384]{1,0:T(8,128)(2,1)}, u32[]{:S(2)}) copy-start(bf16[1152,384]{1,0:T(8,128)(2,1)} %copy-done.2) | copy-start | bytes 2654212
  72.8 24.9 %copy-start.8 = (f32[128]{0:T(128)S(1)}, f32[128]{0:T(128)}, u32[]{:S(2)}) copy-start(f32[128]{0:T(128)} %param.12) | copy-start | bytes 1540
  72.8 24.9 %copy-start.9 = (f32[128]{0:T(128)S(1)}, f32[128]{0:T(128)}, u32[]{:S(2)}) copy-start(f32[128]{0:T(128)} %param.13) | copy-start | bytes 1540
  72.8 24.9 %copy-start.10 = (f32[128]{0:T(128)S(1)}, f32[128]{0:T(128)}, u32[]{:S(2)}) copy-start(f32[128]{0:T(128)} %param.15) | copy-start | bytes 1540
  78.9 18.8 %copy-start.5 = (bf16[1536,256]{1,0:T(8,128)(2,1)S(1)}, bf16[1536,256]{1,0:T(8,128)(2,1)}, u32[]{:S(2)}) copy-start(bf16[1536,256]{1,0:T(8,128)(2,1)} %copy-done.4) | copy-start | bytes 2359300
  78.9 18.8 %copy-start.7 = (bf16[1152,256]{1,0:T(8,128)(2,1)S(1)}, bf16[1152,256]{1,0:T(8,128)(2,1)}, u32[]{:S(2)}) copy-start(bf16[1152,256]{1,0:T(8,128)(2,1)} %copy-done.6) | copy-start | bytes 1769476
